TPU v7x, 256 devices: a whole 4x4x8 slice. The times are simulated.
256 devices in a mesh: slide: 4 (over x_hi, core), seq: 64 (over z, x_lo, y).
Axes of the slice: x: 4 (x_hi: 2, x_lo: 2; x = x_hi * 2 + x_lo), y: 4, z: 8, core: 2. Of those that a mesh axis runs over, the one named last changes fastest.
Arguments:
- query_rows: bfloat16 [4, 16384, 768], P('slide', 'seq'), may hold values from -270 to 270
- key_rows: bfloat16 [4, 16384, 768], P('slide', 'seq'), may hold values from -6 to 6
- value_rows: bfloat16 [4, 16384, 768], P('slide', 'seq'), may hold values from -6 to 6
- grad_out: bfloat16 [4, 16384, 768], P('slide', 'seq'), may hold values from -6 to 6
- out_weight: bfloat16 [768, 768], replicated, may hold values from -0.21875 to 0.21875
- tile_counts: int32 [4], P('slide'), may hold values from 4096 to 16384, as said below
Outputs:
- layer_out: bfloat16 [4, 16384, 768], P('slide', 'seq')
- grad_query: bfloat16 [4, 16384, 768], P('slide', 'seq')
- grad_key: bfloat16 [4, 16384, 768], P('slide', 'seq')
- grad_value: bfloat16 [4, 16384, 768], P('slide', 'seq')
- grad_weight: float32 [768, 768], P('seq')
Inputs may be any that keep to these rules, and one draw needn't show every extreme that they name: Positions 0 to tile_counts - 1 of a slide are valid; in every draw one slide has all 16384 positions valid.
All inputs are finite; a program needn't handle non-finite values.
Results may differ from a plain program's by a relative error of at most 0.0095.
Values may be sent and summed in bfloat16 or wider, within the bound.
No kernel may reach another device: no remote copies, remote signals or barrier semaphores. Data moves between devices by JAX's collectives and lax.ppermute only.
A program may use at most 128 MiB of HBM per device.

v0:
```python
import jax
import jax.numpy as jnp
from jax import lax
from jax.sharding import PartitionSpec as P

HEADS = 16
DILATION_FACTOR = 16


masked_score = -1e30


def strided_flags(head_count):
    return (
        jnp.arange(DILATION_FACTOR, dtype=jnp.int32)[None, :]
        == (jnp.arange(head_count, dtype=jnp.int32) % DILATION_FACTOR)[:, None]
    )


def dilate(input_matrix, head_count):
    count_of_rows, feature_width = input_matrix.shape
    blocked_layout = input_matrix.reshape(
        count_of_rows // DILATION_FACTOR, DILATION_FACTOR, head_count, feature_width // head_count
    )
    chosen = strided_flags(head_count).T[None, :, :, None]
    return jnp.sum(jnp.where(chosen, blocked_layout, jnp.zeros((), input_matrix.dtype)), axis=1)


def undilate(strided_tensor, head_count):
    chosen = strided_flags(head_count).T[None, :, :, None]
    spread_rows = jnp.where(
        chosen, strided_tensor[:, None, :, :], jnp.zeros((), strided_tensor.dtype)
    )
    return spread_rows.reshape(
        strided_tensor.shape[0] * DILATION_FACTOR, strided_tensor.shape[1], strided_tensor.shape[2]
    )


def select_strided(softmax_statistic, head_count):
    blocked_layout = softmax_statistic.reshape(
        softmax_statistic.shape[0], softmax_statistic.shape[1] // DILATION_FACTOR, DILATION_FACTOR
    )
    return jnp.sum(
        jnp.where(
            strided_flags(head_count)[:, None, :],
            blocked_layout,
            jnp.zeros((), softmax_statistic.dtype),
        ),
        axis=-1,
    )


def spread_stat(strided_tensor, full_tensor, head_count):
    blocked_layout = full_tensor.reshape(
        full_tensor.shape[0], full_tensor.shape[1] // DILATION_FACTOR, DILATION_FACTOR
    )
    return jnp.where(
        strided_flags(head_count)[:, None, :], strided_tensor[:, :, None], blocked_layout
    ).reshape(full_tensor.shape)


def product(form, left, right):
    return jnp.einsum(form, left, right, preferred_element_type=jnp.float32)


def on_device(query_rows, key_rows, value_rows, grad_out, out_weight, tile_counts):
    queries = query_rows[0]
    keys_local = key_rows[0]
    values_local = value_rows[0]
    grad_rows = grad_out[0]
    tile_count = tile_counts[0]
    count_of_rows, feature_width = queries.shape
    head_count = HEADS
    head_width = feature_width // head_count
    dilated_rows = count_of_rows // DILATION_FACTOR
    score_scale = head_width ** (-0.5)
    row_start = lax.axis_index("seq") * count_of_rows
    valid_rows = row_start + jnp.arange(count_of_rows, dtype=jnp.int32) < tile_count
    q_heads = queries.reshape(count_of_rows, head_count, head_width)
    k_heads = keys_local.reshape(count_of_rows, head_count, head_width)
    v_heads = values_local.reshape(count_of_rows, head_count, head_width)
    q_strided = dilate(queries, head_count)
    k_strided = dilate(keys_local, head_count)
    v_strided = dilate(values_local, head_count)
    head_start_index = (jnp.arange(head_count, dtype=jnp.int32) % DILATION_FACTOR)[:, None]
    scores_near = product("qhd,khd->hqk", q_heads, k_heads) * score_scale
    scores_near = jnp.where(valid_rows[None, None, :], scores_near, masked_score)
    max_near = jnp.max(scores_near, axis=-1)
    near_strided = select_strided(max_near, head_count)
    seq_count = lax.axis_size("seq")
    k_flat, v_flat = (
        lax.all_gather(k_strided.reshape(dilated_rows, feature_width), "seq", axis=0, tiled=True),
        lax.all_gather(v_strided.reshape(dilated_rows, feature_width), "seq", axis=0, tiled=True),
    )
    slide_wide_rows = k_flat.shape[0]
    k_global = k_flat.reshape(slide_wide_rows, head_count, head_width)
    v_global = v_flat.reshape(slide_wide_rows, head_count, head_width)
    global_position = (
        jnp.arange(slide_wide_rows, dtype=jnp.int32)[None, :] * DILATION_FACTOR + head_start_index
    )
    scores_far = product("qhd,khd->hqk", q_strided, k_global) * score_scale
    scores_far = jnp.where((global_position < tile_count)[:, None, :], scores_far, masked_score)
    max_strided = jnp.maximum(jnp.max(scores_far, axis=-1), near_strided)
    exp_far = jnp.exp(scores_far - max_strided[:, :, None])
    far_sum = jnp.sum(exp_far, axis=-1)
    far_accum = product("hqk,khd->qhd", exp_far.astype(jnp.bfloat16), v_global)
    max_rows = spread_stat(max_strided, max_near, head_count)
    exp_near = jnp.exp(scores_near - max_rows[:, :, None])
    sum_near = jnp.sum(exp_near, axis=-1)
    sum_rows = sum_near + spread_stat(far_sum, jnp.zeros_like(sum_near), head_count)
    sum_strided = select_strided(sum_rows, head_count)
    accum = product("hqk,khd->qhd", exp_near.astype(jnp.bfloat16), v_heads)
    accum = accum + undilate(far_accum, head_count)
    out_heads = (accum / sum_rows.T[:, :, None]).astype(jnp.bfloat16)
    attended = out_heads.reshape(count_of_rows, feature_width)
    layer_out = jnp.where(
        valid_rows[:, None], jnp.dot(attended, out_weight, preferred_element_type=jnp.float32), 0.0
    ).astype(jnp.bfloat16)
    grad_masked = jnp.where(valid_rows[:, None], grad_rows, jnp.zeros((), grad_rows.dtype))
    d_attended = lax.dot_general(
        grad_masked, out_weight, (((1,), (1,)), ((), ())), preferred_element_type=jnp.float32
    ).astype(jnp.bfloat16)
    weight_part = lax.dot_general(
        attended, grad_masked, (((0,), (0,)), ((), ())), preferred_element_type=jnp.float32
    )
    grad_heads = d_attended.reshape(count_of_rows, head_count, head_width)
    delta_rows = jnp.sum(grad_heads.astype(jnp.float32) * out_heads.astype(jnp.float32), axis=-1).T
    delta_strided = select_strided(delta_rows, head_count)
    grad_strided = dilate(d_attended, head_count)
    prob_near = exp_near / sum_rows[:, :, None]
    dprob_near = product("qhd,khd->hqk", grad_heads, v_heads)
    dscore_near = (prob_near * (dprob_near - delta_rows[:, :, None])).astype(jnp.bfloat16)
    grad_q = product("hqk,khd->qhd", dscore_near, k_heads) * score_scale
    grad_k = product("hqk,qhd->khd", dscore_near, q_heads) * score_scale
    grad_v = product("hqk,qhd->khd", prob_near.astype(jnp.bfloat16), grad_heads)
    prob_far = exp_far / sum_strided[:, :, None]
    dprob_far = product("qhd,khd->hqk", grad_strided, v_global)
    dscore_far = (prob_far * (dprob_far - delta_strided[:, :, None])).astype(jnp.bfloat16)
    grad_q = grad_q + undilate(
        product("hqk,khd->qhd", dscore_far, k_global) * score_scale, head_count
    )
    key_terms = product("hqk,qhd->khd", dscore_far, q_strided) * score_scale
    value_terms = product("hqk,qhd->khd", prob_far.astype(jnp.bfloat16), grad_strided)
    key_part, value_part = (
        lax.psum_scatter(
            key_terms.reshape(slide_wide_rows, feature_width),
            "seq",
            scatter_dimension=0,
            tiled=True,
        ),
        lax.psum_scatter(
            value_terms.reshape(slide_wide_rows, feature_width),
            "seq",
            scatter_dimension=0,
            tiled=True,
        ),
    )
    far_key = key_part.reshape(dilated_rows, head_count, head_width)
    far_value = value_part.reshape(dilated_rows, head_count, head_width)
    grad_k = grad_k + undilate(far_key, head_count)
    grad_v = grad_v + undilate(far_value, head_count)
    weight_full = lax.psum(weight_part, ("slide", "seq"))
    share_rows = feature_width // seq_count
    grad_weight = lax.dynamic_slice_in_dim(
        weight_full, lax.axis_index("seq") * share_rows, share_rows, 0
    )
    return (
        layer_out[None],
        grad_q.reshape(count_of_rows, feature_width).astype(jnp.bfloat16)[None],
        grad_k.reshape(count_of_rows, feature_width).astype(jnp.bfloat16)[None],
        grad_v.reshape(count_of_rows, feature_width).astype(jnp.bfloat16)[None],
        grad_weight,
    )


def solution(mesh):
    return jax.shard_map(
        on_device,
        mesh=mesh,
        in_specs=(
            P("slide", "seq", None),
            P("slide", "seq", None),
            P("slide", "seq", None),
            P("slide", "seq", None),
            P(),
            P("slide"),
        ),
        out_specs=(
            P("slide", "seq", None),
            P("slide", "seq", None),
            P("slide", "seq", None),
            P("slide", "seq", None),
            P("seq", None),
        ),
        check_vma=False,
    )
```

profile of v0, /device:TPU:4, one launch (start us, length us, event | category | flops | bytes accessed | tf_op | source)
XLA Modules:
  0.0 1558.1 jit_solution(3191078678994760648)
XLA Ops:
  14.2 2.9 reshape_squeeze.21
  17.1 2.9 reshape_squeeze.23
  20.1 2.9 select_reduce_fusion
  31.6 3.0 fusion
  34.9 290.3 %all-gather.3.cloned.1.call-done = bf16[1024,768]{1,0:T(8,128)(2,1)} async-done(((bf16[16,768]{1,0:T(8,128)(2,1)}), bf16[1024,768]{1,0:T(8,128)(2,1)}) %all-gather.3.cloned.1.call-update) | async-done | bytes 1572880 | tf_op jit(solution)/shard_map/all_gather | solution.py:92
  325.2 2.6 copy.52
  330.2 293.7 %all-gather.5.cloned.1.call-done = bf16[1024,768]{1,0:T(8,128)(2,1)} async-done(((bf16[16,768]{1,0:T(8,128)(2,1)}), bf16[1024,768]{1,0:T(8,128)(2,1)}) %all-gather.5.cloned.1.call-update) | async-done | bytes 1572880 | tf_op jit(solution)/shard_map/all_gather | solution.py:93
  623.9 2.6 copy.57
  630.2 2.5 copy.59
  632.7 3.3 fusion.2
  636.2 2.4 multiply_reduce_fusion
  641.7 2.3 fusion.46
  644.0 3.6 copy.84
  649.8 2.4 convolution_multiply_fusion
  652.2 3.6 copy.82
  659.8 4.2 multiply_convert_fusion
  667.2 2.3 fusion.34
  669.4 231.2 %all-reduce.2.cloned.1.call-done = f32[768,768]{1,0:T(8,128)} async-done(((f32[768,768]{1,0:T(8,128)}), f32[768,768]{1,0:T(8,128)}) %all-reduce.2.cloned.1.call-update) | async-done | bytes 2359312 | tf_op jit(solution)/shard_map/psum | solution.py:162
  902.2 318.9 %reduce-scatter.9.cloned.1.call-done = f32[16,768]{1,0:T(8,128)} async-done(((f32[1024,768]{1,0:T(8,128)}), f32[16,768]{1,0:T(8,128)}) %reduce-scatter.9.cloned.1.call-update) | async-done | bytes 49168
  1225.5 3.4 copy.73
  1228.9 4.5 fusion.31
  1235.3 303.8 %reduce-scatter.7.cloned.1.call-done = f32[16,768]{1,0:T(8,128)} async-done(((f32[1024,768]{1,0:T(8,128)}), f32[16,768]{1,0:T(8,128)}) %reduce-scatter.7.cloned.1.call-update) | async-done | bytes 49168
  1543.6 3.4 copy.69
  1546.9 2.7 fusion.29
  (83 shorter events, 47.9 us)
Async XLA Ops:
  7.2 1.3 copy-start
  7.2 318.0 %all-gather.3.cloned.1.call-start = ((), (), s32[]{:S(2)}) async-start(), calls=%async_computation.2 | async-start | bytes 1597440 | tf_op jit(solution)/shard_map/all_gather | solution.py:92
  10.0 0.7 copy-start.7
  23.7 600.2 %all-gather.5.cloned.1.call-start = ((), (), s32[]{:S(2)}) async-start(), calls=%async_computation.3 | async-start | bytes 1597440 | tf_op jit(solution)/shard_map/all_gather | solution.py:93
  24.5 876.1 %all-reduce.2.cloned.1.call-start = ((), (), s32[]{:S(2)}) async-start(), calls=%async_computation.4 | async-start | bytes 4718592 | tf_op jit(solution)/shard_map/psum | solution.py:162
  27.9 6.6 copy-start.3
  29.2 298.5 %copy-start.4 = (bf16[1,256,768]{1,2,0:T(8,128)(2,1)}, bf16[1,256,768]{1,2,0:T(8,128)(2,1)S(1)}, u32[]{:S(2)}) copy-start(bf16[1,256,768]{1,2,0:T(8,128)(2,1)S(1)} %copy.51) | copy-start | bytes 1179652
  632.7 3.4 copy-start.1
  636.2 3.1 copy-start.8
  638.5 0.7 copy-start.9
  641.3 579.8 %reduce-scatter.9.cloned.1.call-start = ((), (), s32[]{:S(2)}) async-start(), calls=%async_computation.6 | async-start | bytes 3194880
  647.7 891.5 %reduce-scatter.7.cloned.1.call-start = ((), (), s32[]{:S(2)}) async-start(), calls=%async_computation.5 | async-start | bytes 3194880
  655.7 1.4 copy-start.2
  659.8 4.2 copy-start.5
  659.8 4.3 copy-start.6
Sparse Core Ops, SparseCore 0:
  23.8 301.2 all-gather.2
  327.5 296.3 all-gather.4
  641.4 259.2 all-reduce.1
  903.0 318.0 reduce-scatter.8
  1223.6 315.5 reduce-scatter.6
where the time goes:
time: 1560 us
  waiting for transfers between devices  1440 us (92%)
  local copies, waits for them, and re-layouts  63 us (4%)
  matrix products  34.6 us (2%)
    unnamed x7, waiting for transfers between devices  623 us
    all_gather x1, waiting for transfers between devices, on_device(): lax.all_gather(v_strided.reshape(dilated_rows, feature_width), 'seq', axi...  294 us
    all_gather x1, waiting for transfers between devices, on_device(): lax.all_gather(k_strided.reshape(dilated_rows, feature_width), 'seq', axi...  290 us
    psum x1, waiting for transfers between devices, on_device(): weight_full = lax.psum(weight_part, ('slide', 'seq'))  231 us
  transfers between devices with their start and end apart: 5, of which 5 were waited for; matrix products, arithmetic and copies ran while one was open for 4% of the time, Pallas kernels for 0%

commit v1 on v0

v1 whole, which is shorter than its diff:
```python
import jax
import jax.numpy as jnp
from jax import lax
from jax.experimental import pallas as pl
from jax.experimental.pallas import tpu as pltpu
from jax.sharding import PartitionSpec as P

HEADS = 16
HEAD_WIDTH = 48
ROWS = 256
WIDTH = 768
PEERS = 64
LANES = 128
SCALE = HEAD_WIDTH ** -0.5
MASKED = -1e30
BF = jnp.bfloat16
F32 = jnp.float32
SEND_ROWS = 40
BACK_ROWS = 56
PART_ROWS = 40


def iota(shape, dim):
    return lax.broadcasted_iota(jnp.int32, shape, dim)


def head_of(feature):
    return (feature * 1366) >> 16


def onehot(mask):
    return jnp.where(mask, 1.0, 0.0).astype(BF)


def nn(a, b):
    return lax.dot_general(a, b, (((1,), (0,)), ((), ())), preferred_element_type=F32)


def nt(a, b):
    return lax.dot_general(a, b, (((1,), (1,)), ((), ())), preferred_element_type=F32)


def tn(a, b):
    return lax.dot_general(a, b, (((0,), (0,)), ((), ())), preferred_element_type=F32)


def own_head_mask():
    return onehot(head_of(iota((ROWS, WIDTH), 1)) == (iota((ROWS, WIDTH), 0) & 15))


def fold(offset):
    f = iota((WIDTH, LANES), 0)
    lane = iota((WIDTH, LANES), 1) - offset
    return onehot((f - HEAD_WIDTH * head_of(f)) == lane)


def unfold(offset):
    f = iota((LANES, WIDTH), 1)
    lane = iota((LANES, WIDTH), 0) - offset
    return onehot((f - HEAD_WIDTH * head_of(f)) == lane)


def split3(x):
    hi = x.astype(BF).astype(F32)
    mid = (x - hi).astype(BF).astype(F32)
    return hi, mid, (x - hi - mid).astype(BF).astype(F32)


def pack_kernel(sc_ref, q_ref, k_ref, v_ref, g_ref, out_ref, scr):
    row_start, tile_count = sc_ref[0], sc_ref[1]
    own = own_head_mask()
    q_own = q_ref[...] * own
    valid_key = (row_start + iota((ROWS, ROWS), 1)) < tile_count
    s = jnp.where(valid_key, nt(q_own, k_ref[...]) * SCALE, MASKED)
    m = jnp.max(s, axis=1, keepdims=True)
    p = jnp.exp(s - m)
    l = jnp.sum(p, axis=1, keepdims=True)
    o = (nn(p.astype(BF), v_ref[...]) * (1.0 / l)).astype(BF) * own
    hi, mid, lo = split3(m + jnp.log(l))
    first, second = fold(0), fold(HEAD_WIDTH)
    lane = iota((ROWS, LANES), 1)
    d = nn(q_own, first) + nn(o, second)
    d = jnp.where(lane == 96, hi, jnp.where(lane == 97, mid, jnp.where(lane == 98, lo, d)))
    c = (nn(k_ref[...] * own, first) + nn(v_ref[...] * own, second)).astype(BF)
    r = iota((PEERS * 16, ROWS), 0)
    col = iota((PEERS * 16, ROWS), 1)
    x = nn(onehot(col == 16 * (r & 15) + (r >> 6)), c)
    mine = 16 * (4 * ((r >> 4) & 3) + (r & 3)) + (r >> 6)
    for a in range(4):
        part = d if a == 3 else pltpu.roll(d, 96 - 32 * a, 1)
        part = jnp.where(lane >= 96, part, 0.0).astype(BF)
        x = x + nn(onehot((col == mine) & (((r >> 2) & 3) == a)), part)
    out_ref[:, 0:16, :] = x.astype(BF).reshape(PEERS, 16, LANES)
    valid_row = (row_start + iota((ROWS, WIDTH), 0)) < tile_count
    g = jnp.where(valid_row, g_ref[...].astype(F32), 0.0).astype(BF)
    r2, c2 = iota((ROWS, ROWS), 0), iota((ROWS, ROWS), 1)
    gx = nn(onehot(c2 == 16 * (4 * (r2 & 3) + (r2 >> 6)) + ((r2 & 63) >> 2)), g)
    for t in range(6):
        for ii in range(4):
            scr[pl.ds(4 * t + ii, PEERS, stride=24), :] = gx[64 * ii : 64 * ii + 64, 128 * t : 128 * t + 128]
    out_ref[:, 16:40, :] = scr[...].reshape(PEERS, 24, LANES).astype(BF)


def near_kernel(sc_ref, q_ref, k_ref, v_ref, g_ref, w_ref, dq_ref, dk_ref, dv_ref, att_ref, ga_ref, keep_ref, send_ref,
                qt, kt, vt, gat, at, dqt, dkt, dvt, big, halves):
    row_start, tile_count, core = sc_ref[0], sc_ref[1], sc_ref[3]
    valid_row = (row_start + iota((ROWS, WIDTH), 0)) < tile_count
    g = jnp.where(valid_row, g_ref[...].astype(F32), 0.0).astype(BF)
    gat[...] = nt(w_ref[...], g).astype(BF)
    ga_ref[...] = nt(g, w_ref[...]).astype(BF)
    qt[...] = q_ref[...].T
    kt[...] = k_ref[...].T
    vt[...] = v_ref[...].T
    valid_key = (row_start + iota((ROWS, ROWS), 0)) < tile_count
    column = iota((1, ROWS), 1) & 15
    for h in range(HEADS):
        f = HEAD_WIDTH * h
        a, b = f // LANES * LANES, -(-(f + HEAD_WIDTH) // LANES) * LANES
        lane = a + iota((ROWS, b - a), 1)
        here = onehot((lane >= f) & (lane < f + HEAD_WIDTH))
        rows = slice(f, f + HEAD_WIDTH)
        s = jnp.where(valid_key, nn(k_ref[:, a:b] * here, qt[a:b, :]) * SCALE, MASKED)
        m = jnp.max(s, axis=0, keepdims=True)
        p = jnp.exp(s - m)
        l = jnp.sum(p, axis=0, keepdims=True)
        inv = jnp.where(column == h, 0.0, 1.0 / l)
        att = (nn(vt[rows, :], p.astype(BF)) * inv).astype(BF)
        at[rows, :] = att
        ga = gat[rows, :]
        delta = jnp.sum(ga.astype(F32) * att.astype(F32), axis=0, keepdims=True)
        dp = nn(v_ref[:, a:b] * here, gat[a:b, :])
        p = p * inv
        ds = (p * (dp - delta)).astype(BF)
        dqt[rows, :] = nn(kt[rows, :], ds) * SCALE
        dkt[rows, :] = nt(qt[rows, :], ds) * SCALE
        dvt[rows, :] = nt(ga, p.astype(BF))
    dq_ref[...] = dqt[...].T
    dk_ref[...] = dkt[...].T
    dv_ref[...] = dvt[...].T
    att_ref[...] = at[...].T
    partial = nn(at[...], g)
    for t in range(6):
        big[t] = partial[:, 128 * t : 128 * t + 128]
    zero = jnp.zeros((PEERS, LANES), F32)
    for c in range(2):
        for i in range(6):
            for t in range(6):
                piece = big[t, pl.ds(6 * c + i, PEERS, stride=12), :]
                halves[c, pl.ds(6 * i + t, PEERS, stride=PART_ROWS), :] = piece
        for i in range(36, PART_ROWS):
            halves[c, pl.ds(i, PEERS, stride=PART_ROWS), :] = zero
    first, second = halves[0], halves[1]
    shape = (PEERS, PART_ROWS, LANES)
    keep_ref[...] = jnp.where(core == 0, first, second).astype(BF).reshape(shape)
    send_ref[...] = jnp.where(core == 0, second, first).astype(BF).reshape(shape)


def far_kernel(sc_ref, x_ref, w_ref, keep_ref, got_ref, back_ref, skeep_ref, ssend_ref, xs, gs, ps, ss, so):
    tile_count, head, core = sc_ref[1], sc_ref[2], sc_ref[3]
    x = x_ref[:, 0:16, :].reshape(PEERS * 16, LANES)
    xs[...] = x.astype(F32)
    gs[...] = x_ref[:, 16:40, :].astype(F32).reshape(PEERS * 24, LANES)
    lane = iota((PEERS, LANES), 1)
    parts, grads = [], []
    for ii in range(4):
        total = jnp.zeros((PEERS, LANES), F32)
        for a in range(4):
            piece = xs[pl.ds(4 * a + ii, PEERS, stride=16), :]
            piece = piece if a == 3 else pltpu.roll(piece, 32 + 32 * a, 1)
            total = jnp.where((lane >> 5) == a, piece, total)
        parts.append(total)
        grads.append(jnp.concatenate([gs[pl.ds(4 * t + ii, PEERS, stride=24), :] for t in range(6)], axis=1))
    d = jnp.concatenate(parts, axis=0)
    g = jnp.concatenate(grads, axis=0).astype(BF)
    dt = d.T
    row = iota((LANES, ROWS), 0)
    q_t = jnp.where(row < 48, dt, 0.0).astype(BF)
    q_row = jnp.where(iota((ROWS, LANES), 1) < 48, d, 0.0).astype(BF)
    lse_near = jnp.sum(jnp.where((row >= 96) & (row < 99), dt, 0.0), axis=0, keepdims=True)
    valid_key = (16 * iota((PEERS * 16, ROWS), 0) + head) < tile_count
    s = jnp.where(valid_key, nn(x, q_t) * SCALE, MASKED)
    m = jnp.maximum(jnp.max(s, axis=0, keepdims=True), lse_near)
    p = jnp.exp(s - m)
    near = jnp.exp(lse_near - m)
    l = jnp.sum(p, axis=0, keepdims=True) + near
    inv = 1.0 / l
    xt = xs[...].T.astype(BF)
    middle = (row >= 48) & (row < 96)
    att = jnp.where(middle, (nn(xt, p.astype(BF)) + near * dt) * inv, 0.0).astype(BF)
    w_head = w_ref[pl.ds(pl.multiple_of(head * HEAD_WIDTH, 16), HEAD_WIDTH), :]
    w_pad = jnp.concatenate([jnp.zeros((48, WIDTH), BF), w_head, jnp.zeros((32, WIDTH), BF)], axis=0)
    ga_t = nt(w_pad, g)
    ga_row = ga_t.T.astype(BF)
    ga_t = ga_t.astype(BF)
    delta = jnp.sum(ga_t.astype(F32) * att.astype(F32), axis=0, keepdims=True)
    dp = nn(x, ga_t)
    p = p * inv
    ds = (p * (dp - delta)).astype(BF)
    dq = nn(xt, ds) * SCALE
    hi, mid, lo = split3(m + jnp.log(l))
    e = jnp.where(row < 48, dq, att.astype(F32))
    e = jnp.where(row == 96, hi, jnp.where(row == 97, mid, jnp.where(row == 98, lo, e)))
    e = e.T
    ps[...] = nn(ds, q_row) * SCALE + nn(p.astype(BF), ga_row)
    for ii in range(4):
        for a in range(4):
            piece = e[64 * ii : 64 * ii + 64, :]
            piece = piece if a == 3 else pltpu.roll(piece, 96 - 32 * a, 1)
            at = pl.ds(4 * a + ii, PEERS, stride=16)
            ps[at, :] = jnp.where(lane >= 96, piece, ps[at, :])
    back_ref[:, 0:16, :] = ps[...].astype(BF).reshape(PEERS, 16, LANES)
    back_ref[:, 16:56, :] = (keep_ref[...].astype(F32) + got_ref[...].astype(F32)).astype(BF)
    partial = nn(att, g)
    for t in range(6):
        ss[t] = partial[48:96, 128 * t : 128 * t + 128]
    zero = jnp.zeros((4, LANES), F32)
    for c in range(2):
        for i in range(6):
            for t in range(6):
                piece = ss[t, pl.ds(6 * c + i, 4, stride=12), :]
                so[c, pl.ds(6 * i + t, 4, stride=PART_ROWS), :] = piece
        for i in range(36, PART_ROWS):
            so[c, pl.ds(i, 4, stride=PART_ROWS), :] = zero
    first, second = so[0], so[1]
    shape = (4, PART_ROWS, LANES)
    skeep_ref[...] = jnp.where(core == 0, first, second).astype(BF).reshape(shape)
    ssend_ref[...] = jnp.where(core == 0, second, first).astype(BF).reshape(shape)


def add_kernel(sc_ref, back_ref, keep_ref, got_ref, out_ref):
    out_ref[:, 0:16, :] = back_ref[:, 0:16, :]
    extra = keep_ref[...].astype(F32) + got_ref[...].astype(F32)
    out_ref[:, 16:56, :] = (back_ref[:, 16:56, :].astype(F32) + extra).astype(BF)


def final_kernel(sc_ref, q_ref, k_ref, v_ref, w_ref, x_ref, dq0_ref, dk0_ref, dv0_ref, att0_ref, ga_ref,
                 out_ref, dq_ref, dk_ref, dv_ref):
    row_start, tile_count = sc_ref[0], sc_ref[1]
    x = x_ref[:, 0:16, :].reshape(PEERS * 16, LANES)
    row, col = iota((ROWS, PEERS * 16), 0), iota((ROWS, PEERS * 16), 1)
    lane = iota((ROWS, LANES), 1)
    dkv = nn(onehot(row == 16 * (col & 15) + (col >> 6)), x)
    dkv = jnp.where(lane < 96, dkv, 0.0).astype(BF)
    source = 64 * (row & 15) + 16 * (row >> 6) + ((row >> 4) & 3)
    e = jnp.zeros((ROWS, LANES), F32)
    for a in range(4):
        piece = nn(onehot(col == source + 4 * a), x)
        piece = piece if a == 3 else pltpu.roll(piece, 32 + 32 * a, 1)
        e = jnp.where((lane >> 5) == a, piece, e)
    lse = jnp.sum(jnp.where((lane >= 96) & (lane < 99), e, 0.0), axis=1, keepdims=True)
    e = jnp.where(lane < 96, e, 0.0).astype(BF)
    own = own_head_mask()
    own32 = own.astype(F32)
    first, second = unfold(0), unfold(HEAD_WIDTH)
    att = (att0_ref[...].astype(F32) + nn(e, second) * own32).astype(BF)
    valid_row = (row_start + iota((ROWS, WIDTH), 0)) < tile_count
    out_ref[...] = jnp.where(valid_row, nn(att, w_ref[...]), 0.0).astype(BF)
    q_own = q_ref[...] * own
    ga_own = ga_ref[...] * own
    valid_key = (row_start + iota((ROWS, ROWS), 1)) < tile_count
    s = jnp.where(valid_key, nt(q_own, k_ref[...]) * SCALE, MASKED)
    p = jnp.exp(s - lse)
    delta = jnp.sum(ga_own.astype(F32) * att.astype(F32), axis=1, keepdims=True)
    ds = (p * (nt(ga_own, v_ref[...]) - delta)).astype(BF)
    dq_ref[...] = (dq0_ref[...] + (nn(ds, k_ref[...]) * SCALE + nn(e, first)) * own32).astype(BF)
    dk_ref[...] = (dk0_ref[...] + tn(ds, q_own) * SCALE + nn(dkv, first) * own32).astype(BF)
    dv_ref[...] = (dv0_ref[...] + tn(p.astype(BF), ga_own) + nn(dkv, second) * own32).astype(BF)


def call(kernel, inputs, outs, scratch=()):
    vmem = pl.BlockSpec(memory_space=pltpu.VMEM)
    return pl.pallas_call(
        kernel,
        out_shape=[jax.ShapeDtypeStruct(s, t) for s, t in outs],
        in_specs=[pl.BlockSpec(memory_space=pltpu.SMEM)] + [vmem] * (len(inputs) - 1),
        out_specs=[vmem] * len(outs),
        scratch_shapes=list(scratch),
        compiler_params=pltpu.CompilerParams(vmem_limit_bytes=56 * 1024 * 1024),
    )(*inputs)


def on_device(query_rows, key_rows, value_rows, grad_out, out_weight, tile_counts):
    q, k, v, g = query_rows[0], key_rows[0], value_rows[0], grad_out[0]
    place = lax.axis_index("seq")
    core = lax.axis_index("slide") % 2
    sc = jnp.stack([place * ROWS, tile_counts[0], place // 4, core]).astype(jnp.int32)
    other_core = [(0, 1), (1, 0), (2, 3), (3, 2)]

    (send,) = call(pack_kernel, (sc, q, k, v, g), [((PEERS, SEND_ROWS, LANES), BF)], [pltpu.VMEM((PEERS * 24, LANES), F32)])
    x = lax.all_to_all(send, "seq", 0, 0)

    tall = lambda t: pltpu.VMEM((WIDTH, ROWS), t)
    flat = (ROWS, WIDTH)
    part = (PEERS, PART_ROWS, LANES)
    dq0, dk0, dv0, att0, ga, keep, swap = call(
        near_kernel,
        (sc, q, k, v, g, out_weight),
        [(flat, F32)] * 3 + [(flat, BF)] * 2 + [(part, BF)] * 2,
        [tall(BF)] * 5 + [tall(F32)] * 3 + [pltpu.VMEM((6, WIDTH, LANES), F32), pltpu.VMEM((2, PEERS * PART_ROWS, LANES), F32)],
    )
    got = lax.ppermute(swap, "slide", other_core)

    small = (4, PART_ROWS, LANES)
    back, skeep, sswap = call(
        far_kernel,
        (sc, x, out_weight, keep, got),
        [((PEERS, BACK_ROWS, LANES), BF), (small, BF), (small, BF)],
        [
            pltpu.VMEM((PEERS * 16, LANES), F32),
            pltpu.VMEM((PEERS * 24, LANES), F32),
            pltpu.VMEM((PEERS * 16, LANES), F32),
            pltpu.VMEM((6, HEAD_WIDTH, LANES), F32),
            pltpu.VMEM((2, 4 * PART_ROWS, LANES), F32),
        ],
    )
    sgot = lax.ppermute(sswap, "slide", other_core)
    block = pl.BlockSpec((4, BACK_ROWS, LANES), lambda i, s: (s[2], 0, 0))
    whole = pl.BlockSpec(small, lambda i, s: (0, 0, 0))
    back = pl.pallas_call(
        add_kernel,
        out_shape=jax.ShapeDtypeStruct((PEERS, BACK_ROWS, LANES), BF),
        grid_spec=pltpu.PrefetchScalarGridSpec(
            num_scalar_prefetch=1, grid=(1,), in_specs=[block, whole, whole], out_specs=block
        ),
        input_output_aliases={1: 0},
    )(sc, back, skeep, sgot)
    y = lax.all_to_all(back, "seq", 0, 0)

    weight = jnp.sum(y[:, 16:56, :].astype(F32), axis=0)
    weight = lax.all_gather(weight, "slide")
    weight = (weight[0:2] + weight[2:4])[:, 0:36].reshape(12, WIDTH)

    outs = call(
        final_kernel, (sc, q, k, v, out_weight, y, dq0, dk0, dv0, att0, ga), [(flat, BF)] * 4
    )
    return tuple(o[None] for o in outs) + (weight,)


def solution(mesh):
    rows = P("slide", "seq", None)
    return jax.shard_map(
        on_device,
        mesh=mesh,
        in_specs=(rows, rows, rows, rows, P(), P("slide")),
        out_specs=(rows, rows, rows, rows, P("seq", None)),
        check_vma=False,
    )
```

time: 1560 us -> 97.4 us (0.06)
  the two profiles are of different devices: /device:TPU:4 before, /device:TPU:1 now
where the time goes in v1:
time: 97.4 us; the launch traced here: 97 us
  blocking collectives  38.7 us (40%)
  Pallas kernels  30.6 us (31%)
  starting transfers between devices  18.1 us (19%)
  waiting for transfers between devices  5.43 us (6%)
  local copies, waits for them, and re-layouts  2.08 us (2%)
  between operations  1.32 us (1%)
    all_to_all x1, blocking collectives, on_device(): y = lax.all_to_all(back, 'seq', 0, 0)  29.1 us
    pallas_call x4, Pallas kernels, call(): pl.pallas_call(kernel, out_shape=[jax.ShapeDtypeStruct(s, t) for s, t in...  28.5 us
    all_to_all x1, starting transfers between devices, on_device(): x = lax.all_to_all(send, 'seq', 0, 0)  13.6 us
    all_gather x1, blocking collectives, on_device(): weight = lax.all_gather(weight, 'slide')  9.6 us
    ppermute x1, starting transfers between devices, on_device(): sgot = lax.ppermute(sswap, 'slide', other_core)  3.56 us
    all_to_all x1, waiting for transfers between devices, on_device(): x = lax.all_to_all(send, 'seq', 0, 0)  2.41 us
    pallas_call x1, Pallas kernels, on_device(): pl.pallas_call(add_kernel, out_shape=jax.ShapeDtypeStruct((PEERS, BACK_RO...  2.16 us
  transfers between devices with their start and end apart: 3, of which 3 were waited for; matrix products, arithmetic and copies ran while one was open for 0% of the time, Pallas kernels for 13%

profile of v1, /device:TPU:1, one launch (start us, length us, event | category | flops | bytes accessed | tf_op | source)
XLA Modules:
  0.0 97.0 jit_solution(9184645986678664324)
XLA Ops:
  1.3 0.6 pad_add_fusion.sc_ref
  1.9 4.4 %shard_map.101 = bf16[64,40,128]{2,1,0:T(8,128)(2,1)} custom-call(s32[4]{0:T(128)} %pad_add_fusion.sc_ref, bf16[256,768]{1,0:T(8,128)(2,1)} %bitcast.13, bf16[256,768]{1,0:T(8,128)(2,1)} %bitcast.16, bf16[256,768]{1,0:T(8,128)(2,1)} %bitcast.19, bf16[256,768]{1,0:T(8,128)(2,1)} %bitcast.22), custom_call_target="tpu_custom_call" | custom-call | tf_op jit(solution)/shard_map/pallas_call | solution.py:272
  6.3 13.6 %all-to-all-start = ((bf16[64,40,128]{2,1,0:T(8,128)(2,1)}), bf16[64,40,128]{2,1,0:T(8,128)(2,1)S(1)}, u32[]{:S(2)}, u32[]{:S(2)}) async-start(bf16[64,40,128]{2,1,0:T(8,128)(2,1)} %shard_map.101), calls=%async_computation | async-start | bytes 1310720 | tf_op jit(solution)/shard_map/all_to_all | solution.py:290
  19.9 12.6 %shard_map.102 = (f32[256,768]{1,0:T(8,128)}, f32[256,768]{1,0:T(8,128)}, f32[256,768]{1,0:T(8,128)}, bf16[256,768]{1,0:T(8,128)(2,1)}, bf16[256,768]{1,0:T(8,12...) custom-call(s32[4]{0:T(128)} %pad_add_fusion.sc_ref, bf16[256,768]{1,0:T(8,128)(2,1)} %bitcast.14, ...), custom_call_target="tpu_custom_call" | custom-call | tf_op jit(solution)/shard_map/pallas_call | solution.py:272
  32.5 1.0 collective-permute-start
  33.4 1.9 %collective-permute-done.got_ref = bf16[64,40,128]{2,1,0:T(8,128)(2,1)S(1)} collective-permute-done((bf16[64,40,128]{2,1,0:T(8,128)(2,1)}, bf16[64,40,128]{2,1,0:T(8,128)(2,1)S(1)}, u32[]{:S(2)}, u32[]{:S(2)}) %collective-permute-start) | collective-permute-done | bytes 655392 | tf_op jit(solution)/shard_map/ppermute | solution.py:301
  35.4 0.0 copy-start.2
  35.4 2.4 %all-to-all-done.x_ref = bf16[64,40,128]{2,1,0:T(8,128)(2,1)S(1)} async-done(((bf16[64,40,128]{2,1,0:T(8,128)(2,1)}), bf16[64,40,128]{2,1,0:T(8,128)(2,1)S(1)}, u32[]{:S(2)}, u32[]{:S(2)}) %all-to-all-start) | async-done | bytes 655392 | tf_op jit(solution)/shard_map/all_to_all | solution.py:290
  37.8 0.0 copy-start.1
  37.8 0.0 copy-done.2
  37.8 0.8 copy-done.1
  38.6 5.5 %shard_map.103 = (bf16[64,56,128]{2,1,0:T(8,128)(2,1)}, bf16[4,40,128]{2,1,0:T(8,128)(2,1)}, bf16[4,40,128]{2,1,0:T(8,128)(2,1)}) custom-call(s32[4]{0:T(128)} %pad_add_fusion.sc_ref, bf16[64,40,128]{2,1,0:T(8,128)(2,1)} %copy-done.1, bf16[768,768]{1,0:T(8,128)(2,1)} %w_ref.5, bf16[64,40,128]{2,1,0:T(8,128)(2,1)} %get-tuple-element.19.keep_ref, ...), custom_call_target="tpu_custom_call" | custom-call | tf_op jit(solution)/shard_map/pallas_call | solution.py:272
  44.1 3.6 %collective-permute-start.1 = (bf16[4,40,128]{2,1,0:T(8,128)(2,1)}, bf16[4,40,128]{2,1,0:T(8,128)(2,1)S(1)}, u32[]{:S(2)}, u32[]{:S(2)}) collective-permute-start(bf16[4,40,128]{2,1,0:T(8,128)(2,1)} %get-tuple-element.23), channel_id=1, source_target_pairs={{0,64},{64,0},{128,192},{192,128},{1,65},{65,1},{129,193},{193,129... | collective-permute-start | bytes 122888 | tf_op jit(solution)/shard_map/ppermute | solution.py:316
  47.7 1.1 %collective-permute-done.1.got_ref = bf16[4,40,128]{2,1,0:T(8,128)(2,1)S(1)} collective-permute-done((bf16[4,40,128]{2,1,0:T(8,128)(2,1)}, bf16[4,40,128]{2,1,0:T(8,128)(2,1)S(1)}, u32[]{:S(2)}, u32[]{:S(2)}) %collective-permute-start.1) | collective-permute-done | bytes 40992 | tf_op jit(solution)/shard_map/ppermute | solution.py:316
  48.7 0.0 copy-start.3
  48.7 0.6 copy-done.3
  49.4 2.2 %shard_map.104 = bf16[64,56,128]{2,1,0:T(8,128)(2,1)} custom-call(s32[4]{0:T(128)} %pad_add_fusion.sc_ref, bf16[64,56,128]{2,1,0:T(8,128)(2,1)} %get-tuple-element.21.back_ref, bf16[4,40,128]{2,1,0:T(8,128)(2,1)} %get-tuple-element.22.keep_ref, bf16[4,40,128]{2,1,0:T(8,128)(2,1)} %copy-done.3), custom_call_target="tpu_custom_call", output_to_operand_aliasing={{}: (1, {})} | custom-call | tf_op jit(solution)/shard_map/pallas_call | solution.py:319
  51.5 29.1 %all_to_all.10.x_ref = bf16[64,56,128]{2,1,0:T(8,128)(2,1)S(1)} all-to-all(bf16[64,56,128]{2,1,0:T(8,128)(2,1)} %shard_map.104), channel_id=1, replica_groups=mesh['slide'=4,'seq'=64] {'seq'}, dimensions={0} | all-to-all | bytes 1835008 | tf_op jit(solution)/shard_map/all_to_all | solution.py:327
  80.7 0.0 copy-start
  80.7 0.1 convert_reduce_fusion
  80.8 9.6 %all-gather = f32[160,128]{1,0:T(8,128)S(1)} all-gather(f32[40,128]{1,0:T(8,128)S(1)} %convert_reduce_fusion), channel_id=2, replica_groups=mesh['slide'=4,'seq'=64] {'slide'}, dimensions={0}, use_global_device_ids=true | all-gather | bytes 102400 | tf_op jit(solution)/shard_map/all_gather | solution.py:330
  90.4 0.6 reshape.13
  91.0 0.0 copy-done
  91.0 6.0 %shard_map.105 = (bf16[256,768]{1,0:T(8,128)(2,1)}, bf16[256,768]{1,0:T(8,128)(2,1)}, bf16[256,768]{1,0:T(8,128)(2,1)}, bf16[256,768]{1,0:T(8,128)(2,1)}) custom-call(s32[4]{0:T(128)} %pad_add_fusion.sc_ref, bf16[256,768]{1,0:T(8,128)(2,1)} %bitcast.15, bf16[256,768]{1,0:T(8,128)(2,1)} %bitcast.18, bf16[256,768]{1,0:T(8,128)(2,1)} %bitcast.21, ...), custom_call_target="tpu_custom_call" | custom-call | tf_op jit(solution)/shard_map/pallas_call | solution.py:272
  (1 shorter events, 0.0 us)
Async XLA Ops:
  6.3 31.5 %all-to-all-start = ((bf16[64,40,128]{2,1,0:T(8,128)(2,1)}), bf16[64,40,128]{2,1,0:T(8,128)(2,1)S(1)}, u32[]{:S(2)}, u32[]{:S(2)}) async-start(bf16[64,40,128]{2,1,0:T(8,128)(2,1)} %shard_map.101), calls=%async_computation | async-start | bytes 1310720 | tf_op jit(solution)/shard_map/all_to_all | solution.py:290
  32.5 2.9 %collective-permute-start = (bf16[64,40,128]{2,1,0:T(8,128)(2,1)}, bf16[64,40,128]{2,1,0:T(8,128)(2,1)S(1)}, u32[]{:S(2)}, u32[]{:S(2)}) collective-permute-start(bf16[64,40,128]{2,1,0:T(8,128)(2,1)} %get-tuple-element.20), channel_id=1, source_target_pairs={{0,64},{64,0},{128,192},{192,128},{1,65},{65,1},{129,193},{193,129... | collective-permute-start | bytes 1966088 | tf_op jit(solution)/shard_map/ppermute | solution.py:301
  35.4 2.4 %copy-start.2 = (bf16[64,40,128]{2,1,0:T(8,128)(2,1)}, bf16[64,40,128]{2,1,0:T(8,128)(2,1)S(1)}, u32[]{:S(2)}) copy-start(bf16[64,40,128]{2,1,0:T(8,128)(2,1)S(1)} %collective-permute-done.got_ref) | copy-start | bytes 1966084
  37.8 0.8 copy-start.1
  44.1 4.6 %collective-permute-start.1 = (bf16[4,40,128]{2,1,0:T(8,128)(2,1)}, bf16[4,40,128]{2,1,0:T(8,128)(2,1)S(1)}, u32[]{:S(2)}, u32[]{:S(2)}) collective-permute-start(bf16[4,40,128]{2,1,0:T(8,128)(2,1)} %get-tuple-element.23), channel_id=1, source_target_pairs={{0,64},{64,0},{128,192},{192,128},{1,65},{65,1},{129,193},{193,129... | collective-permute-start | bytes 122888 | tf_op jit(solution)/shard_map/ppermute | solution.py:316
  48.7 0.6 copy-start.3
  80.7 10.4 %copy-start = (bf16[64,56,128]{2,1,0:T(8,128)(2,1)}, bf16[64,56,128]{2,1,0:T(8,128)(2,1)S(1)}, u32[]{:S(2)}) copy-start(bf16[64,56,128]{2,1,0:T(8,128)(2,1)S(1)} %all_to_all.10.x_ref) | copy-start | bytes 2752516

commit v2 on v1

v2 whole, which is shorter than its diff:
```python
import jax
import jax.numpy as jnp
from jax import lax
from jax.experimental import pallas as pl
from jax.experimental.pallas import tpu as pltpu
from jax.sharding import PartitionSpec as P

HEADS = 16
HEAD_WIDTH = 48
ROWS = 256
WIDTH = 768
PEERS = 64
LANES = 128
SCALE = HEAD_WIDTH ** -0.5
MASKED = -1e30
BF = jnp.bfloat16
F32 = jnp.float32
SEND_ROWS = 40
BACK_ROWS = 56
PART_ROWS = 40


def iota(shape, dim):
    return lax.broadcasted_iota(jnp.int32, shape, dim)


def head_of(feature):
    return (feature * 1366) >> 16


def onehot(mask):
    return jnp.where(mask, 1.0, 0.0).astype(BF)


def nn(a, b):
    return lax.dot_general(a, b, (((1,), (0,)), ((), ())), preferred_element_type=F32)


def nt(a, b):
    return lax.dot_general(a, b, (((1,), (1,)), ((), ())), preferred_element_type=F32)


def tn(a, b):
    return lax.dot_general(a, b, (((0,), (0,)), ((), ())), preferred_element_type=F32)


def own_head_mask():
    return onehot(head_of(iota((ROWS, WIDTH), 1)) == (iota((ROWS, WIDTH), 0) & 15))


def fold(offset):
    f = iota((WIDTH, LANES), 0)
    lane = iota((WIDTH, LANES), 1) - offset
    return onehot((f - HEAD_WIDTH * head_of(f)) == lane)


def unfold(offset):
    f = iota((LANES, WIDTH), 1)
    lane = iota((LANES, WIDTH), 0) - offset
    return onehot((f - HEAD_WIDTH * head_of(f)) == lane)


def split3(x):
    hi = x.astype(BF).astype(F32)
    mid = (x - hi).astype(BF).astype(F32)
    return hi, mid, (x - hi - mid).astype(BF).astype(F32)


def pack_kernel(sc_ref, q_ref, k_ref, v_ref, g_ref, out_ref, next_ref, rows, grads):
    for n in range(5):
        next_ref[n] = sc_ref[n]
    row_start, tile_count = sc_ref[0], sc_ref[1]
    own = own_head_mask()
    q_own = q_ref[...] * own
    valid_key = (row_start + iota((ROWS, ROWS), 1)) < tile_count
    s = jnp.where(valid_key, nt(q_own, k_ref[...]) * SCALE, MASKED)
    m = jnp.max(s, axis=1, keepdims=True)
    p = jnp.exp(s - m)
    l = jnp.sum(p, axis=1, keepdims=True)
    o = (nn(p.astype(BF), v_ref[...]) * (1.0 / l)).astype(BF) * own
    hi, mid, lo = split3(m + jnp.log(l))
    first, second = fold(0), fold(HEAD_WIDTH)
    lane = iota((ROWS, LANES), 1)
    d = nn(q_own, first) + nn(o, second)
    d = jnp.where(lane == 96, hi, jnp.where(lane == 97, mid, jnp.where(lane == 98, lo, d)))
    c = nn(k_ref[...] * own, first) + nn(v_ref[...] * own, second)
    late = iota((16, LANES), 1) >= 96
    for a in range(4):
        turned = d if a == 3 else pltpu.roll(d, 96 - 32 * a, 1)
        for ii in range(4):
            i = 4 * a + ii
            for j in range(4):
                at = 16 * (4 * j + ii)
                rows[pl.ds(16 * j + i, 16, stride=64), :] = jnp.where(late, turned[at : at + 16], c[16 * i : 16 * i + 16])
    out_ref[:, 0:16, :] = rows[...].astype(BF).reshape(PEERS, 16, LANES)
    valid_row = (row_start + iota((ROWS, WIDTH), 0)) < tile_count
    g = jnp.where(valid_row, g_ref[...].astype(F32), 0.0)
    for j in range(4):
        for ii in range(4):
            at = 16 * (4 * j + ii)
            for t in range(6):
                grads[pl.ds(24 * j + 4 * t + ii, 16, stride=96), :] = g[at : at + 16, 128 * t : 128 * t + 128]
    out_ref[:, 16:40, :] = grads[...].astype(BF).reshape(PEERS, 24, LANES)


def head_window(h):
    f = HEAD_WIDTH * h
    a, b = f // LANES * LANES, -(-(f + HEAD_WIDTH) // LANES) * LANES
    lane = a + iota((ROWS, b - a), 1)
    return slice(a, b), slice(f, f + HEAD_WIDTH), onehot((lane >= f) & (lane < f + HEAD_WIDTH))


def forward_kernel(sc_ref, q_ref, k_ref, v_ref, g_ref, at_ref, lse_ref, keep_ref, send_ref, qt, vt, big, part):
    row_start, tile_count, core = sc_ref[0], sc_ref[1], sc_ref[3]
    valid_row = (row_start + iota((ROWS, WIDTH), 0)) < tile_count
    g = jnp.where(valid_row, g_ref[...].astype(F32), 0.0).astype(BF)
    qt[...] = q_ref[...].T
    vt[...] = v_ref[...].T
    valid_key = (row_start + iota((ROWS, ROWS), 0)) < tile_count
    column = iota((1, ROWS), 1) & 15
    for h in range(HEADS):
        window, rows, here = head_window(h)
        s = jnp.where(valid_key, nn(k_ref[:, window] * here, qt[window, :]) * SCALE, MASKED)
        m = jnp.max(s, axis=0, keepdims=True)
        p = jnp.exp(s - m)
        l = jnp.sum(p, axis=0, keepdims=True)
        inv = jnp.where(column == h, 0.0, 1.0 / l)
        at_ref[rows, :] = (nn(vt[rows, :], p.astype(BF)) * inv).astype(BF)
        lse_ref[h : h + 1, :] = jnp.where(column == h, 1e30, m + jnp.log(l))
    partial = nn(at_ref[...], g)
    for t in range(6):
        big[t] = partial[:, 128 * t : 128 * t + 128]
    zero = jnp.zeros((PEERS, LANES), F32)
    for i in range(36, PART_ROWS):
        part[pl.ds(i, PEERS, stride=PART_ROWS), :] = zero
    for ref, c in ((keep_ref, core), (send_ref, 1 - core)):
        for i in range(6):
            for t in range(6):
                part[pl.ds(6 * i + t, PEERS, stride=PART_ROWS), :] = big[t, pl.ds(6 * c + i, PEERS, stride=12), :]
        ref[...] = part[...].astype(BF).reshape(PEERS, PART_ROWS, LANES)


def join_kernel(sc_ref, keep_ref, got_ref, out_ref):
    out_ref[:, 0:16, :] = jnp.zeros((PEERS, 16, LANES), BF)
    out_ref[:, 16:56, :] = (keep_ref[...].astype(F32) + got_ref[...].astype(F32)).astype(BF)


def backward_kernel(sc_ref, q_ref, k_ref, v_ref, g_ref, w_ref, at_ref, lse_ref, strided_ref,
                    dq_ref, dk_ref, dv_ref, layer_ref, ga_ref, s_ref, dp_ref, pass_ref, qt, kt, gat, dqt, dkt, dvt):
    row_start, tile_count = sc_ref[0], sc_ref[1]
    pass_ref[...] = strided_ref[...]
    valid_row = (row_start + iota((ROWS, WIDTH), 0)) < tile_count
    g = jnp.where(valid_row, g_ref[...].astype(F32), 0.0).astype(BF)
    gat[...] = nt(w_ref[...], g).astype(BF)
    ga_row = nt(g, w_ref[...]).astype(BF)
    qt[...] = q_ref[...].T
    kt[...] = k_ref[...].T
    valid_key = (row_start + iota((ROWS, ROWS), 0)) < tile_count
    for h in range(HEADS):
        window, rows, here = head_window(h)
        s = jnp.where(valid_key, nn(k_ref[:, window] * here, qt[window, :]) * SCALE, MASKED)
        p = jnp.exp(s - lse_ref[h : h + 1, :])
        ga = gat[rows, :]
        delta = jnp.sum(ga.astype(F32) * at_ref[rows, :].astype(F32), axis=0, keepdims=True)
        dp = nn(v_ref[:, window] * here, gat[window, :])
        ds = (p * (dp - delta)).astype(BF)
        dqt[rows, :] = nn(kt[rows, :], ds) * SCALE
        dkt[rows, :] = nt(qt[rows, :], ds) * SCALE
        dvt[rows, :] = nt(ga, p.astype(BF))
    dq_ref[...] = dqt[...].T
    dk_ref[...] = dkt[...].T
    dv_ref[...] = dvt[...].T
    own = own_head_mask()
    ga_own = ga_row * own
    ga_ref[...] = ga_own
    layer_ref[...] = nn(at_ref[...].T, w_ref[...])
    valid_key = (row_start + iota((ROWS, ROWS), 1)) < tile_count
    s_ref[...] = jnp.where(valid_key, nt(q_ref[...] * own, k_ref[...]) * SCALE, MASKED)
    dp_ref[...] = nt(ga_own, v_ref[...])


def far_kernel(sc_ref, x_ref, w_ref, joined_ref, back_ref, strided_ref, xs, gs, ps):
    tile_count, head = sc_ref[1], sc_ref[2]
    x = x_ref[:, 0:16, :].reshape(PEERS * 16, LANES)
    xs[...] = x.astype(F32)
    gs[...] = x_ref[:, 16:40, :].astype(F32).reshape(PEERS * 24, LANES)
    lane = iota((PEERS, LANES), 1)
    parts, grads = [], []
    for ii in range(4):
        total = jnp.zeros((PEERS, LANES), F32)
        for a in range(4):
            piece = xs[pl.ds(4 * a + ii, PEERS, stride=16), :]
            piece = piece if a == 3 else pltpu.roll(piece, 32 + 32 * a, 1)
            total = jnp.where((lane >> 5) == a, piece, total)
        parts.append(total)
        grads.append(jnp.concatenate([gs[pl.ds(4 * t + ii, PEERS, stride=24), :] for t in range(6)], axis=1))
    d = jnp.concatenate(parts, axis=0)
    g = jnp.concatenate(grads, axis=0).astype(BF)
    dt = d.T
    row = iota((LANES, ROWS), 0)
    q_t = jnp.where(row < 48, dt, 0.0).astype(BF)
    q_row = jnp.where(iota((ROWS, LANES), 1) < 48, d, 0.0).astype(BF)
    lse_near = jnp.sum(jnp.where((row >= 96) & (row < 99), dt, 0.0), axis=0, keepdims=True)
    valid_key = (16 * iota((PEERS * 16, ROWS), 0) + head) < tile_count
    s = jnp.where(valid_key, nn(x, q_t) * SCALE, MASKED)
    m = jnp.maximum(jnp.max(s, axis=0, keepdims=True), lse_near)
    p = jnp.exp(s - m)
    near = jnp.exp(lse_near - m)
    l = jnp.sum(p, axis=0, keepdims=True) + near
    inv = 1.0 / l
    xt = xs[...].T.astype(BF)
    middle = (row >= 48) & (row < 96)
    att = jnp.where(middle, (nn(xt, p.astype(BF)) + near * dt) * inv, 0.0).astype(BF)
    w_pad = jnp.concatenate([jnp.zeros((48, WIDTH), BF), w_ref[...], jnp.zeros((32, WIDTH), BF)], axis=0)
    ga_t = nt(w_pad, g)
    ga_row = ga_t.T.astype(BF)
    ga_t = ga_t.astype(BF)
    delta = jnp.sum(ga_t.astype(F32) * att.astype(F32), axis=0, keepdims=True)
    dp = nn(x, ga_t)
    p = p * inv
    ds = (p * (dp - delta)).astype(BF)
    dq = nn(xt, ds) * SCALE
    hi, mid, lo = split3(m + jnp.log(l))
    e = jnp.where(row < 48, dq, att.astype(F32))
    e = jnp.where(row == 96, hi, jnp.where(row == 97, mid, jnp.where(row == 98, lo, e)))
    e = e.T
    ps[...] = nn(ds, q_row) * SCALE + nn(p.astype(BF), ga_row)
    for a in range(4):
        turned = e if a == 3 else pltpu.roll(e, 96 - 32 * a, 1)
        for ii in range(4):
            at = pl.ds(4 * a + ii, PEERS, stride=16)
            ps[at, :] = jnp.where(lane >= 96, turned[64 * ii : 64 * ii + 64], ps[at, :])
    back_ref[...] = ps[...].astype(BF).reshape(PEERS, 16, LANES)
    partial = nn(att, g)
    for j in range(4):
        strided_ref[j] = partial[48 + 12 * j : 60 + 12 * j]


def final_kernel(sc_ref, q_ref, k_ref, w_ref, x_ref, s_ref, dp_ref, ga_ref, layer_ref, dq0_ref, dk0_ref, dv0_ref,
                 out_ref, dq_ref, dk_ref, dv_ref, xs):
    row_start, tile_count = sc_ref[0], sc_ref[1]
    xs[...] = x_ref[:, 0:16, :].astype(F32).reshape(PEERS * 16, LANES)
    lane = iota((16, LANES), 1)
    e_rows = [None] * 16
    dkv_rows = []
    for i in range(16):
        a, ii = i // 4, i % 4
        total = None
        for j in range(4):
            piece = xs[pl.ds(16 * j + i, 16, stride=64), :]
            total = piece if total is None else total + piece
            moved = piece if a == 3 else pltpu.roll(piece, 32 + 32 * a, 1)
            old = e_rows[4 * j + ii]
            e_rows[4 * j + ii] = moved if old is None else jnp.where((lane >> 5) == a, moved, old)
        dkv_rows.append(total)
    dkv = jnp.concatenate(dkv_rows, axis=0)
    e = jnp.concatenate(e_rows, axis=0)
    lane = iota((ROWS, LANES), 1)
    dkv = jnp.where(lane < 96, dkv, 0.0).astype(BF)
    lse = jnp.sum(jnp.where((lane >= 96) & (lane < 99), e, 0.0), axis=1, keepdims=True)
    e = jnp.where(lane < 96, e, 0.0).astype(BF)
    own = own_head_mask()
    own32 = own.astype(F32)
    first, second = unfold(0), unfold(HEAD_WIDTH)
    att = nn(e, second).astype(BF) * own
    valid_row = (row_start + iota((ROWS, WIDTH), 0)) < tile_count
    out_ref[...] = jnp.where(valid_row, layer_ref[...] + nn(att, w_ref[...]), 0.0).astype(BF)
    q_own = q_ref[...] * own
    ga_own = ga_ref[...]
    p = jnp.exp(s_ref[...] - lse)
    delta = jnp.sum(ga_own.astype(F32) * att.astype(F32), axis=1, keepdims=True)
    ds = (p * (dp_ref[...] - delta)).astype(BF)
    dq_ref[...] = (dq0_ref[...] + (nn(ds, k_ref[...]) * SCALE + nn(e, first)) * own32).astype(BF)
    dk_ref[...] = (dk0_ref[...] + tn(ds, q_own) * SCALE + nn(dkv, first) * own32).astype(BF)
    dv_ref[...] = (dv0_ref[...] + tn(p.astype(BF), ga_own) + nn(dkv, second) * own32).astype(BF)


def call(kernel, inputs, outs, scratch=(), scalars=False):
    vmem = pl.BlockSpec(memory_space=pltpu.VMEM)
    smem = pl.BlockSpec(memory_space=pltpu.SMEM)
    return pl.pallas_call(
        kernel,
        out_shape=[jax.ShapeDtypeStruct(s, t) for s, t in outs],
        in_specs=[smem] + [vmem] * (len(inputs) - 1),
        out_specs=[vmem] * (len(outs) - 1) + [smem if scalars else vmem],
        scratch_shapes=[pltpu.VMEM(s, t) for s, t in scratch],
        compiler_params=pltpu.CompilerParams(vmem_limit_bytes=56 * 1024 * 1024),
    )(*inputs)


def on_device(query_rows, key_rows, value_rows, grad_out, out_weight, tile_counts):
    q, k, v, g = query_rows[0], key_rows[0], value_rows[0], grad_out[0]
    place = lax.axis_index("seq")
    slide = lax.axis_index("slide")
    core, far_x = slide % 2, slide // 2
    sc = jnp.stack([place * ROWS, tile_counts[0], place // 4, core, far_x]).astype(jnp.int32)
    other_core = [(0, 1), (1, 0), (2, 3), (3, 2)]
    other_x = [(0, 2), (2, 0), (1, 3), (3, 1)]
    flat, tall = (ROWS, WIDTH), (WIDTH, ROWS)

    send, sc2 = call(
        pack_kernel, (sc, q, k, v, g), [((PEERS, SEND_ROWS, LANES), BF), ((5,), jnp.int32)],
        [((PEERS * 16, LANES), F32), ((PEERS * 24, LANES), F32)], scalars=True,
    )
    x = lax.all_to_all(send, "seq", 0, 0)

    part = (PEERS, PART_ROWS, LANES)
    at0, lse0, keep, swap = call(
        forward_kernel, (sc2, q, k, v, g), [(tall, BF), ((HEADS, ROWS), F32), (part, BF), (part, BF)],
        [(tall, BF), (tall, BF), ((6, WIDTH, LANES), F32), ((PEERS * PART_ROWS, LANES), F32)],
    )
    got = lax.ppermute(swap, "slide", other_core)
    (joined,) = call(join_kernel, (sc2, keep, got), [((PEERS, BACK_ROWS, LANES), BF)])

    w_head = lax.dynamic_slice_in_dim(out_weight, place // 4 * HEAD_WIDTH, HEAD_WIDTH, 0)
    whole = lambda *shape: pl.BlockSpec(shape, lambda i: (0,) * len(shape))
    back, strided = pl.pallas_call(
        far_kernel,
        grid=(1,),
        out_shape=[jax.ShapeDtypeStruct((PEERS, BACK_ROWS, LANES), BF), jax.ShapeDtypeStruct((4, 12, WIDTH), F32)],
        in_specs=[
            pl.BlockSpec(memory_space=pltpu.SMEM),
            whole(PEERS, SEND_ROWS, LANES),
            whole(HEAD_WIDTH, WIDTH),
            pl.BlockSpec(memory_space=pl.ANY),
        ],
        out_specs=[whole(PEERS, 16, LANES), whole(4, 12, WIDTH)],
        scratch_shapes=[pltpu.VMEM((PEERS * n, LANES), F32) for n in (16, 24, 16)],
        input_output_aliases={3: 0},
        compiler_params=pltpu.CompilerParams(vmem_limit_bytes=56 * 1024 * 1024),
    )(sc, x, w_head, joined)
    y = lax.all_to_all(back, "seq", 0, 0)

    dq0, dk0, dv0, layer0, ga, s0, dp0, strided = call(
        backward_kernel, (sc, q, k, v, g, out_weight, at0, lse0, strided),
        [(flat, F32)] * 4 + [(flat, BF)] + [((ROWS, ROWS), F32)] * 2 + [((4, 12, WIDTH), F32)],
        [(tall, BF)] * 3 + [(tall, F32)] * 3,
    )
    rest = jnp.sum(y[:, 16:52, :].astype(F32), axis=0).reshape(6, WIDTH)
    weight = lax.dynamic_update_slice_in_dim(jnp.zeros((12, WIDTH), F32), rest, 6 * core, 0)
    quarter = place % 4
    for step in range(4):
        mine = lax.dynamic_index_in_dim(strided, (quarter + step) % 4, 0, keepdims=False)
        if step:
            ring = [(d, d // 4 * 4 + (d + step) % 4) for d in range(PEERS)]
            mine = lax.ppermute(mine, "seq", ring)
        weight = weight + mine
    weight = weight + sum(lax.ppermute(weight, "slide", [(n, n ^ bits) for n in range(4)]) for bits in (2, 3, 1))

    outs = call(
        final_kernel, (sc, q, k, out_weight, y, s0, dp0, ga, layer0, dq0, dk0, dv0), [(flat, BF)] * 4,
        [((PEERS * 16, LANES), F32)],
    )
    return tuple(o[None] for o in outs) + (weight,)


def solution(mesh):
    rows = P("slide", "seq", None)
    return jax.shard_map(
        on_device,
        mesh=mesh,
        in_specs=(rows, rows, rows, rows, P(), P("slide")),
        out_specs=(rows, rows, rows, rows, P("seq", None)),
        check_vma=False,
    )
```

time: 97.4 us -> 87.9 us (0.902)
  blocking collectives: 38.7 us -> 0 us
  starting transfers between devices: 18.1 us -> 35 us
  waiting for transfers between devices: 5.43 us -> 10.3 us
  Pallas kernels: 30.6 us -> 33.8 us
  local copies, waits for them, and re-layouts: 2.08 us -> 5.03 us
    all_to_all x1 -> x0, blocking collectives: 29.1 us -> none  [on_device(): y = lax.all_to_all(back, 'seq', 0, 0)]
    all_gather x1 -> x0, blocking collectives: 9.6 us -> none  [on_device(): weight = lax.all_gather(weight, 'slide')]
    ppermute x1 -> x6, starting transfers between devices: 3.56 us -> 12.8 us  [the longest x3 8.29 us: on_device(): lax.ppermute(weight, 'slide', [(n, n ^ bits) for n in range(4)])]
    all_to_all x0 -> x1, starting transfers between devices: none -> 7.68 us  [on_device(): y = lax.all_to_all(back, 'seq', 0, 0)]
    all_to_all x0 -> x1, waiting for transfers between devices: none -> 5.93 us  [on_device(): y = lax.all_to_all(back, 'seq', 0, 0)]
    pallas_call x1, Pallas kernels: 2.16 us -> 4.21 us  [on_device(): pl.pallas_call(far_kernel, grid=(1,), out_shape=[jax.ShapeDtypeStruct((PE...]
    ppermute x1, waiting for transfers between devices: 1.93 us -> 0.41 us  [on_device(): got = lax.ppermute(swap, 'slide', other_core)]
    dynamic_slice x0 -> x1, local copies, waits for them, and re-layouts: none -> 1.52 us  [on_device(): lax.dynamic_slice_in_dim(out_weight, place // 4 * HEAD_WIDTH, HEAD_WIDTH, 0)]
  transfers between devices with their start and end apart: 3 -> 9, of which waited for: 3 -> 3; matrix products, arithmetic and copies ran while one was open for 0% -> 4% of each run, Pallas kernels for 13% -> 29%
where the time goes in v2:
time: 87.9 us; the launch traced here: 87.3 us
  starting transfers between devices  35 us (40%)
  Pallas kernels  33.8 us (38%)
  waiting for transfers between devices  10.3 us (12%)
  local copies, waits for them, and re-layouts  5.03 us (6%)
  other arithmetic  1.67 us (2%)
  between operations  1.5 us (2%)
    pallas_call x5, Pallas kernels, call(): pl.pallas_call(kernel, out_shape=[jax.ShapeDtypeStruct(s, t) for s, t in...  29.6 us
    all_to_all x1, starting transfers between devices, on_device(): x = lax.all_to_all(send, 'seq', 0, 0)  13.6 us
    ppermute x3, starting transfers between devices, on_device(): lax.ppermute(weight, 'slide', [(n, n ^ bits) for n in range(4)])  8.29 us
    all_to_all x1, starting transfers between devices, on_device(): y = lax.all_to_all(back, 'seq', 0, 0)  7.68 us
    all_to_all x1, waiting for transfers between devices, on_device(): y = lax.all_to_all(back, 'seq', 0, 0)  5.93 us
    ppermute x3, starting transfers between devices, on_device(): mine = lax.ppermute(mine, 'seq', ring)  4.48 us
    pallas_call x1, Pallas kernels, on_device(): pl.pallas_call(far_kernel, grid=(1,), out_shape=[jax.ShapeDtypeStruct((PE...  4.21 us
    all_to_all x1, waiting for transfers between devices, on_device(): x = lax.all_to_all(send, 'seq', 0, 0)  3.91 us
  transfers between devices with their start and end apart: 9, of which 3 were waited for; matrix products, arithmetic and copies ran while one was open for 4% of the time, Pallas kernels for 29%

profile of v2, /device:TPU:1, one launch (start us, length us, event | category | flops | bytes accessed | tf_op | source)
XLA Modules:
  0.0 87.3 jit_solution(15439848581001288054)
XLA Ops:
  1.3 0.7 stack.19.sc_ref
  2.0 4.3 %shard_map.101 = (bf16[64,40,128]{2,1,0:T(8,128)(2,1)}, s32[5]{0:T(128)}) custom-call(s32[5]{0:T(128)} %stack.19.sc_ref, bf16[256,768]{1,0:T(8,128)(2,1)} %bitcast.22, bf16[256,768]{1,0:T(8,128)(2,1)} %bitcast.26, bf16[256,768]{1,0:T(8,128)(2,1)} %bitcast.30, bf16[256,768]{1,0:T(8,128)(2,1)} %bitcast.33), custom_call_target="tpu_custom_call" | custom-call | tf_op jit(solution)/shard_map/pallas_call | solution.py:281
  6.2 13.6 %all-to-all-start = ((bf16[64,40,128]{2,1,0:T(8,128)(2,1)}), bf16[64,40,128]{2,1,0:T(8,128)(2,1)S(1)}, u32[]{:S(2)}, u32[]{:S(2)}) async-start(bf16[64,40,128]{2,1,0:T(8,128)(2,1)} %get-tuple-element.25), calls=%async_computation | async-start | bytes 1310720 | tf_op jit(solution)/shard_map/all_to_all | solution.py:305
  19.9 7.8 %shard_map.102 = (bf16[768,256]{1,0:T(8,128)(2,1)}, f32[16,256]{1,0:T(8,128)}, bf16[64,40,128]{2,1,0:T(8,128)(2,1)}, bf16[64,40,128]{2,1,0:T(8,128)(2,1)}) custom-call(s32[5]{0:T(128)} %get-tuple-element.26.sc_ref, bf16[256,768]{1,0:T(8,128)(2,1)} %bitcast.23, bf16[256,768]{1,0:T(8,128)(2,1)} %bitcast.27, bf16[256,768]{1,0:T(8,128)(2,1)} %bitcast.31, ...), custom_call_target="tpu_custom_call" | custom-call | tf_op jit(solution)/shard_map/pallas_call | solution.py:281
  27.7 1.0 %collective-permute-start = (bf16[64,40,128]{2,1,0:T(8,128)(2,1)}, bf16[64,40,128]{2,1,0:T(8,128)(2,1)S(1)}, u32[]{:S(2)}, u32[]{:S(2)}) collective-permute-start(bf16[64,40,128]{2,1,0:T(8,128)(2,1)} %get-tuple-element.28), channel_id=1, source_target_pairs={{0,64},{64,0},{128,192},{192,128},{1,65},{65,1},{129,193},{193,129... | collective-permute-start | bytes 1966088 | tf_op jit(solution)/shard_map/ppermute | solution.py:312
  28.6 1.5 %constant_dynamic-slice_fusion.w_ref = bf16[48,768]{1,0:T(8,128)(2,1)} fusion(bf16[768,768]{1,0:T(8,128)(2,1)} %w_ref.3, s32[]{:T(128)S(6)} %select_n.61), kind=kLoop, calls=%fused_computation.8 | loop fusion | bytes 147460 | tf_op jit(solution)/shard_map/dynamic_slice | solution.py:315
  30.2 0.4 collective-permute-done.got_ref
  30.6 0.8 copy-done.2
  31.4 2.4 %shard_map.103.joined_ref = bf16[64,56,128]{2,1,0:T(8,128)(2,1)} custom-call(s32[5]{0:T(128)} %get-tuple-element.26.sc_ref, bf16[64,40,128]{2,1,0:T(8,128)(2,1)} %get-tuple-element.27.keep_ref, bf16[64,40,128]{2,1,0:T(8,128)(2,1)} %copy-done.2), custom_call_target="tpu_custom_call" | custom-call | tf_op jit(solution)/shard_map/pallas_call | solution.py:281
  33.8 3.9 %all-to-all-done.x_ref = bf16[64,40,128]{2,1,0:T(8,128)(2,1)S(1)} async-done(((bf16[64,40,128]{2,1,0:T(8,128)(2,1)}), bf16[64,40,128]{2,1,0:T(8,128)(2,1)S(1)}, u32[]{:S(2)}, u32[]{:S(2)}) %all-to-all-start) | async-done | bytes 655392 | tf_op jit(solution)/shard_map/all_to_all | solution.py:305
  37.7 0.9 %copy-done.1 = bf16[64,40,128]{2,1,0:T(8,128)(2,1)} copy-done((bf16[64,40,128]{2,1,0:T(8,128)(2,1)}, bf16[64,40,128]{2,1,0:T(8,128)(2,1)S(1)}, u32[]{:S(2)}) %copy-start.1) | copy-done | bytes 655384
  38.6 4.2 %shard_map.104 = (bf16[64,56,128]{2,1,0:T(8,128)(2,1)}, f32[4,12,768]{2,1,0:T(8,128)}) custom-call(s32[5]{0:T(128)} %stack.19.sc_ref, bf16[64,40,128]{2,1,0:T(8,128)(2,1)} %copy-done.1, bf16[48,768]{1,0:T(8,128)(2,1)} %constant_dynamic-slice_fusion.w_ref, bf16[64,56,128]{2,1,0:T(8,128)(2,1)} %shard_map.103.joined_ref), custom_call_target="tpu_custom_call", output_to_operand_aliasing={{0}: (3, {})} | custom-call | tf_op jit(solution)/shard_map/pallas_call | solution.py:317
  42.8 7.7 %all-to-all-start.1 = ((bf16[64,56,128]{2,1,0:T(8,128)(2,1)}), bf16[64,56,128]{2,1,0:T(8,128)(2,1)S(1)}, u32[]{:S(2)}, u32[]{:S(2)}) async-start(bf16[64,56,128]{2,1,0:T(8,128)(2,1)} %get-tuple-element.29), calls=%async_computation.1 | async-start | bytes 1835008 | tf_op jit(solution)/shard_map/all_to_all | solution.py:332
  50.6 9.8 %shard_map.105 = (f32[256,768]{1,0:T(8,128)}, f32[256,768]{1,0:T(8,128)}, f32[256,768]{1,0:T(8,128)}, f32[256,768]{1,0:T(8,128)}, bf16[256,768]{1,0:T(8,128)(2,1...) custom-call(s32[5]{0:T(128)} %stack.19.sc_ref, bf16[256,768]{1,0:T(8,128)(2,1)} %bitcast.24, ...), custom_call_target="tpu_custom_call" | custom-call | tf_op jit(solution)/shard_map/pallas_call | solution.py:281
  60.4 0.9 %dynamic-slice_bitcast_fusion.2 = (f32[12,768]{1,0:T(8,128)S(1)}, f32[12,768]{1,0:T(8,128)S(1)}, f32[12,768]{1,0:T(8,128)S(1)}, f32[12,768]{1,0:T(8,128)S(1)}) fusion(f32[4,12,768]{2,1,0:T(8,128)} %get-tuple-element.44, s32[]{:T(128)S(6)} %select_n.69, s32[]{:T(128)S(6)} %select_n.73, s32[]{:T(128)S(6)} %select_n.71, s32[]{:T(128)S(6)} %select_n.64), kind=kLoop, calls=%fused_computation.5 | loop fusion | bytes 294928 | tf_op jit(solution)/shard_map/jit(dynamic_index_in_dim)/squeeze | solution.py:343
  61.3 0.9 %collective-permute-start.1 = (f32[12,768]{1,0:T(8,128)S(1)}, f32[12,768]{1,0:T(8,128)S(1)}, u32[]{:S(2)}, u32[]{:S(2)}) collective-permute-start(f32[12,768]{1,0:T(8,128)S(1)} %get-tuple-element.45), channel_id=1, source_target_pairs={{0,1},{1,2},{2,3},{3,0},{4,5},{5,6},{6,7},{7,4},{8,9},{9,10},{10,1... | collective-permute-start | bytes 110600 | tf_op jit(solution)/shard_map/ppermute | solution.py:346
  62.2 2.4 %collective-permute-start.2 = (f32[12,768]{1,0:T(8,128)S(1)}, f32[12,768]{1,0:T(8,128)S(1)}, u32[]{:S(2)}, u32[]{:S(2)}) collective-permute-start(f32[12,768]{1,0:T(8,128)S(1)} %get-tuple-element.47), channel_id=1, source_target_pairs={{0,2},{1,3},{2,0},{3,1},{4,6},{5,7},{6,4},{7,5},{8,10},{9,11},{10,... | collective-permute-start | bytes 110600 | tf_op jit(solution)/shard_map/ppermute | solution.py:346
  64.6 1.2 %collective-permute-start.3 = (f32[12,768]{1,0:T(8,128)S(1)}, f32[12,768]{1,0:T(8,128)S(1)}, u32[]{:S(2)}, u32[]{:S(2)}) collective-permute-start(f32[12,768]{1,0:T(8,128)S(1)} %get-tuple-element.46), channel_id=1, source_target_pairs={{0,3},{1,0},{2,1},{3,2},{4,7},{5,4},{6,5},{7,6},{8,11},{9,8},{10,9... | collective-permute-start | bytes 110600 | tf_op jit(solution)/shard_map/ppermute | solution.py:346
  65.8 5.9 %all-to-all-done.1.x_ref = bf16[64,56,128]{2,1,0:T(8,128)(2,1)S(1)} async-done(((bf16[64,56,128]{2,1,0:T(8,128)(2,1)}), bf16[64,56,128]{2,1,0:T(8,128)(2,1)S(1)}, u32[]{:S(2)}, u32[]{:S(2)}) %all-to-all-start.1) | async-done | bytes 917536 | tf_op jit(solution)/shard_map/all_to_all | solution.py:332
  71.9 0.9 %bitcast_add_fusion = f32[6,768]{1,0:T(8,128)S(1)} fusion(f32[6,768]{1,0:T(8,128)S(1)} %reshape.14, f32[4,12,768]{2,1,0:T(8,128)} %get-tuple-element.44, s32[]{:T(128)S(6)} %select_n.65, s32[]{:T(128)S(6)} %select_n.67), kind=kLoop, calls=%fused_computation.7 | loop fusion | flops 4608 | bytes 55304 | tf_op jit(solution)/shard_map/dynamic_update_slice | solution.py:340
  73.1 2.5 %collective-permute-start.4 = (f32[12,768]{1,0:T(8,128)S(1)}, f32[12,768]{1,0:T(8,128)S(1)}, u32[]{:S(2)}, u32[]{:S(2)}) collective-permute-start(f32[12,768]{1,0:T(8,128)S(1)} %add_add_fusion.1), channel_id=1, source_target_pairs={{0,128},{64,192},{128,0},{192,64},{1,129},{65,193},{129,1},{193,65... | collective-permute-start | bytes 110600 | tf_op jit(solution)/shard_map/ppermute | solution.py:348
  75.6 5.7 %collective-permute-start.5 = (f32[12,768]{1,0:T(8,128)S(1)}, f32[12,768]{1,0:T(8,128)S(1)}, u32[]{:S(2)}, u32[]{:S(2)}) collective-permute-start(f32[12,768]{1,0:T(8,128)S(1)} %add_add_fusion.1), channel_id=1, source_target_pairs={{0,192},{64,128},{128,64},{192,0},{1,193},{65,129},{129,65},{193,1... | collective-permute-start | bytes 110600 | tf_op jit(solution)/shard_map/ppermute | solution.py:348
  81.3 5.3 %shard_map.106 = (bf16[256,768]{1,0:T(8,128)(2,1)}, bf16[256,768]{1,0:T(8,128)(2,1)}, bf16[256,768]{1,0:T(8,128)(2,1)}, bf16[256,768]{1,0:T(8,128)(2,1)}) custom-call(s32[5]{0:T(128)} %stack.19.sc_ref, bf16[256,768]{1,0:T(8,128)(2,1)} %bitcast.25, bf16[256,768]{1,0:T(8,128)(2,1)} %bitcast.29, bf16[768,768]{1,0:T(8,128)(2,1)} %w_ref.3, ...), custom_call_target="tpu_custom_call" | custom-call | tf_op jit(solution)/shard_map/pallas_call | solution.py:281
  86.7 0.6 add_add_fusion
  (15 shorter events, 0.4 us)
Async XLA Ops:
  6.2 31.5 %all-to-all-start = ((bf16[64,40,128]{2,1,0:T(8,128)(2,1)}), bf16[64,40,128]{2,1,0:T(8,128)(2,1)S(1)}, u32[]{:S(2)}, u32[]{:S(2)}) async-start(bf16[64,40,128]{2,1,0:T(8,128)(2,1)} %get-tuple-element.25), calls=%async_computation | async-start | bytes 1310720 | tf_op jit(solution)/shard_map/all_to_all | solution.py:305
  27.7 2.9 %collective-permute-start = (bf16[64,40,128]{2,1,0:T(8,128)(2,1)}, bf16[64,40,128]{2,1,0:T(8,128)(2,1)S(1)}, u32[]{:S(2)}, u32[]{:S(2)}) collective-permute-start(bf16[64,40,128]{2,1,0:T(8,128)(2,1)} %get-tuple-element.28), channel_id=1, source_target_pairs={{0,64},{64,0},{128,192},{192,128},{1,65},{65,1},{129,193},{193,129... | collective-permute-start | bytes 1966088 | tf_op jit(solution)/shard_map/ppermute | solution.py:312
  30.6 0.8 copy-start.2
  37.7 0.9 %copy-start.1 = (bf16[64,40,128]{2,1,0:T(8,128)(2,1)}, bf16[64,40,128]{2,1,0:T(8,128)(2,1)S(1)}, u32[]{:S(2)}) copy-start(bf16[64,40,128]{2,1,0:T(8,128)(2,1)S(1)} %all-to-all-done.x_ref) | copy-start | bytes 1966084
  42.8 28.9 %all-to-all-start.1 = ((bf16[64,56,128]{2,1,0:T(8,128)(2,1)}), bf16[64,56,128]{2,1,0:T(8,128)(2,1)S(1)}, u32[]{:S(2)}, u32[]{:S(2)}) async-start(bf16[64,56,128]{2,1,0:T(8,128)(2,1)} %get-tuple-element.29), calls=%async_computation.1 | async-start | bytes 1835008 | tf_op jit(solution)/shard_map/all_to_all | solution.py:332
  61.3 11.7 %collective-permute-start.1 = (f32[12,768]{1,0:T(8,128)S(1)}, f32[12,768]{1,0:T(8,128)S(1)}, u32[]{:S(2)}, u32[]{:S(2)}) collective-permute-start(f32[12,768]{1,0:T(8,128)S(1)} %get-tuple-element.45), channel_id=1, source_target_pairs={{0,1},{1,2},{2,3},{3,0},{4,5},{5,6},{6,7},{7,4},{8,9},{9,10},{10,1... | collective-permute-start | bytes 110600 | tf_op jit(solution)/shard_map/ppermute | solution.py:346
  62.2 10.8 %collective-permute-start.2 = (f32[12,768]{1,0:T(8,128)S(1)}, f32[12,768]{1,0:T(8,128)S(1)}, u32[]{:S(2)}, u32[]{:S(2)}) collective-permute-start(f32[12,768]{1,0:T(8,128)S(1)} %get-tuple-element.47), channel_id=1, source_target_pairs={{0,2},{1,3},{2,0},{3,1},{4,6},{5,7},{6,4},{7,5},{8,10},{9,11},{10,... | collective-permute-start | bytes 110600 | tf_op jit(solution)/shard_map/ppermute | solution.py:346
  64.6 8.4 %collective-permute-start.3 = (f32[12,768]{1,0:T(8,128)S(1)}, f32[12,768]{1,0:T(8,128)S(1)}, u32[]{:S(2)}, u32[]{:S(2)}) collective-permute-start(f32[12,768]{1,0:T(8,128)S(1)} %get-tuple-element.46), channel_id=1, source_target_pairs={{0,3},{1,0},{2,1},{3,2},{4,7},{5,4},{6,5},{7,6},{8,11},{9,8},{10,9... | collective-permute-start | bytes 110600 | tf_op jit(solution)/shard_map/ppermute | solution.py:346
  71.7 9.6 %copy-start = (bf16[64,56,128]{2,1,0:T(8,128)(2,1)}, bf16[64,56,128]{2,1,0:T(8,128)(2,1)S(1)}, u32[]{:S(2)}) copy-start(bf16[64,56,128]{2,1,0:T(8,128)(2,1)S(1)} %all-to-all-done.1.x_ref) | copy-start | bytes 2752516
  73.1 13.6 %collective-permute-start.4 = (f32[12,768]{1,0:T(8,128)S(1)}, f32[12,768]{1,0:T(8,128)S(1)}, u32[]{:S(2)}, u32[]{:S(2)}) collective-permute-start(f32[12,768]{1,0:T(8,128)S(1)} %add_add_fusion.1), channel_id=1, source_target_pairs={{0,128},{64,192},{128,0},{192,64},{1,129},{65,193},{129,1},{193,65... | collective-permute-start | bytes 110600 | tf_op jit(solution)/shard_map/ppermute | solution.py:348
  75.6 11.1 %collective-permute-start.5 = (f32[12,768]{1,0:T(8,128)S(1)}, f32[12,768]{1,0:T(8,128)S(1)}, u32[]{:S(2)}, u32[]{:S(2)}) collective-permute-start(f32[12,768]{1,0:T(8,128)S(1)} %add_add_fusion.1), channel_id=1, source_target_pairs={{0,192},{64,128},{128,64},{192,0},{1,193},{65,129},{129,65},{193,1... | collective-permute-start | bytes 110600 | tf_op jit(solution)/shard_map/ppermute | solution.py:348
  81.3 5.3 %collective-permute-start.6 = (f32[12,768]{1,0:T(8,128)S(1)}, f32[12,768]{1,0:T(8,128)S(1)}, u32[]{:S(2)}, u32[]{:S(2)}) collective-permute-start(f32[12,768]{1,0:T(8,128)S(1)} %add_add_fusion.1), channel_id=1, source_target_pairs={{0,64},{64,0},{128,192},{192,128},{1,65},{65,1},{129,193},{193,129... | collective-permute-start | bytes 110600 | tf_op jit(solution)/shard_map/ppermute | solution.py:348

commit v3 on v2

--- a/solution.py
+++ b/solution.py
@@ -18,6 +18,9 @@
 SEND_ROWS = 40
 BACK_ROWS = 56
 PART_ROWS = 40
+LIMIT = 48
+GROUP = 4
+POWER = SCALE * 1.4426950408889634
 
 
 def iota(shape, dim):
@@ -66,10 +69,11 @@
     return hi, mid, (x - hi - mid).astype(BF).astype(F32)
 
 
-def pack_kernel(sc_ref, q_ref, k_ref, v_ref, g_ref, out_ref, next_ref, rows, grads):
-    for n in range(5):
-        next_ref[n] = sc_ref[n]
-    row_start, tile_count = sc_ref[0], sc_ref[1]
+def pack_kernel(count_ref, q_ref, k_ref, v_ref, g_ref, out_ref, next_ref, rows, grads):
+    place, slide = lax.axis_index("seq"), lax.axis_index("slide")
+    row_start, tile_count = place * ROWS, count_ref[0]
+    for n, value in enumerate((row_start, tile_count, place // 4, slide % 2, slide // 2)):
+        next_ref[n] = value
     own = own_head_mask()
     q_own = q_ref[...] * own
     valid_key = (row_start + iota((ROWS, ROWS), 1)) < tile_count
@@ -118,15 +122,16 @@
     vt[...] = v_ref[...].T
     valid_key = (row_start + iota((ROWS, ROWS), 0)) < tile_count
     column = iota((1, ROWS), 1) & 15
-    for h in range(HEADS):
-        window, rows, here = head_window(h)
-        s = jnp.where(valid_key, nn(k_ref[:, window] * here, qt[window, :]) * SCALE, MASKED)
-        m = jnp.max(s, axis=0, keepdims=True)
-        p = jnp.exp(s - m)
-        l = jnp.sum(p, axis=0, keepdims=True)
-        inv = jnp.where(column == h, 0.0, 1.0 / l)
-        at_ref[rows, :] = (nn(vt[rows, :], p.astype(BF)) * inv).astype(BF)
-        lse_ref[h : h + 1, :] = jnp.where(column == h, 1e30, m + jnp.log(l))
+    for start in range(0, HEADS, GROUP):
+        group = [(h, *head_window(h)) for h in range(start, start + GROUP)]
+        scores = [jnp.where(valid_key, nn(k_ref[:, w] * here, qt[w, :]), MASKED) for _, w, _, here in group]
+        tops = [jnp.max(s, axis=0, keepdims=True) * POWER for s in scores]
+        probs = [jnp.exp2(s * POWER - m) for s, m in zip(scores, tops)]
+        totals = [jnp.sum(p, axis=0, keepdims=True) for p in probs]
+        sums = [nn(vt[rows, :], p.astype(BF)) for (_, _, rows, _), p in zip(group, probs)]
+        for (h, _, rows, _), o, m, l in zip(group, sums, tops, totals):
+            at_ref[rows, :] = (o * jnp.where(column == h, 0.0, 1.0 / l)).astype(BF)
+            lse_ref[h : h + 1, :] = jnp.where(column == h, 1e30, m + jnp.log2(l))
     partial = nn(at_ref[...], g)
     for t in range(6):
         big[t] = partial[:, 128 * t : 128 * t + 128]
@@ -156,17 +161,20 @@
     qt[...] = q_ref[...].T
     kt[...] = k_ref[...].T
     valid_key = (row_start + iota((ROWS, ROWS), 0)) < tile_count
-    for h in range(HEADS):
-        window, rows, here = head_window(h)
-        s = jnp.where(valid_key, nn(k_ref[:, window] * here, qt[window, :]) * SCALE, MASKED)
-        p = jnp.exp(s - lse_ref[h : h + 1, :])
-        ga = gat[rows, :]
-        delta = jnp.sum(ga.astype(F32) * at_ref[rows, :].astype(F32), axis=0, keepdims=True)
-        dp = nn(v_ref[:, window] * here, gat[window, :])
-        ds = (p * (dp - delta)).astype(BF)
-        dqt[rows, :] = nn(kt[rows, :], ds) * SCALE
-        dkt[rows, :] = nt(qt[rows, :], ds) * SCALE
-        dvt[rows, :] = nt(ga, p.astype(BF))
+    for start in range(0, HEADS, GROUP):
+        group = [(h, *head_window(h)) for h in range(start, start + GROUP)]
+        scores = [jnp.where(valid_key, nn(k_ref[:, w] * here, qt[w, :]), MASKED) for _, w, _, here in group]
+        slopes = [nn(v_ref[:, w] * here, gat[w, :]) for _, w, _, here in group]
+        probs = [jnp.exp2(s * POWER - lse_ref[h : h + 1, :]) for (h, _, _, _), s in zip(group, scores)]
+        deltas = [
+            jnp.sum(gat[rows, :].astype(F32) * at_ref[rows, :].astype(F32), axis=0, keepdims=True)
+            for _, _, rows, _ in group
+        ]
+        steps = [(p * (dp - delta)).astype(BF) for p, dp, delta in zip(probs, slopes, deltas)]
+        for (_, _, rows, _), p, ds in zip(group, probs, steps):
+            dqt[rows, :] = nn(kt[rows, :], ds) * SCALE
+            dkt[rows, :] = nt(qt[rows, :], ds) * SCALE
+            dvt[rows, :] = nt(gat[rows, :], p.astype(BF))
     dq_ref[...] = dqt[...].T
     dk_ref[...] = dkt[...].T
     dv_ref[...] = dvt[...].T
@@ -236,10 +244,20 @@
         strided_ref[j] = partial[48 + 12 * j : 60 + 12 * j]
 
 
+def weight_kernel(sc_ref, y_ref, a_ref, b_ref, c_ref, d_ref, out_ref, scr):
+    core = sc_ref[3]
+    scr[...] = jnp.sum(y_ref[:, 16:56, :].astype(F32), axis=0)
+    rest = jnp.concatenate([scr[pl.ds(t, 6, stride=6), :] for t in range(6)], axis=1)
+    zero = jnp.zeros((6, WIDTH), F32)
+    total = (a_ref[...] + b_ref[...]) + (c_ref[...] + d_ref[...])
+    out_ref[0:6, :] = total[0:6] + jnp.where(core == 0, rest, zero)
+    out_ref[6:12, :] = total[6:12] + jnp.where(core == 0, zero, rest)
+
+
 def final_kernel(sc_ref, q_ref, k_ref, w_ref, x_ref, s_ref, dp_ref, ga_ref, layer_ref, dq0_ref, dk0_ref, dv0_ref,
                  out_ref, dq_ref, dk_ref, dv_ref, xs):
     row_start, tile_count = sc_ref[0], sc_ref[1]
-    xs[...] = x_ref[:, 0:16, :].astype(F32).reshape(PEERS * 16, LANES)
+    xs[...] = x_ref[...].astype(F32).reshape(PEERS * 16, LANES)
     lane = iota((16, LANES), 1)
     e_rows = [None] * 16
     dkv_rows = []
@@ -275,49 +293,58 @@
     dv_ref[...] = (dv0_ref[...] + tn(p.astype(BF), ga_own) + nn(dkv, second) * own32).astype(BF)
 
 
-def call(kernel, inputs, outs, scratch=(), scalars=False):
+def call(kernel, inputs, outs, scratch=(), scalars=False, near=(), keep=(), limit=LIMIT, **more):
     vmem = pl.BlockSpec(memory_space=pltpu.VMEM)
     smem = pl.BlockSpec(memory_space=pltpu.SMEM)
+    put = pltpu.with_memory_space_constraint
+    placed = [put(x, pltpu.VMEM if n + 1 in near else pltpu.HBM) for n, x in enumerate(inputs[1:])]
+    shapes = [(pltpu.VMEM if n in keep else pltpu.HBM)(s, t) for n, (s, t) in enumerate(outs)]
+    if scalars:
+        shapes[-1] = jax.ShapeDtypeStruct(*outs[-1])
+    settings = dict(
+        in_specs=[smem] + [vmem] * len(placed),
+        out_specs=[vmem] * (len(outs) - 1) + [smem if scalars else vmem],
+    )
+    settings.update(more)
     return pl.pallas_call(
         kernel,
-        out_shape=[jax.ShapeDtypeStruct(s, t) for s, t in outs],
-        in_specs=[smem] + [vmem] * (len(inputs) - 1),
-        out_specs=[vmem] * (len(outs) - 1) + [smem if scalars else vmem],
+        out_shape=shapes,
         scratch_shapes=[pltpu.VMEM(s, t) for s, t in scratch],
-        compiler_params=pltpu.CompilerParams(vmem_limit_bytes=56 * 1024 * 1024),
-    )(*inputs)
+        compiler_params=pltpu.CompilerParams(vmem_limit_bytes=limit * 1024 * 1024),
+        **settings,
+    )(inputs[0], *placed)
 
 
 def on_device(query_rows, key_rows, value_rows, grad_out, out_weight, tile_counts):
     q, k, v, g = query_rows[0], key_rows[0], value_rows[0], grad_out[0]
     place = lax.axis_index("seq")
-    slide = lax.axis_index("slide")
-    core, far_x = slide % 2, slide // 2
-    sc = jnp.stack([place * ROWS, tile_counts[0], place // 4, core, far_x]).astype(jnp.int32)
     other_core = [(0, 1), (1, 0), (2, 3), (3, 2)]
-    other_x = [(0, 2), (2, 0), (1, 3), (3, 1)]
     flat, tall = (ROWS, WIDTH), (WIDTH, ROWS)
 
-    send, sc2 = call(
-        pack_kernel, (sc, q, k, v, g), [((PEERS, SEND_ROWS, LANES), BF), ((5,), jnp.int32)],
+    send, sc = call(
+        pack_kernel, (tile_counts, q, k, v, g), [((PEERS, SEND_ROWS, LANES), BF), ((5,), jnp.int32)],
         [((PEERS * 16, LANES), F32), ((PEERS * 24, LANES), F32)], scalars=True,
     )
     x = lax.all_to_all(send, "seq", 0, 0)
 
     part = (PEERS, PART_ROWS, LANES)
     at0, lse0, keep, swap = call(
-        forward_kernel, (sc2, q, k, v, g), [(tall, BF), ((HEADS, ROWS), F32), (part, BF), (part, BF)],
+        forward_kernel, (sc, q, k, v, g), [(tall, BF), ((HEADS, ROWS), F32), (part, BF), (part, BF)],
         [(tall, BF), (tall, BF), ((6, WIDTH, LANES), F32), ((PEERS * PART_ROWS, LANES), F32)],
     )
     got = lax.ppermute(swap, "slide", other_core)
-    (joined,) = call(join_kernel, (sc2, keep, got), [((PEERS, BACK_ROWS, LANES), BF)])
+    (joined,) = call(join_kernel, (sc, keep, got), [((PEERS, BACK_ROWS, LANES), BF)])
 
     w_head = lax.dynamic_slice_in_dim(out_weight, place // 4 * HEAD_WIDTH, HEAD_WIDTH, 0)
+    held = pl.BlockSpec(memory_space=pltpu.VMEM)
     whole = lambda *shape: pl.BlockSpec(shape, lambda i: (0,) * len(shape))
-    back, strided = pl.pallas_call(
+    back, strided = call(
         far_kernel,
+        (sc, x, w_head, joined),
+        [((PEERS, BACK_ROWS, LANES), BF), ((4, 12, WIDTH), F32)],
+        [((PEERS * n, LANES), F32) for n in (16, 24, 16)],
+        near=(1,),
         grid=(1,),
-        out_shape=[jax.ShapeDtypeStruct((PEERS, BACK_ROWS, LANES), BF), jax.ShapeDtypeStruct((4, 12, WIDTH), F32)],
         in_specs=[
             pl.BlockSpec(memory_space=pltpu.SMEM),
             whole(PEERS, SEND_ROWS, LANES),
@@ -325,33 +352,37 @@
             pl.BlockSpec(memory_space=pl.ANY),
         ],
         out_specs=[whole(PEERS, 16, LANES), whole(4, 12, WIDTH)],
-        scratch_shapes=[pltpu.VMEM((PEERS * n, LANES), F32) for n in (16, 24, 16)],
         input_output_aliases={3: 0},
-        compiler_params=pltpu.CompilerParams(vmem_limit_bytes=56 * 1024 * 1024),
-    )(sc, x, w_head, joined)
+    )
     y = lax.all_to_all(back, "seq", 0, 0)
 
     dq0, dk0, dv0, layer0, ga, s0, dp0, strided = call(
         backward_kernel, (sc, q, k, v, g, out_weight, at0, lse0, strided),
         [(flat, F32)] * 4 + [(flat, BF)] + [((ROWS, ROWS), F32)] * 2 + [((4, 12, WIDTH), F32)],
         [(tall, BF)] * 3 + [(tall, F32)] * 3,
-    )
-    rest = jnp.sum(y[:, 16:52, :].astype(F32), axis=0).reshape(6, WIDTH)
-    weight = lax.dynamic_update_slice_in_dim(jnp.zeros((12, WIDTH), F32), rest, 6 * core, 0)
+        keep=(0, 1, 2),
+    )
     quarter = place % 4
+    pieces = []
     for step in range(4):
         mine = lax.dynamic_index_in_dim(strided, (quarter + step) % 4, 0, keepdims=False)
-        if step:
-            ring = [(d, d // 4 * 4 + (d + step) % 4) for d in range(PEERS)]
-            mine = lax.ppermute(mine, "seq", ring)
-        weight = weight + mine
-    weight = weight + sum(lax.ppermute(weight, "slide", [(n, n ^ bits) for n in range(4)]) for bits in (2, 3, 1))
+        ring = [(d, d // 4 * 4 + (d + step) % 4) for d in range(PEERS)]
+        pieces.append(lax.ppermute(mine, "seq", ring) if step else mine)
+    (weight,) = call(
+        weight_kernel, (sc, y, *pieces), [((12, WIDTH), F32)], [((PART_ROWS, LANES), F32)], near=(1,)
+    )
+    others = [lax.ppermute(weight, "slide", [(n, n ^ bits) for n in range(4)]) for bits in (2, 3, 1)]
 
     outs = call(
-        final_kernel, (sc, q, k, out_weight, y, s0, dp0, ga, layer0, dq0, dk0, dv0), [(flat, BF)] * 4,
+        final_kernel,
+        (sc, q, k, out_weight, y, s0, dp0, ga, layer0, dq0, dk0, dv0),
+        [(flat, BF)] * 4,
         [((PEERS * 16, LANES), F32)],
-    )
-    return tuple(o[None] for o in outs) + (weight,)
+        near=(4, 9, 10, 11),
+        grid=(1,),
+        in_specs=[pl.BlockSpec(memory_space=pltpu.SMEM)] + [held] * 3 + [whole(PEERS, 16, LANES)] + [held] * 7,
+    )
+    return tuple(o[None] for o in outs) + (weight + others[0] + others[1] + others[2],)
 
 
 def solution(mesh):

time: 87.9 us -> 85.5 us (0.973)
  waiting for transfers between devices: 10.3 us -> 14.8 us
  Pallas kernels: 33.8 us -> 29.4 us
  local copies, waits for them, and re-layouts: 5.03 us -> 3.88 us
  other arithmetic: 1.67 us -> 0.63 us
    pallas_call x6 -> x7, Pallas kernels: 33.8 us -> 29.4 us  [call(): pl.pallas_call(kernel, out_shape=shapes, scratch_shapes=[pltpu.VMEM(s, t)...]
    ppermute x3, waiting for transfers between devices: 0.01 us -> 3.12 us  [on_device(): pieces.append(lax.ppermute(mine, 'seq', ring) if step else mine)]
    all_to_all x1, waiting for transfers between devices: 3.91 us -> 6.21 us  [on_device(): x = lax.all_to_all(send, 'seq', 0, 0)]
    all_to_all x1, waiting for transfers between devices: 5.93 us -> 5 us  [on_device(): y = lax.all_to_all(back, 'seq', 0, 0)]
    dynamic_update_slice x1 -> x0, other arithmetic: 0.88 us -> none  [on_device(): lax.dynamic_update_slice_in_dim(jnp.zeros((12, WIDTH), F32), rest, 6 * co...]
  transfers between devices with their start and end apart: 9 -> 9, of which waited for: 3 -> 6; matrix products, arithmetic and copies ran while one was open for 4% -> 4% of each run, Pallas kernels for 29% -> 23%
where the time goes in v3:
time: 85.5 us; the launch traced here: 84.9 us
  starting transfers between devices  34.8 us (41%)
  Pallas kernels  29.4 us (34%)
  waiting for transfers between devices  14.8 us (17%)
  local copies, waits for them, and re-layouts  3.88 us (5%)
  between operations  1.42 us (2%)
    pallas_call x7, Pallas kernels, call(): pl.pallas_call(kernel, out_shape=shapes, scratch_shapes=[pltpu.VMEM(s, t)...  29.4 us
    all_to_all x1, starting transfers between devices, on_device(): x = lax.all_to_all(send, 'seq', 0, 0)  13.6 us
    ppermute x3, starting transfers between devices, on_device(): lax.ppermute(weight, 'slide', [(n, n ^ bits) for n in range(4)])  8.2 us
    all_to_all x1, starting transfers between devices, on_device(): y = lax.all_to_all(back, 'seq', 0, 0)  7.68 us
    all_to_all x1, waiting for transfers between devices, on_device(): x = lax.all_to_all(send, 'seq', 0, 0)  6.21 us
    all_to_all x1, waiting for transfers between devices, on_device(): y = lax.all_to_all(back, 'seq', 0, 0)  5 us
    ppermute x3, starting transfers between devices, on_device(): pieces.append(lax.ppermute(mine, 'seq', ring) if step else mine)  4.41 us
    ppermute x3, waiting for transfers between devices, on_device(): pieces.append(lax.ppermute(mine, 'seq', ring) if step else mine)  3.12 us
  transfers between devices with their start and end apart: 9, of which 6 were waited for; matrix products, arithmetic and copies ran while one was open for 4% of the time, Pallas kernels for 23%

profile of v3, /device:TPU:1, one launch (start us, length us, event | category | flops | bytes accessed | tf_op | source)
XLA Modules:
  0.0 84.9 jit_solution(4023972002891802559)
XLA Ops:
  1.3 4.2 %shard_map.101 = (bf16[64,40,128]{2,1,0:T(8,128)(2,1)}, s32[5]{0:T(128)S(1)}) custom-call(s32[1]{0:T(128)S(6)} %copy.13.count_ref, bf16[256,768]{1,0:T(8,128)(2,1)} %bitcast.16, bf16[256,768]{1,0:T(8,128)(2,1)} %bitcast.20, bf16[256,768]{1,0:T(8,128)(2,1)} %bitcast.24, bf16[256,768]{1,0:T(8,128)(2,1)} %bitcast.27), custom_call_target="tpu_custom_call" | custom-call | tf_op jit(solution)/shard_map/pallas_call | solution.py:309
  5.5 13.6 %all-to-all-start = ((bf16[64,40,128]{2,1,0:T(8,128)(2,1)}), bf16[64,40,128]{2,1,0:T(8,128)(2,1)S(1)}, u32[]{:S(2)}, u32[]{:S(2)}) async-start(bf16[64,40,128]{2,1,0:T(8,128)(2,1)} %get-tuple-element.26), calls=%async_computation | async-start | bytes 1310720 | tf_op jit(solution)/shard_map/all_to_all | solution.py:328
  19.1 5.5 %shard_map.102 = (bf16[768,256]{1,0:T(8,128)(2,1)}, f32[16,256]{1,0:T(8,128)}, bf16[64,40,128]{2,1,0:T(8,128)(2,1)}, bf16[64,40,128]{2,1,0:T(8,128)(2,1)}) custom-call(s32[5]{0:T(128)S(1)} %get-tuple-element.25.sc_ref, bf16[256,768]{1,0:T(8,128)(2,1)} %bitcast.17, bf16[256,768]{1,0:T(8,128)(2,1)} %bitcast.21, bf16[256,768]{1,0:T(8,128)(2,1)} %bitcast.25, ...), custom_call_target="tpu_custom_call" | custom-call | tf_op jit(solution)/shard_map/pallas_call | solution.py:309
  24.7 1.0 %collective-permute-start = (bf16[64,40,128]{2,1,0:T(8,128)(2,1)}, bf16[64,40,128]{2,1,0:T(8,128)(2,1)S(1)}, u32[]{:S(2)}, u32[]{:S(2)}) collective-permute-start(bf16[64,40,128]{2,1,0:T(8,128)(2,1)} %get-tuple-element.28), channel_id=1, source_target_pairs={{0,64},{64,0},{128,192},{192,128},{1,65},{65,1},{129,193},{193,129... | collective-permute-start | bytes 1966088 | tf_op jit(solution)/shard_map/ppermute | solution.py:335
  25.6 1.5 %constant_dynamic-slice_fusion.w_ref = bf16[48,768]{1,0:T(8,128)(2,1)} fusion(bf16[768,768]{1,0:T(8,128)(2,1)} %w_ref.3, s32[]{:T(128)S(6)} %select_n.44), kind=kLoop, calls=%fused_computation.5 | loop fusion | bytes 147460 | tf_op jit(solution)/shard_map/dynamic_slice | solution.py:338
  27.1 0.4 collective-permute-done.got_ref
  27.5 0.8 copy-done
  28.4 2.4 %shard_map.103.joined_ref = bf16[64,56,128]{2,1,0:T(8,128)(2,1)} custom-call(s32[5]{0:T(128)S(1)} %get-tuple-element.25.sc_ref, bf16[64,40,128]{2,1,0:T(8,128)(2,1)} %get-tuple-element.27.keep_ref, bf16[64,40,128]{2,1,0:T(8,128)(2,1)} %copy-done), custom_call_target="tpu_custom_call" | custom-call | tf_op jit(solution)/shard_map/pallas_call | solution.py:309
  30.8 6.2 %all-to-all-done.x_ref = bf16[64,40,128]{2,1,0:T(8,128)(2,1)S(1)} async-done(((bf16[64,40,128]{2,1,0:T(8,128)(2,1)}), bf16[64,40,128]{2,1,0:T(8,128)(2,1)S(1)}, u32[]{:S(2)}, u32[]{:S(2)}) %all-to-all-start) | async-done | bytes 655392 | tf_op jit(solution)/shard_map/all_to_all | solution.py:328
  37.0 4.0 %shard_map.104 = (bf16[64,56,128]{2,1,0:T(8,128)(2,1)}, f32[4,12,768]{2,1,0:T(8,128)}) custom-call(s32[5]{0:T(128)S(1)} %get-tuple-element.25.sc_ref, bf16[64,40,128]{2,1,0:T(8,128)(2,1)S(1)} %all-to-all-done.x_ref, bf16[48,768]{1,0:T(8,128)(2,1)} %constant_dynamic-slice_fusion.w_ref, ...), custom_call_target="tpu_custom_call", output_to_operand_aliasing={{0}: (3, {})} | custom-call | tf_op jit(solution)/shard_map/pallas_call | solution.py:309
  41.0 7.7 %all-to-all-start.1 = ((bf16[64,56,128]{2,1,0:T(8,128)(2,1)}), bf16[64,56,128]{2,1,0:T(8,128)(2,1)S(1)}, u32[]{:S(2)}, u32[]{:S(2)}) async-start(bf16[64,56,128]{2,1,0:T(8,128)(2,1)} %get-tuple-element.29), calls=%async_computation.1 | async-start | bytes 1835008 | tf_op jit(solution)/shard_map/all_to_all | solution.py:357
  48.8 7.1 %shard_map.105 = (f32[256,768]{1,0:T(8,128)S(1)}, f32[256,768]{1,0:T(8,128)S(1)}, f32[256,768]{1,0:T(8,128)S(1)}, f32[256,768]{1,0:T(8,128)}, bf16[256,768]{1,0:...) custom-call(s32[5]{0:T(128)S(1)} %get-tuple-element.25.sc_ref, ...), custom_call_target="tpu_custom_call" | custom-call | tf_op jit(solution)/shard_map/pallas_call | solution.py:309
  55.9 1.5 %dynamic-slice_bitcast_fusion = (f32[12,768]{1,0:T(8,128)S(1)}, f32[12,768]{1,0:T(8,128)S(1)}, f32[12,768]{1,0:T(8,128)S(1)}, f32[12,768]{1,0:T(8,128)}) fusion(f32[4,12,768]{2,1,0:T(8,128)} %get-tuple-element.44, s32[]{:T(128)S(6)} %select_n.53, s32[]{:T(128)S(6)} %select_n.51, s32[]{:T(128)S(6)} %select_n.49, s32[]{:T(128)S(6)} %select_n.47), kind=kLoop, calls=%fused_computation.1 | loop fusion | bytes 294928 | tf_op jit(solution)/shard_map/jit(dynamic_index_in_dim)/squeeze | solution.py:368
  57.4 0.8 collective-permute-start.1
  58.3 2.4 %collective-permute-start.2 = (f32[12,768]{1,0:T(8,128)S(1)}, f32[12,768]{1,0:T(8,128)S(1)}, u32[]{:S(2)}, u32[]{:S(2)}) collective-permute-start(f32[12,768]{1,0:T(8,128)S(1)} %get-tuple-element.46), channel_id=1, source_target_pairs={{0,2},{1,3},{2,0},{3,1},{4,6},{5,7},{6,4},{7,5},{8,10},{9,11},{10,... | collective-permute-start | bytes 110600 | tf_op jit(solution)/shard_map/ppermute | solution.py:370
  60.7 1.2 %collective-permute-start.3 = (f32[12,768]{1,0:T(8,128)S(1)}, f32[12,768]{1,0:T(8,128)S(1)}, u32[]{:S(2)}, u32[]{:S(2)}) collective-permute-start(f32[12,768]{1,0:T(8,128)S(1)} %get-tuple-element.45), channel_id=1, source_target_pairs={{0,3},{1,0},{2,1},{3,2},{4,7},{5,4},{6,5},{7,6},{8,11},{9,8},{10,9... | collective-permute-start | bytes 110600 | tf_op jit(solution)/shard_map/ppermute | solution.py:370
  62.2 1.1 %collective-permute-done.2.c_ref = f32[12,768]{1,0:T(8,128)S(1)} collective-permute-done((f32[12,768]{1,0:T(8,128)S(1)}, f32[12,768]{1,0:T(8,128)S(1)}, u32[]{:S(2)}, u32[]{:S(2)}) %collective-permute-start.2) | collective-permute-done | bytes 36896 | tf_op jit(solution)/shard_map/ppermute | solution.py:370
  63.3 1.7 %collective-permute-done.3.d_ref = f32[12,768]{1,0:T(8,128)S(1)} collective-permute-done((f32[12,768]{1,0:T(8,128)S(1)}, f32[12,768]{1,0:T(8,128)S(1)}, u32[]{:S(2)}, u32[]{:S(2)}) %collective-permute-start.3) | collective-permute-done | bytes 36896 | tf_op jit(solution)/shard_map/ppermute | solution.py:370
  65.0 5.0 %all-to-all-done.1.x_ref.y_ref = bf16[64,56,128]{2,1,0:T(8,128)(2,1)S(1)} async-done(((bf16[64,56,128]{2,1,0:T(8,128)(2,1)}), bf16[64,56,128]{2,1,0:T(8,128)(2,1)S(1)}, u32[]{:S(2)}, u32[]{:S(2)}) %all-to-all-start.1) | async-done | bytes 917536 | tf_op jit(solution)/shard_map/all_to_all | solution.py:357
  70.0 1.6 %shard_map.107 = f32[12,768]{1,0:T(8,128)} custom-call(s32[5]{0:T(128)S(1)} %get-tuple-element.25.sc_ref, bf16[64,56,128]{2,1,0:T(8,128)(2,1)S(1)} %all-to-all-done.1.x_ref.y_ref, f32[12,768]{1,0:T(8,128)} %get-tuple-element.48.a_ref, f32[12,768]{1,0:T(8,128)} %copy-done.2, f32[12,768]{1,0:T(8,128)} %copy-done.3, f32[12,768]{1,0:T(8,128)} %copy-done.4), custom_call_target="tpu_custom_call" | custom-call | tf_op jit(solution)/shard_map/pallas_call | solution.py:309
  71.6 2.4 %collective-permute-start.4 = (f32[12,768]{1,0:T(8,128)}, f32[12,768]{1,0:T(8,128)S(1)}, u32[]{:S(2)}, u32[]{:S(2)}) collective-permute-start(f32[12,768]{1,0:T(8,128)} %shard_map.107), channel_id=1, source_target_pairs={{0,128},{64,192},{128,0},{192,64},{1,129},{65,193},{129,1},{193,65... | collective-permute-start | bytes 110600 | tf_op jit(solution)/shard_map/ppermute | solution.py:374
  74.0 5.8 %collective-permute-start.5 = (f32[12,768]{1,0:T(8,128)}, f32[12,768]{1,0:T(8,128)S(1)}, u32[]{:S(2)}, u32[]{:S(2)}) collective-permute-start(f32[12,768]{1,0:T(8,128)} %shard_map.107), channel_id=1, source_target_pairs={{0,192},{64,128},{128,64},{192,0},{1,193},{65,129},{129,65},{193,1... | collective-permute-start | bytes 110600 | tf_op jit(solution)/shard_map/ppermute | solution.py:374
  79.8 4.5 %shard_map.106 = (bf16[256,768]{1,0:T(8,128)(2,1)}, bf16[256,768]{1,0:T(8,128)(2,1)}, bf16[256,768]{1,0:T(8,128)(2,1)}, bf16[256,768]{1,0:T(8,128)(2,1)}) custom-call(s32[5]{0:T(128)S(1)} %get-tuple-element.25.sc_ref, bf16[256,768]{1,0:T(8,128)(2,1)} %bitcast.19, bf16[256,768]{1,0:T(8,128)(2,1)} %bitcast.23, bf16[768,768]{1,0:T(8,128)(2,1)} %w_ref.3, ...), custom_call_target="tpu_custom_call" | custom-call | tf_op jit(solution)/shard_map/pallas_call | solution.py:309
  84.3 0.6 add_add_fusion
  (14 shorter events, 0.4 us)
Async XLA Ops:
  5.5 31.5 %all-to-all-start = ((bf16[64,40,128]{2,1,0:T(8,128)(2,1)}), bf16[64,40,128]{2,1,0:T(8,128)(2,1)S(1)}, u32[]{:S(2)}, u32[]{:S(2)}) async-start(bf16[64,40,128]{2,1,0:T(8,128)(2,1)} %get-tuple-element.26), calls=%async_computation | async-start | bytes 1310720 | tf_op jit(solution)/shard_map/all_to_all | solution.py:328
  24.7 2.9 %collective-permute-start = (bf16[64,40,128]{2,1,0:T(8,128)(2,1)}, bf16[64,40,128]{2,1,0:T(8,128)(2,1)S(1)}, u32[]{:S(2)}, u32[]{:S(2)}) collective-permute-start(bf16[64,40,128]{2,1,0:T(8,128)(2,1)} %get-tuple-element.28), channel_id=1, source_target_pairs={{0,64},{64,0},{128,192},{192,128},{1,65},{65,1},{129,193},{193,129... | collective-permute-start | bytes 1966088 | tf_op jit(solution)/shard_map/ppermute | solution.py:335
  27.5 0.8 copy-start
  41.0 28.9 %all-to-all-start.1 = ((bf16[64,56,128]{2,1,0:T(8,128)(2,1)}), bf16[64,56,128]{2,1,0:T(8,128)(2,1)S(1)}, u32[]{:S(2)}, u32[]{:S(2)}) async-start(bf16[64,56,128]{2,1,0:T(8,128)(2,1)} %get-tuple-element.29), calls=%async_computation.1 | async-start | bytes 1835008 | tf_op jit(solution)/shard_map/all_to_all | solution.py:357
  57.4 4.8 %collective-permute-start.1 = (f32[12,768]{1,0:T(8,128)S(1)}, f32[12,768]{1,0:T(8,128)S(1)}, u32[]{:S(2)}, u32[]{:S(2)}) collective-permute-start(f32[12,768]{1,0:T(8,128)S(1)} %get-tuple-element.47), channel_id=1, source_target_pairs={{0,1},{1,2},{2,3},{3,0},{4,5},{5,6},{6,7},{7,4},{8,9},{9,10},{10,1... | collective-permute-start | bytes 110600 | tf_op jit(solution)/shard_map/ppermute | solution.py:370
  58.3 5.0 %collective-permute-start.2 = (f32[12,768]{1,0:T(8,128)S(1)}, f32[12,768]{1,0:T(8,128)S(1)}, u32[]{:S(2)}, u32[]{:S(2)}) collective-permute-start(f32[12,768]{1,0:T(8,128)S(1)} %get-tuple-element.46), channel_id=1, source_target_pairs={{0,2},{1,3},{2,0},{3,1},{4,6},{5,7},{6,4},{7,5},{8,10},{9,11},{10,... | collective-permute-start | bytes 110600 | tf_op jit(solution)/shard_map/ppermute | solution.py:370
  60.7 4.3 %collective-permute-start.3 = (f32[12,768]{1,0:T(8,128)S(1)}, f32[12,768]{1,0:T(8,128)S(1)}, u32[]{:S(2)}, u32[]{:S(2)}) collective-permute-start(f32[12,768]{1,0:T(8,128)S(1)} %get-tuple-element.45), channel_id=1, source_target_pairs={{0,3},{1,0},{2,1},{3,2},{4,7},{5,4},{6,5},{7,6},{8,11},{9,8},{10,9... | collective-permute-start | bytes 110600 | tf_op jit(solution)/shard_map/ppermute | solution.py:370
  62.2 7.8 %copy-start.2 = (f32[12,768]{1,0:T(8,128)}, f32[12,768]{1,0:T(8,128)S(1)}, u32[]{:S(2)}) copy-start(f32[12,768]{1,0:T(8,128)S(1)} %collective-permute-done.1.b_ref) | copy-start | bytes 110596
  63.3 6.7 %copy-start.3 = (f32[12,768]{1,0:T(8,128)}, f32[12,768]{1,0:T(8,128)S(1)}, u32[]{:S(2)}) copy-start(f32[12,768]{1,0:T(8,128)S(1)} %collective-permute-done.2.c_ref) | copy-start | bytes 110596
  65.0 5.0 %copy-start.4 = (f32[12,768]{1,0:T(8,128)}, f32[12,768]{1,0:T(8,128)S(1)}, u32[]{:S(2)}) copy-start(f32[12,768]{1,0:T(8,128)S(1)} %collective-permute-done.3.d_ref) | copy-start | bytes 110596
  71.6 12.7 %collective-permute-start.4 = (f32[12,768]{1,0:T(8,128)}, f32[12,768]{1,0:T(8,128)S(1)}, u32[]{:S(2)}, u32[]{:S(2)}) collective-permute-start(f32[12,768]{1,0:T(8,128)} %shard_map.107), channel_id=1, source_target_pairs={{0,128},{64,192},{128,0},{192,64},{1,129},{65,193},{129,1},{193,65... | collective-permute-start | bytes 110600 | tf_op jit(solution)/shard_map/ppermute | solution.py:374
  74.0 10.2 %collective-permute-start.5 = (f32[12,768]{1,0:T(8,128)}, f32[12,768]{1,0:T(8,128)S(1)}, u32[]{:S(2)}, u32[]{:S(2)}) collective-permute-start(f32[12,768]{1,0:T(8,128)} %shard_map.107), channel_id=1, source_target_pairs={{0,192},{64,128},{128,64},{192,0},{1,193},{65,129},{129,65},{193,1... | collective-permute-start | bytes 110600 | tf_op jit(solution)/shard_map/ppermute | solution.py:374
  79.8 4.5 %collective-permute-start.6 = (f32[12,768]{1,0:T(8,128)}, f32[12,768]{1,0:T(8,128)S(1)}, u32[]{:S(2)}, u32[]{:S(2)}) collective-permute-start(f32[12,768]{1,0:T(8,128)} %shard_map.107), channel_id=1, source_target_pairs={{0,64},{64,0},{128,192},{192,128},{1,65},{65,1},{129,193},{193,129... | collective-permute-start | bytes 110600 | tf_op jit(solution)/shard_map/ppermute | solution.py:374
  79.8 4.5 %copy-start.1 = (f32[12,768]{1,0:T(8,128)S(1)}, f32[12,768]{1,0:T(8,128)}, u32[]{:S(2)}) copy-start(f32[12,768]{1,0:T(8,128)} %shard_map.107) | copy-start | bytes 110596

commit v4 on v3

--- a/solution.py
+++ b/solution.py
@@ -70,10 +70,8 @@
 
 
 def pack_kernel(count_ref, q_ref, k_ref, v_ref, g_ref, out_ref, next_ref, rows, grads):
-    place, slide = lax.axis_index("seq"), lax.axis_index("slide")
-    row_start, tile_count = place * ROWS, count_ref[0]
-    for n, value in enumerate((row_start, tile_count, place // 4, slide % 2, slide // 2)):
-        next_ref[n] = value
+    row_start, tile_count = lax.axis_index("seq") * ROWS, count_ref[0]
+    next_ref[...] = jnp.full(next_ref.shape, tile_count, jnp.int32)
     own = own_head_mask()
     q_own = q_ref[...] * own
     valid_key = (row_start + iota((ROWS, ROWS), 1)) < tile_count
@@ -114,8 +112,8 @@
     return slice(a, b), slice(f, f + HEAD_WIDTH), onehot((lane >= f) & (lane < f + HEAD_WIDTH))
 
 
-def forward_kernel(sc_ref, q_ref, k_ref, v_ref, g_ref, at_ref, lse_ref, keep_ref, send_ref, qt, vt, big, part):
-    row_start, tile_count, core = sc_ref[0], sc_ref[1], sc_ref[3]
+def forward_kernel(count_ref, q_ref, k_ref, v_ref, g_ref, at_ref, lse_ref, keep_ref, send_ref, qt, vt, big, part):
+    row_start, tile_count, core = lax.axis_index("seq") * ROWS, count_ref[0:1, 0:1], lax.axis_index("slide") % 2
     valid_row = (row_start + iota((ROWS, WIDTH), 0)) < tile_count
     g = jnp.where(valid_row, g_ref[...].astype(F32), 0.0).astype(BF)
     qt[...] = q_ref[...].T
@@ -145,14 +143,14 @@
         ref[...] = part[...].astype(BF).reshape(PEERS, PART_ROWS, LANES)
 
 
-def join_kernel(sc_ref, keep_ref, got_ref, out_ref):
+def join_kernel(keep_ref, got_ref, out_ref):
     out_ref[:, 0:16, :] = jnp.zeros((PEERS, 16, LANES), BF)
     out_ref[:, 16:56, :] = (keep_ref[...].astype(F32) + got_ref[...].astype(F32)).astype(BF)
 
 
-def backward_kernel(sc_ref, q_ref, k_ref, v_ref, g_ref, w_ref, at_ref, lse_ref, strided_ref,
+def backward_kernel(count_ref, q_ref, k_ref, v_ref, g_ref, w_ref, at_ref, lse_ref, strided_ref,
                     dq_ref, dk_ref, dv_ref, layer_ref, ga_ref, s_ref, dp_ref, pass_ref, qt, kt, gat, dqt, dkt, dvt):
-    row_start, tile_count = sc_ref[0], sc_ref[1]
+    row_start, tile_count = lax.axis_index("seq") * ROWS, count_ref[0:1, 0:1]
     pass_ref[...] = strided_ref[...]
     valid_row = (row_start + iota((ROWS, WIDTH), 0)) < tile_count
     g = jnp.where(valid_row, g_ref[...].astype(F32), 0.0).astype(BF)
@@ -187,8 +185,8 @@
     dp_ref[...] = nt(ga_own, v_ref[...])
 
 
-def far_kernel(sc_ref, x_ref, w_ref, joined_ref, back_ref, strided_ref, xs, gs, ps):
-    tile_count, head = sc_ref[1], sc_ref[2]
+def far_kernel(count_ref, x_ref, w_ref, joined_ref, back_ref, strided_ref, xs, gs, ps):
+    tile_count, head = count_ref[0:1, 0:1], lax.axis_index("seq") // 4
     x = x_ref[:, 0:16, :].reshape(PEERS * 16, LANES)
     xs[...] = x.astype(F32)
     gs[...] = x_ref[:, 16:40, :].astype(F32).reshape(PEERS * 24, LANES)
@@ -244,8 +242,8 @@
         strided_ref[j] = partial[48 + 12 * j : 60 + 12 * j]
 
 
-def weight_kernel(sc_ref, y_ref, a_ref, b_ref, c_ref, d_ref, out_ref, scr):
-    core = sc_ref[3]
+def weight_kernel(y_ref, a_ref, b_ref, c_ref, d_ref, out_ref, scr):
+    core = lax.axis_index("slide") % 2
     scr[...] = jnp.sum(y_ref[:, 16:56, :].astype(F32), axis=0)
     rest = jnp.concatenate([scr[pl.ds(t, 6, stride=6), :] for t in range(6)], axis=1)
     zero = jnp.zeros((6, WIDTH), F32)
@@ -254,9 +252,9 @@
     out_ref[6:12, :] = total[6:12] + jnp.where(core == 0, zero, rest)
 
 
-def final_kernel(sc_ref, q_ref, k_ref, w_ref, x_ref, s_ref, dp_ref, ga_ref, layer_ref, dq0_ref, dk0_ref, dv0_ref,
+def final_kernel(count_ref, q_ref, k_ref, w_ref, x_ref, s_ref, dp_ref, ga_ref, layer_ref, dq0_ref, dk0_ref, dv0_ref,
                  out_ref, dq_ref, dk_ref, dv_ref, xs):
-    row_start, tile_count = sc_ref[0], sc_ref[1]
+    row_start, tile_count = lax.axis_index("seq") * ROWS, count_ref[0:1, 0:1]
     xs[...] = x_ref[...].astype(F32).reshape(PEERS * 16, LANES)
     lane = iota((16, LANES), 1)
     e_rows = [None] * 16
@@ -295,24 +293,20 @@
 
 def call(kernel, inputs, outs, scratch=(), scalars=False, near=(), keep=(), limit=LIMIT, **more):
     vmem = pl.BlockSpec(memory_space=pltpu.VMEM)
-    smem = pl.BlockSpec(memory_space=pltpu.SMEM)
     put = pltpu.with_memory_space_constraint
-    placed = [put(x, pltpu.VMEM if n + 1 in near else pltpu.HBM) for n, x in enumerate(inputs[1:])]
-    shapes = [(pltpu.VMEM if n in keep else pltpu.HBM)(s, t) for n, (s, t) in enumerate(outs)]
+    placed = [put(x, pltpu.VMEM if n in near else pltpu.HBM) for n, x in enumerate(inputs)]
+    specs = [vmem] * len(inputs)
     if scalars:
-        shapes[-1] = jax.ShapeDtypeStruct(*outs[-1])
-    settings = dict(
-        in_specs=[smem] + [vmem] * len(placed),
-        out_specs=[vmem] * (len(outs) - 1) + [smem if scalars else vmem],
-    )
+        placed[0], specs[0] = inputs[0], pl.BlockSpec(memory_space=pltpu.SMEM)
+    settings = dict(in_specs=specs, out_specs=[vmem] * len(outs))
     settings.update(more)
     return pl.pallas_call(
         kernel,
-        out_shape=shapes,
+        out_shape=[(pltpu.VMEM if n in keep else pltpu.HBM)(s, t) for n, (s, t) in enumerate(outs)],
         scratch_shapes=[pltpu.VMEM(s, t) for s, t in scratch],
         compiler_params=pltpu.CompilerParams(vmem_limit_bytes=limit * 1024 * 1024),
         **settings,
-    )(inputs[0], *placed)
+    )(*placed)
 
 
 def on_device(query_rows, key_rows, value_rows, grad_out, out_weight, tile_counts):
@@ -321,32 +315,34 @@
     other_core = [(0, 1), (1, 0), (2, 3), (3, 2)]
     flat, tall = (ROWS, WIDTH), (WIDTH, ROWS)
 
-    send, sc = call(
-        pack_kernel, (tile_counts, q, k, v, g), [((PEERS, SEND_ROWS, LANES), BF), ((5,), jnp.int32)],
-        [((PEERS * 16, LANES), F32), ((PEERS * 24, LANES), F32)], scalars=True,
+    send, count = call(
+        pack_kernel, (tile_counts, q, k, v, g), [((PEERS, SEND_ROWS, LANES), BF), ((8, LANES), jnp.int32)],
+        [((PEERS * 16, LANES), F32), ((PEERS * 24, LANES), F32)], keep=(0, 1), scalars=True,
     )
     x = lax.all_to_all(send, "seq", 0, 0)
 
     part = (PEERS, PART_ROWS, LANES)
     at0, lse0, keep, swap = call(
-        forward_kernel, (sc, q, k, v, g), [(tall, BF), ((HEADS, ROWS), F32), (part, BF), (part, BF)],
+        forward_kernel, (count, q, k, v, g), [(tall, BF), ((HEADS, ROWS), F32), (part, BF), (part, BF)],
         [(tall, BF), (tall, BF), ((6, WIDTH, LANES), F32), ((PEERS * PART_ROWS, LANES), F32)],
+        near=(0,),
     )
     got = lax.ppermute(swap, "slide", other_core)
-    (joined,) = call(join_kernel, (sc, keep, got), [((PEERS, BACK_ROWS, LANES), BF)])
+    (joined,) = call(join_kernel, (keep, got), [((PEERS, BACK_ROWS, LANES), BF)], keep=(0,))
 
     w_head = lax.dynamic_slice_in_dim(out_weight, place // 4 * HEAD_WIDTH, HEAD_WIDTH, 0)
     held = pl.BlockSpec(memory_space=pltpu.VMEM)
     whole = lambda *shape: pl.BlockSpec(shape, lambda i: (0,) * len(shape))
     back, strided = call(
         far_kernel,
-        (sc, x, w_head, joined),
+        (count, x, w_head, joined),
         [((PEERS, BACK_ROWS, LANES), BF), ((4, 12, WIDTH), F32)],
         [((PEERS * n, LANES), F32) for n in (16, 24, 16)],
-        near=(1,),
+        near=(0, 1, 2, 3),
+        keep=(0,),
         grid=(1,),
         in_specs=[
-            pl.BlockSpec(memory_space=pltpu.SMEM),
+            whole(8, LANES),
             whole(PEERS, SEND_ROWS, LANES),
             whole(HEAD_WIDTH, WIDTH),
             pl.BlockSpec(memory_space=pl.ANY),
@@ -357,9 +353,10 @@
     y = lax.all_to_all(back, "seq", 0, 0)
 
     dq0, dk0, dv0, layer0, ga, s0, dp0, strided = call(
-        backward_kernel, (sc, q, k, v, g, out_weight, at0, lse0, strided),
+        backward_kernel, (count, q, k, v, g, out_weight, at0, lse0, strided),
         [(flat, F32)] * 4 + [(flat, BF)] + [((ROWS, ROWS), F32)] * 2 + [((4, 12, WIDTH), F32)],
         [(tall, BF)] * 3 + [(tall, F32)] * 3,
+        near=(0,),
         keep=(0, 1, 2),
     )
     quarter = place % 4
@@ -369,18 +366,18 @@
         ring = [(d, d // 4 * 4 + (d + step) % 4) for d in range(PEERS)]
         pieces.append(lax.ppermute(mine, "seq", ring) if step else mine)
     (weight,) = call(
-        weight_kernel, (sc, y, *pieces), [((12, WIDTH), F32)], [((PART_ROWS, LANES), F32)], near=(1,)
+        weight_kernel, (y, *pieces), [((12, WIDTH), F32)], [((PART_ROWS, LANES), F32)], near=(0, 1, 2, 3, 4), keep=(0,)
     )
     others = [lax.ppermute(weight, "slide", [(n, n ^ bits) for n in range(4)]) for bits in (2, 3, 1)]
 
     outs = call(
         final_kernel,
-        (sc, q, k, out_weight, y, s0, dp0, ga, layer0, dq0, dk0, dv0),
+        (count, q, k, out_weight, y, s0, dp0, ga, layer0, dq0, dk0, dv0),
         [(flat, BF)] * 4,
         [((PEERS * 16, LANES), F32)],
-        near=(4, 9, 10, 11),
+        near=(0, 4, 9, 10, 11),
         grid=(1,),
-        in_specs=[pl.BlockSpec(memory_space=pltpu.SMEM)] + [held] * 3 + [whole(PEERS, 16, LANES)] + [held] * 7,
+        in_specs=[held] * 4 + [whole(PEERS, 16, LANES)] + [held] * 7,
     )
     return tuple(o[None] for o in outs) + (weight + others[0] + others[1] + others[2],)
 

time: 85.5 us -> 83 us (0.971)
  Pallas kernels: 29.4 us -> 26.8 us
  waiting for transfers between devices: 14.8 us -> 16.1 us
  local copies, waits for them, and re-layouts: 3.88 us -> 2.62 us
    pallas_call x7, Pallas kernels: 29.4 us -> 26.8 us  [call(): pl.pallas_call(kernel, out_shape=[(pltpu.VMEM if n in keep else pltpu.HBM...]
    all_to_all x1, waiting for transfers between devices: 5 us -> 6.51 us  [on_device(): y = lax.all_to_all(back, 'seq', 0, 0)]
    ppermute x3, waiting for transfers between devices: 3.12 us -> 2.1 us  [on_device(): pieces.append(lax.ppermute(mine, 'seq', ring) if step else mine)]
  transfers between devices with their start and end apart: 9 -> 9, of which waited for: 6 -> 6; matrix products, arithmetic and copies ran while one was open for 4% -> 2% of each run, Pallas kernels for 23% -> 23%
where the time goes in v4:
time: 83 us; the launch traced here: 82.5 us
  starting transfers between devices  35 us (42%)
  Pallas kernels  26.8 us (32%)
  waiting for transfers between devices  16.1 us (19%)
  local copies, waits for them, and re-layouts  2.62 us (3%)
  between operations  1.41 us (2%)
    pallas_call x7, Pallas kernels, call(): pl.pallas_call(kernel, out_shape=[(pltpu.VMEM if n in keep else pltpu.HBM...  26.8 us
    all_to_all x1, starting transfers between devices, on_device(): x = lax.all_to_all(send, 'seq', 0, 0)  13.6 us
    ppermute x3, starting transfers between devices, on_device(): lax.ppermute(weight, 'slide', [(n, n ^ bits) for n in range(4)])  8.29 us
    all_to_all x1, starting transfers between devices, on_device(): y = lax.all_to_all(back, 'seq', 0, 0)  7.68 us
    all_to_all x1, waiting for transfers between devices, on_device(): y = lax.all_to_all(back, 'seq', 0, 0)  6.51 us
    all_to_all x1, waiting for transfers between devices, on_device(): x = lax.all_to_all(send, 'seq', 0, 0)  6.4 us
    ppermute x3, starting transfers between devices, on_device(): pieces.append(lax.ppermute(mine, 'seq', ring) if step else mine)  4.49 us
    ppermute x3, waiting for transfers between devices, on_device(): pieces.append(lax.ppermute(mine, 'seq', ring) if step else mine)  2.1 us
  transfers between devices with their start and end apart: 9, of which 6 were waited for; matrix products, arithmetic and copies ran while one was open for 2% of the time, Pallas kernels for 23%

profile of v4, /device:TPU:1, one launch (start us, length us, event | category | flops | bytes accessed | tf_op | source)
XLA Modules:
  0.0 82.5 jit_solution(18030230265793895757)
XLA Ops:
  1.3 4.2 %shard_map.101 = (bf16[64,40,128]{2,1,0:T(8,128)(2,1)}, s32[8,128]{1,0:T(8,128)S(1)}) custom-call(s32[1]{0:T(128)S(6)} %copy.13.count_ref, bf16[256,768]{1,0:T(8,128)(2,1)} %bitcast.16, bf16[256,768]{1,0:T(8,128)(2,1)} %bitcast.20, bf16[256,768]{1,0:T(8,128)(2,1)} %bitcast.24, bf16[256,768]{1,0:T(8,128)(2,1)} %bitcast.27), custom_call_target="tpu_custom_call" | custom-call | tf_op jit(solution)/shard_map/pallas_call | solution.py:303
  5.5 13.6 %all-to-all-start = ((bf16[64,40,128]{2,1,0:T(8,128)(2,1)}), bf16[64,40,128]{2,1,0:T(8,128)(2,1)S(1)}, u32[]{:S(2)}, u32[]{:S(2)}) async-start(bf16[64,40,128]{2,1,0:T(8,128)(2,1)} %get-tuple-element.26), calls=%async_computation | async-start | bytes 1310720 | tf_op jit(solution)/shard_map/all_to_all | solution.py:322
  19.1 5.4 %shard_map.102 = (bf16[768,256]{1,0:T(8,128)(2,1)}, f32[16,256]{1,0:T(8,128)}, bf16[64,40,128]{2,1,0:T(8,128)(2,1)}, bf16[64,40,128]{2,1,0:T(8,128)(2,1)}) custom-call(s32[8,128]{1,0:T(8,128)S(1)} %get-tuple-element.25.count_ref, bf16[256,768]{1,0:T(8,128)(2,1)} %bitcast.17, bf16[256,768]{1,0:T(8,128)(2,1)} %bitcast.21, bf16[256,768]{1,0:T(8,128)(2,1)} %bitcast.25, ...), custom_call_target="tpu_custom_call" | custom-call | tf_op jit(solution)/shard_map/pallas_call | solution.py:303
  24.5 0.9 %collective-permute-start = (bf16[64,40,128]{2,1,0:T(8,128)(2,1)}, bf16[64,40,128]{2,1,0:T(8,128)(2,1)S(1)}, u32[]{:S(2)}, u32[]{:S(2)}) collective-permute-start(bf16[64,40,128]{2,1,0:T(8,128)(2,1)} %get-tuple-element.28), channel_id=1, source_target_pairs={{0,64},{64,0},{128,192},{192,128},{1,65},{65,1},{129,193},{193,129... | collective-permute-start | bytes 1966088 | tf_op jit(solution)/shard_map/ppermute | solution.py:330
  25.4 0.9 %constant_dynamic-slice_fusion.w_ref = bf16[48,768]{1,0:T(8,128)(2,1)S(1)} fusion(bf16[768,768]{1,0:T(8,128)(2,1)} %w_ref.3, s32[]{:T(128)S(6)} %select_n.44), kind=kLoop, calls=%fused_computation.5 | loop fusion | bytes 147460 | tf_op jit(solution)/shard_map/dynamic_slice | solution.py:333
  26.3 1.0 %collective-permute-done.got_ref = bf16[64,40,128]{2,1,0:T(8,128)(2,1)S(1)} collective-permute-done((bf16[64,40,128]{2,1,0:T(8,128)(2,1)}, bf16[64,40,128]{2,1,0:T(8,128)(2,1)S(1)}, u32[]{:S(2)}, u32[]{:S(2)}) %collective-permute-start) | collective-permute-done | bytes 655392 | tf_op jit(solution)/shard_map/ppermute | solution.py:330
  27.4 0.8 %copy-done = bf16[64,40,128]{2,1,0:T(8,128)(2,1)} copy-done((bf16[64,40,128]{2,1,0:T(8,128)(2,1)}, bf16[64,40,128]{2,1,0:T(8,128)(2,1)S(1)}, u32[]{:S(2)}) %copy-start) | copy-done | bytes 655384
  28.2 2.4 %shard_map.103.joined_ref = bf16[64,56,128]{2,1,0:T(8,128)(2,1)} custom-call(bf16[64,40,128]{2,1,0:T(8,128)(2,1)} %get-tuple-element.27.keep_ref, bf16[64,40,128]{2,1,0:T(8,128)(2,1)} %copy-done), custom_call_target="tpu_custom_call" | custom-call | tf_op jit(solution)/shard_map/pallas_call | solution.py:303
  30.6 6.4 %all-to-all-done.x_ref = bf16[64,40,128]{2,1,0:T(8,128)(2,1)S(1)} async-done(((bf16[64,40,128]{2,1,0:T(8,128)(2,1)}), bf16[64,40,128]{2,1,0:T(8,128)(2,1)S(1)}, u32[]{:S(2)}, u32[]{:S(2)}) %all-to-all-start) | async-done | bytes 655392 | tf_op jit(solution)/shard_map/all_to_all | solution.py:322
  37.0 3.1 %shard_map.104 = (bf16[64,56,128]{2,1,0:T(8,128)(2,1)}, f32[4,12,768]{2,1,0:T(8,128)}) custom-call(s32[8,128]{1,0:T(8,128)S(1)} %get-tuple-element.25.count_ref, bf16[64,40,128]{2,1,0:T(8,128)(2,1)S(1)} %all-to-all-done.x_ref, bf16[48,768]{1,0:T(8,128)(2,1)S(1)} %constant_dynamic-slice_fusion.w_ref, ...), custom_call_target="tpu_custom_call", output_to_operand_aliasing={{0}: (3, {})} | custom-call | tf_op jit(solution)/shard_map/pallas_call | solution.py:303
  40.1 7.7 %all-to-all-start.1 = ((bf16[64,56,128]{2,1,0:T(8,128)(2,1)}), bf16[64,56,128]{2,1,0:T(8,128)(2,1)S(1)}, u32[]{:S(2)}, u32[]{:S(2)}) async-start(bf16[64,56,128]{2,1,0:T(8,128)(2,1)} %get-tuple-element.29), calls=%async_computation.1 | async-start | bytes 1835008 | tf_op jit(solution)/shard_map/all_to_all | solution.py:353
  47.9 7.2 %shard_map.105 = (f32[256,768]{1,0:T(8,128)S(1)}, f32[256,768]{1,0:T(8,128)S(1)}, f32[256,768]{1,0:T(8,128)S(1)}, f32[256,768]{1,0:T(8,128)}, bf16[256,768]{1,0:...) custom-call(s32[8,128]{1,0:T(8,128)S(1)} %get-tuple-element.25.count_ref, ...), custom_call_target="tpu_custom_call" | custom-call | tf_op jit(solution)/shard_map/pallas_call | solution.py:303
  55.0 0.9 %dynamic-slice_bitcast_fusion = (f32[12,768]{1,0:T(8,128)S(1)}, f32[12,768]{1,0:T(8,128)S(1)}, f32[12,768]{1,0:T(8,128)S(1)}, f32[12,768]{1,0:T(8,128)S(1)}) fusion(f32[4,12,768]{2,1,0:T(8,128)} %get-tuple-element.44, s32[]{:T(128)S(6)} %select_n.53, s32[]{:T(128)S(6)} %select_n.51, s32[]{:T(128)S(6)} %select_n.49, s32[]{:T(128)S(6)} %select_n.47), kind=kLoop, calls=%fused_computation.1 | loop fusion | bytes 294928 | tf_op jit(solution)/shard_map/jit(dynamic_index_in_dim)/squeeze | solution.py:365
  55.9 0.9 %collective-permute-start.1 = (f32[12,768]{1,0:T(8,128)S(1)}, f32[12,768]{1,0:T(8,128)S(1)}, u32[]{:S(2)}, u32[]{:S(2)}) collective-permute-start(f32[12,768]{1,0:T(8,128)S(1)} %get-tuple-element.47), channel_id=1, source_target_pairs={{0,1},{1,2},{2,3},{3,0},{4,5},{5,6},{6,7},{7,4},{8,9},{9,10},{10,1... | collective-permute-start | bytes 110600 | tf_op jit(solution)/shard_map/ppermute | solution.py:367
  56.8 2.4 %collective-permute-start.2 = (f32[12,768]{1,0:T(8,128)S(1)}, f32[12,768]{1,0:T(8,128)S(1)}, u32[]{:S(2)}, u32[]{:S(2)}) collective-permute-start(f32[12,768]{1,0:T(8,128)S(1)} %get-tuple-element.46), channel_id=1, source_target_pairs={{0,2},{1,3},{2,0},{3,1},{4,6},{5,7},{6,4},{7,5},{8,10},{9,11},{10,... | collective-permute-start | bytes 110600 | tf_op jit(solution)/shard_map/ppermute | solution.py:367
  59.2 1.2 %collective-permute-start.3 = (f32[12,768]{1,0:T(8,128)S(1)}, f32[12,768]{1,0:T(8,128)S(1)}, u32[]{:S(2)}, u32[]{:S(2)}) collective-permute-start(f32[12,768]{1,0:T(8,128)S(1)} %get-tuple-element.45), channel_id=1, source_target_pairs={{0,3},{1,0},{2,1},{3,2},{4,7},{5,4},{6,5},{7,6},{8,11},{9,8},{10,9... | collective-permute-start | bytes 110600 | tf_op jit(solution)/shard_map/ppermute | solution.py:367
  60.4 0.6 collective-permute-done.1.b_ref
  61.0 1.0 %collective-permute-done.2.c_ref = f32[12,768]{1,0:T(8,128)S(1)} collective-permute-done((f32[12,768]{1,0:T(8,128)S(1)}, f32[12,768]{1,0:T(8,128)S(1)}, u32[]{:S(2)}, u32[]{:S(2)}) %collective-permute-start.2) | collective-permute-done | bytes 36896 | tf_op jit(solution)/shard_map/ppermute | solution.py:367
  62.1 0.5 collective-permute-done.3.d_ref
  62.5 6.5 %all-to-all-done.1.x_ref.y_ref = bf16[64,56,128]{2,1,0:T(8,128)(2,1)S(1)} async-done(((bf16[64,56,128]{2,1,0:T(8,128)(2,1)}), bf16[64,56,128]{2,1,0:T(8,128)(2,1)S(1)}, u32[]{:S(2)}, u32[]{:S(2)}) %all-to-all-start.1) | async-done | bytes 917536 | tf_op jit(solution)/shard_map/all_to_all | solution.py:353
  69.2 2.5 %collective-permute-start.4 = (f32[12,768]{1,0:T(8,128)S(1)}, f32[12,768]{1,0:T(8,128)S(1)}, u32[]{:S(2)}, u32[]{:S(2)}) collective-permute-start(f32[12,768]{1,0:T(8,128)S(1)} %shard_map.107), channel_id=1, source_target_pairs={{0,128},{64,192},{128,0},{192,64},{1,129},{65,193},{129,1},{193,65... | collective-permute-start | bytes 110600 | tf_op jit(solution)/shard_map/ppermute | solution.py:371
  71.7 5.8 %collective-permute-start.5 = (f32[12,768]{1,0:T(8,128)S(1)}, f32[12,768]{1,0:T(8,128)S(1)}, u32[]{:S(2)}, u32[]{:S(2)}) collective-permute-start(f32[12,768]{1,0:T(8,128)S(1)} %shard_map.107), channel_id=1, source_target_pairs={{0,192},{64,128},{128,64},{192,0},{1,193},{65,129},{129,65},{193,1... | collective-permute-start | bytes 110600 | tf_op jit(solution)/shard_map/ppermute | solution.py:371
  77.5 4.4 %shard_map.106 = (bf16[256,768]{1,0:T(8,128)(2,1)}, bf16[256,768]{1,0:T(8,128)(2,1)}, bf16[256,768]{1,0:T(8,128)(2,1)}, bf16[256,768]{1,0:T(8,128)(2,1)}) custom-call(s32[8,128]{1,0:T(8,128)S(1)} %get-tuple-element.25.count_ref, bf16[256,768]{1,0:T(8,128)(2,1)} %bitcast.19, bf16[256,768]{1,0:T(8,128)(2,1)} %bitcast.23, bf16[768,768]{1,0:T(8,128)(2,1)} %w_ref.3, ...), custom_call_target="tpu_custom_call" | custom-call | tf_op jit(solution)/shard_map/pallas_call | solution.py:303
  81.9 0.6 add_add_fusion
  (6 shorter events, 0.1 us)
Async XLA Ops:
  5.5 31.5 %all-to-all-start = ((bf16[64,40,128]{2,1,0:T(8,128)(2,1)}), bf16[64,40,128]{2,1,0:T(8,128)(2,1)S(1)}, u32[]{:S(2)}, u32[]{:S(2)}) async-start(bf16[64,40,128]{2,1,0:T(8,128)(2,1)} %get-tuple-element.26), calls=%async_computation | async-start | bytes 1310720 | tf_op jit(solution)/shard_map/all_to_all | solution.py:322
  24.5 2.9 %collective-permute-start = (bf16[64,40,128]{2,1,0:T(8,128)(2,1)}, bf16[64,40,128]{2,1,0:T(8,128)(2,1)S(1)}, u32[]{:S(2)}, u32[]{:S(2)}) collective-permute-start(bf16[64,40,128]{2,1,0:T(8,128)(2,1)} %get-tuple-element.28), channel_id=1, source_target_pairs={{0,64},{64,0},{128,192},{192,128},{1,65},{65,1},{129,193},{193,129... | collective-permute-start | bytes 1966088 | tf_op jit(solution)/shard_map/ppermute | solution.py:330
  27.4 0.8 %copy-start = (bf16[64,40,128]{2,1,0:T(8,128)(2,1)}, bf16[64,40,128]{2,1,0:T(8,128)(2,1)S(1)}, u32[]{:S(2)}) copy-start(bf16[64,40,128]{2,1,0:T(8,128)(2,1)S(1)} %collective-permute-done.got_ref) | copy-start | bytes 1966084
  40.1 28.9 %all-to-all-start.1 = ((bf16[64,56,128]{2,1,0:T(8,128)(2,1)}), bf16[64,56,128]{2,1,0:T(8,128)(2,1)S(1)}, u32[]{:S(2)}, u32[]{:S(2)}) async-start(bf16[64,56,128]{2,1,0:T(8,128)(2,1)} %get-tuple-element.29), calls=%async_computation.1 | async-start | bytes 1835008 | tf_op jit(solution)/shard_map/all_to_all | solution.py:353
  55.9 5.1 %collective-permute-start.1 = (f32[12,768]{1,0:T(8,128)S(1)}, f32[12,768]{1,0:T(8,128)S(1)}, u32[]{:S(2)}, u32[]{:S(2)}) collective-permute-start(f32[12,768]{1,0:T(8,128)S(1)} %get-tuple-element.47), channel_id=1, source_target_pairs={{0,1},{1,2},{2,3},{3,0},{4,5},{5,6},{6,7},{7,4},{8,9},{9,10},{10,1... | collective-permute-start | bytes 110600 | tf_op jit(solution)/shard_map/ppermute | solution.py:367
  56.8 5.2 %collective-permute-start.2 = (f32[12,768]{1,0:T(8,128)S(1)}, f32[12,768]{1,0:T(8,128)S(1)}, u32[]{:S(2)}, u32[]{:S(2)}) collective-permute-start(f32[12,768]{1,0:T(8,128)S(1)} %get-tuple-element.46), channel_id=1, source_target_pairs={{0,2},{1,3},{2,0},{3,1},{4,6},{5,7},{6,4},{7,5},{8,10},{9,11},{10,... | collective-permute-start | bytes 110600 | tf_op jit(solution)/shard_map/ppermute | solution.py:367
  59.2 3.3 %collective-permute-start.3 = (f32[12,768]{1,0:T(8,128)S(1)}, f32[12,768]{1,0:T(8,128)S(1)}, u32[]{:S(2)}, u32[]{:S(2)}) collective-permute-start(f32[12,768]{1,0:T(8,128)S(1)} %get-tuple-element.45), channel_id=1, source_target_pairs={{0,3},{1,0},{2,1},{3,2},{4,7},{5,4},{6,5},{7,6},{8,11},{9,8},{10,9... | collective-permute-start | bytes 110600 | tf_op jit(solution)/shard_map/ppermute | solution.py:367
  69.2 12.7 %collective-permute-start.4 = (f32[12,768]{1,0:T(8,128)S(1)}, f32[12,768]{1,0:T(8,128)S(1)}, u32[]{:S(2)}, u32[]{:S(2)}) collective-permute-start(f32[12,768]{1,0:T(8,128)S(1)} %shard_map.107), channel_id=1, source_target_pairs={{0,128},{64,192},{128,0},{192,64},{1,129},{65,193},{129,1},{193,65... | collective-permute-start | bytes 110600 | tf_op jit(solution)/shard_map/ppermute | solution.py:371
  71.7 10.2 %collective-permute-start.5 = (f32[12,768]{1,0:T(8,128)S(1)}, f32[12,768]{1,0:T(8,128)S(1)}, u32[]{:S(2)}, u32[]{:S(2)}) collective-permute-start(f32[12,768]{1,0:T(8,128)S(1)} %shard_map.107), channel_id=1, source_target_pairs={{0,192},{64,128},{128,64},{192,0},{1,193},{65,129},{129,65},{193,1... | collective-permute-start | bytes 110600 | tf_op jit(solution)/shard_map/ppermute | solution.py:371
  77.5 4.4 %collective-permute-start.6 = (f32[12,768]{1,0:T(8,128)S(1)}, f32[12,768]{1,0:T(8,128)S(1)}, u32[]{:S(2)}, u32[]{:S(2)}) collective-permute-start(f32[12,768]{1,0:T(8,128)S(1)} %shard_map.107), channel_id=1, source_target_pairs={{0,64},{64,0},{128,192},{192,128},{1,65},{65,1},{129,193},{193,129... | collective-permute-start | bytes 110600 | tf_op jit(solution)/shard_map/ppermute | solution.py:371

commit v5 on v4

--- a/solution.py
+++ b/solution.py
@@ -94,7 +94,7 @@
             for j in range(4):
                 at = 16 * (4 * j + ii)
                 rows[pl.ds(16 * j + i, 16, stride=64), :] = jnp.where(late, turned[at : at + 16], c[16 * i : 16 * i + 16])
-    out_ref[:, 0:16, :] = rows[...].astype(BF).reshape(PEERS, 16, LANES)
+    out_ref[:, 0:16, :] = rows[0 : PEERS * 16, :].astype(BF).reshape(PEERS, 16, LANES)
     valid_row = (row_start + iota((ROWS, WIDTH), 0)) < tile_count
     g = jnp.where(valid_row, g_ref[...].astype(F32), 0.0)
     for j in range(4):
@@ -102,7 +102,7 @@
             at = 16 * (4 * j + ii)
             for t in range(6):
                 grads[pl.ds(24 * j + 4 * t + ii, 16, stride=96), :] = g[at : at + 16, 128 * t : 128 * t + 128]
-    out_ref[:, 16:40, :] = grads[...].astype(BF).reshape(PEERS, 24, LANES)
+    out_ref[:, 16:40, :] = grads[0 : PEERS * 24, :].astype(BF).reshape(PEERS, 24, LANES)
 
 
 def head_window(h):
@@ -132,7 +132,7 @@
             lse_ref[h : h + 1, :] = jnp.where(column == h, 1e30, m + jnp.log2(l))
     partial = nn(at_ref[...], g)
     for t in range(6):
-        big[t] = partial[:, 128 * t : 128 * t + 128]
+        big[t, 0:WIDTH, :] = partial[:, 128 * t : 128 * t + 128]
     zero = jnp.zeros((PEERS, LANES), F32)
     for i in range(36, PART_ROWS):
         part[pl.ds(i, PEERS, stride=PART_ROWS), :] = zero
@@ -140,7 +140,7 @@
         for i in range(6):
             for t in range(6):
                 part[pl.ds(6 * i + t, PEERS, stride=PART_ROWS), :] = big[t, pl.ds(6 * c + i, PEERS, stride=12), :]
-        ref[...] = part[...].astype(BF).reshape(PEERS, PART_ROWS, LANES)
+        ref[...] = part[0 : PEERS * PART_ROWS, :].astype(BF).reshape(PEERS, PART_ROWS, LANES)
 
 
 def join_kernel(keep_ref, got_ref, out_ref):
@@ -188,8 +188,8 @@
 def far_kernel(count_ref, x_ref, w_ref, joined_ref, back_ref, strided_ref, xs, gs, ps):
     tile_count, head = count_ref[0:1, 0:1], lax.axis_index("seq") // 4
     x = x_ref[:, 0:16, :].reshape(PEERS * 16, LANES)
-    xs[...] = x.astype(F32)
-    gs[...] = x_ref[:, 16:40, :].astype(F32).reshape(PEERS * 24, LANES)
+    xs[0 : PEERS * 16, :] = x.astype(F32)
+    gs[0 : PEERS * 24, :] = x_ref[:, 16:40, :].astype(F32).reshape(PEERS * 24, LANES)
     lane = iota((PEERS, LANES), 1)
     parts, grads = [], []
     for ii in range(4):
@@ -214,7 +214,7 @@
     near = jnp.exp(lse_near - m)
     l = jnp.sum(p, axis=0, keepdims=True) + near
     inv = 1.0 / l
-    xt = xs[...].T.astype(BF)
+    xt = xs[0 : PEERS * 16, :].T.astype(BF)
     middle = (row >= 48) & (row < 96)
     att = jnp.where(middle, (nn(xt, p.astype(BF)) + near * dt) * inv, 0.0).astype(BF)
     w_pad = jnp.concatenate([jnp.zeros((48, WIDTH), BF), w_ref[...], jnp.zeros((32, WIDTH), BF)], axis=0)
@@ -230,13 +230,13 @@
     e = jnp.where(row < 48, dq, att.astype(F32))
     e = jnp.where(row == 96, hi, jnp.where(row == 97, mid, jnp.where(row == 98, lo, e)))
     e = e.T
-    ps[...] = nn(ds, q_row) * SCALE + nn(p.astype(BF), ga_row)
+    ps[0 : PEERS * 16, :] = nn(ds, q_row) * SCALE + nn(p.astype(BF), ga_row)
     for a in range(4):
         turned = e if a == 3 else pltpu.roll(e, 96 - 32 * a, 1)
         for ii in range(4):
             at = pl.ds(4 * a + ii, PEERS, stride=16)
             ps[at, :] = jnp.where(lane >= 96, turned[64 * ii : 64 * ii + 64], ps[at, :])
-    back_ref[...] = ps[...].astype(BF).reshape(PEERS, 16, LANES)
+    back_ref[...] = ps[0 : PEERS * 16, :].astype(BF).reshape(PEERS, 16, LANES)
     partial = nn(att, g)
     for j in range(4):
         strided_ref[j] = partial[48 + 12 * j : 60 + 12 * j]
@@ -244,7 +244,7 @@
 
 def weight_kernel(y_ref, a_ref, b_ref, c_ref, d_ref, out_ref, scr):
     core = lax.axis_index("slide") % 2
-    scr[...] = jnp.sum(y_ref[:, 16:56, :].astype(F32), axis=0)
+    scr[0:PART_ROWS, :] = jnp.sum(y_ref[:, 16:56, :].astype(F32), axis=0)
     rest = jnp.concatenate([scr[pl.ds(t, 6, stride=6), :] for t in range(6)], axis=1)
     zero = jnp.zeros((6, WIDTH), F32)
     total = (a_ref[...] + b_ref[...]) + (c_ref[...] + d_ref[...])
@@ -255,7 +255,7 @@
 def final_kernel(count_ref, q_ref, k_ref, w_ref, x_ref, s_ref, dp_ref, ga_ref, layer_ref, dq0_ref, dk0_ref, dv0_ref,
                  out_ref, dq_ref, dk_ref, dv_ref, xs):
     row_start, tile_count = lax.axis_index("seq") * ROWS, count_ref[0:1, 0:1]
-    xs[...] = x_ref[...].astype(F32).reshape(PEERS * 16, LANES)
+    xs[0 : PEERS * 16, :] = x_ref[...].astype(F32).reshape(PEERS * 16, LANES)
     lane = iota((16, LANES), 1)
     e_rows = [None] * 16
     dkv_rows = []
@@ -317,14 +317,14 @@
 
     send, count = call(
         pack_kernel, (tile_counts, q, k, v, g), [((PEERS, SEND_ROWS, LANES), BF), ((8, LANES), jnp.int32)],
-        [((PEERS * 16, LANES), F32), ((PEERS * 24, LANES), F32)], keep=(0, 1), scalars=True,
+        [((PEERS * 16 + 64, LANES), F32), ((PEERS * 24 + 96, LANES), F32)], keep=(0, 1), scalars=True,
     )
     x = lax.all_to_all(send, "seq", 0, 0)
 
     part = (PEERS, PART_ROWS, LANES)
     at0, lse0, keep, swap = call(
         forward_kernel, (count, q, k, v, g), [(tall, BF), ((HEADS, ROWS), F32), (part, BF), (part, BF)],
-        [(tall, BF), (tall, BF), ((6, WIDTH, LANES), F32), ((PEERS * PART_ROWS, LANES), F32)],
+        [(tall, BF), (tall, BF), ((6, WIDTH + 16, LANES), F32), (((PEERS + 1) * PART_ROWS, LANES), F32)],
         near=(0,),
     )
     got = lax.ppermute(swap, "slide", other_core)
@@ -337,7 +337,7 @@
         far_kernel,
         (count, x, w_head, joined),
         [((PEERS, BACK_ROWS, LANES), BF), ((4, 12, WIDTH), F32)],
-        [((PEERS * n, LANES), F32) for n in (16, 24, 16)],
+        [(((PEERS + 1) * n, LANES), F32) for n in (16, 24, 16)],
         near=(0, 1, 2, 3),
         keep=(0,),
         grid=(1,),
@@ -366,7 +366,7 @@
         ring = [(d, d // 4 * 4 + (d + step) % 4) for d in range(PEERS)]
         pieces.append(lax.ppermute(mine, "seq", ring) if step else mine)
     (weight,) = call(
-        weight_kernel, (y, *pieces), [((12, WIDTH), F32)], [((PART_ROWS, LANES), F32)], near=(0, 1, 2, 3, 4), keep=(0,)
+        weight_kernel, (y, *pieces), [((12, WIDTH), F32)], [((PART_ROWS + 8, LANES), F32)], near=(0, 1, 2, 3, 4), keep=(0,)
     )
     others = [lax.ppermute(weight, "slide", [(n, n ^ bits) for n in range(4)]) for bits in (2, 3, 1)]
 
@@ -374,7 +374,7 @@
         final_kernel,
         (count, q, k, out_weight, y, s0, dp0, ga, layer0, dq0, dk0, dv0),
         [(flat, BF)] * 4,
-        [((PEERS * 16, LANES), F32)],
+        [((PEERS * 16 + 64, LANES), F32)],
         near=(0, 4, 9, 10, 11),
         grid=(1,),
         in_specs=[held] * 4 + [whole(PEERS, 16, LANES)] + [held] * 7,

time: 83 us -> 83 us (level)
  no operation moved by 1% of the time
where the time goes in v5:
time: 83 us; the launch traced here: 82.5 us
  starting transfers between devices  35 us (42%)
  Pallas kernels  26.8 us (32%)
  waiting for transfers between devices  16.1 us (19%)
  local copies, waits for them, and re-layouts  2.62 us (3%)
  between operations  1.41 us (2%)
    pallas_call x7, Pallas kernels, call(): pl.pallas_call(kernel, out_shape=[(pltpu.VMEM if n in keep else pltpu.HBM...  26.8 us
    all_to_all x1, starting transfers between devices, on_device(): x = lax.all_to_all(send, 'seq', 0, 0)  13.6 us
    ppermute x3, starting transfers between devices, on_device(): lax.ppermute(weight, 'slide', [(n, n ^ bits) for n in range(4)])  8.29 us
    all_to_all x1, starting transfers between devices, on_device(): y = lax.all_to_all(back, 'seq', 0, 0)  7.68 us
    all_to_all x1, waiting for transfers between devices, on_device(): y = lax.all_to_all(back, 'seq', 0, 0)  6.53 us
    all_to_all x1, waiting for transfers between devices, on_device(): x = lax.all_to_all(send, 'seq', 0, 0)  6.42 us
    ppermute x3, starting transfers between devices, on_device(): pieces.append(lax.ppermute(mine, 'seq', ring) if step else mine)  4.49 us
    ppermute x3, waiting for transfers between devices, on_device(): pieces.append(lax.ppermute(mine, 'seq', ring) if step else mine)  2.09 us
  transfers between devices with their start and end apart: 9, of which 6 were waited for; matrix products, arithmetic and copies ran while one was open for 2% of the time, Pallas kernels for 23%

profile of v5, /device:TPU:1, one launch (start us, length us, event | category | flops | bytes accessed | tf_op | source)
XLA Modules:
  0.0 82.5 jit_solution(2248060864799733917)
XLA Ops:
  1.3 4.2 %shard_map.101 = (bf16[64,40,128]{2,1,0:T(8,128)(2,1)}, s32[8,128]{1,0:T(8,128)S(1)}) custom-call(s32[1]{0:T(128)S(6)} %copy.13.count_ref, bf16[256,768]{1,0:T(8,128)(2,1)} %bitcast.16, bf16[256,768]{1,0:T(8,128)(2,1)} %bitcast.20, bf16[256,768]{1,0:T(8,128)(2,1)} %bitcast.24, bf16[256,768]{1,0:T(8,128)(2,1)} %bitcast.27), custom_call_target="tpu_custom_call" | custom-call | tf_op jit(solution)/shard_map/pallas_call | solution.py:303
  5.5 13.6 %all-to-all-start = ((bf16[64,40,128]{2,1,0:T(8,128)(2,1)}), bf16[64,40,128]{2,1,0:T(8,128)(2,1)S(1)}, u32[]{:S(2)}, u32[]{:S(2)}) async-start(bf16[64,40,128]{2,1,0:T(8,128)(2,1)} %get-tuple-element.26), calls=%async_computation | async-start | bytes 1310720 | tf_op jit(solution)/shard_map/all_to_all | solution.py:322
  19.1 5.3 %shard_map.102 = (bf16[768,256]{1,0:T(8,128)(2,1)}, f32[16,256]{1,0:T(8,128)}, bf16[64,40,128]{2,1,0:T(8,128)(2,1)}, bf16[64,40,128]{2,1,0:T(8,128)(2,1)}) custom-call(s32[8,128]{1,0:T(8,128)S(1)} %get-tuple-element.25.count_ref, bf16[256,768]{1,0:T(8,128)(2,1)} %bitcast.17, bf16[256,768]{1,0:T(8,128)(2,1)} %bitcast.21, bf16[256,768]{1,0:T(8,128)(2,1)} %bitcast.25, ...), custom_call_target="tpu_custom_call" | custom-call | tf_op jit(solution)/shard_map/pallas_call | solution.py:303
  24.5 1.0 %collective-permute-start = (bf16[64,40,128]{2,1,0:T(8,128)(2,1)}, bf16[64,40,128]{2,1,0:T(8,128)(2,1)S(1)}, u32[]{:S(2)}, u32[]{:S(2)}) collective-permute-start(bf16[64,40,128]{2,1,0:T(8,128)(2,1)} %get-tuple-element.28), channel_id=1, source_target_pairs={{0,64},{64,0},{128,192},{192,128},{1,65},{65,1},{129,193},{193,129... | collective-permute-start | bytes 1966088 | tf_op jit(solution)/shard_map/ppermute | solution.py:330
  25.4 0.9 %constant_dynamic-slice_fusion.w_ref = bf16[48,768]{1,0:T(8,128)(2,1)S(1)} fusion(bf16[768,768]{1,0:T(8,128)(2,1)} %w_ref.3, s32[]{:T(128)S(6)} %select_n.44), kind=kLoop, calls=%fused_computation.5 | loop fusion | bytes 147460 | tf_op jit(solution)/shard_map/dynamic_slice | solution.py:333
  26.3 1.0 %collective-permute-done.got_ref = bf16[64,40,128]{2,1,0:T(8,128)(2,1)S(1)} collective-permute-done((bf16[64,40,128]{2,1,0:T(8,128)(2,1)}, bf16[64,40,128]{2,1,0:T(8,128)(2,1)S(1)}, u32[]{:S(2)}, u32[]{:S(2)}) %collective-permute-start) | collective-permute-done | bytes 655392 | tf_op jit(solution)/shard_map/ppermute | solution.py:330
  27.4 0.8 %copy-done = bf16[64,40,128]{2,1,0:T(8,128)(2,1)} copy-done((bf16[64,40,128]{2,1,0:T(8,128)(2,1)}, bf16[64,40,128]{2,1,0:T(8,128)(2,1)S(1)}, u32[]{:S(2)}) %copy-start) | copy-done | bytes 655384
  28.2 2.4 %shard_map.103.joined_ref = bf16[64,56,128]{2,1,0:T(8,128)(2,1)} custom-call(bf16[64,40,128]{2,1,0:T(8,128)(2,1)} %get-tuple-element.27.keep_ref, bf16[64,40,128]{2,1,0:T(8,128)(2,1)} %copy-done), custom_call_target="tpu_custom_call" | custom-call | tf_op jit(solution)/shard_map/pallas_call | solution.py:303
  30.6 6.4 %all-to-all-done.x_ref = bf16[64,40,128]{2,1,0:T(8,128)(2,1)S(1)} async-done(((bf16[64,40,128]{2,1,0:T(8,128)(2,1)}), bf16[64,40,128]{2,1,0:T(8,128)(2,1)S(1)}, u32[]{:S(2)}, u32[]{:S(2)}) %all-to-all-start) | async-done | bytes 655392 | tf_op jit(solution)/shard_map/all_to_all | solution.py:322
  37.0 3.1 %shard_map.104 = (bf16[64,56,128]{2,1,0:T(8,128)(2,1)}, f32[4,12,768]{2,1,0:T(8,128)}) custom-call(s32[8,128]{1,0:T(8,128)S(1)} %get-tuple-element.25.count_ref, bf16[64,40,128]{2,1,0:T(8,128)(2,1)S(1)} %all-to-all-done.x_ref, bf16[48,768]{1,0:T(8,128)(2,1)S(1)} %constant_dynamic-slice_fusion.w_ref, ...), custom_call_target="tpu_custom_call", output_to_operand_aliasing={{0}: (3, {})} | custom-call | tf_op jit(solution)/shard_map/pallas_call | solution.py:303
  40.1 7.7 %all-to-all-start.1 = ((bf16[64,56,128]{2,1,0:T(8,128)(2,1)}), bf16[64,56,128]{2,1,0:T(8,128)(2,1)S(1)}, u32[]{:S(2)}, u32[]{:S(2)}) async-start(bf16[64,56,128]{2,1,0:T(8,128)(2,1)} %get-tuple-element.29), calls=%async_computation.1 | async-start | bytes 1835008 | tf_op jit(solution)/shard_map/all_to_all | solution.py:353
  47.9 7.2 %shard_map.105 = (f32[256,768]{1,0:T(8,128)S(1)}, f32[256,768]{1,0:T(8,128)S(1)}, f32[256,768]{1,0:T(8,128)S(1)}, f32[256,768]{1,0:T(8,128)}, bf16[256,768]{1,0:...) custom-call(s32[8,128]{1,0:T(8,128)S(1)} %get-tuple-element.25.count_ref, ...), custom_call_target="tpu_custom_call" | custom-call | tf_op jit(solution)/shard_map/pallas_call | solution.py:303
  55.0 0.9 %dynamic-slice_bitcast_fusion = (f32[12,768]{1,0:T(8,128)S(1)}, f32[12,768]{1,0:T(8,128)S(1)}, f32[12,768]{1,0:T(8,128)S(1)}, f32[12,768]{1,0:T(8,128)S(1)}) fusion(f32[4,12,768]{2,1,0:T(8,128)} %get-tuple-element.44, s32[]{:T(128)S(6)} %select_n.53, s32[]{:T(128)S(6)} %select_n.51, s32[]{:T(128)S(6)} %select_n.49, s32[]{:T(128)S(6)} %select_n.47), kind=kLoop, calls=%fused_computation.1 | loop fusion | bytes 294928 | tf_op jit(solution)/shard_map/jit(dynamic_index_in_dim)/squeeze | solution.py:365
  55.9 0.9 %collective-permute-start.1 = (f32[12,768]{1,0:T(8,128)S(1)}, f32[12,768]{1,0:T(8,128)S(1)}, u32[]{:S(2)}, u32[]{:S(2)}) collective-permute-start(f32[12,768]{1,0:T(8,128)S(1)} %get-tuple-element.47), channel_id=1, source_target_pairs={{0,1},{1,2},{2,3},{3,0},{4,5},{5,6},{6,7},{7,4},{8,9},{9,10},{10,1... | collective-permute-start | bytes 110600 | tf_op jit(solution)/shard_map/ppermute | solution.py:367
  56.8 2.4 %collective-permute-start.2 = (f32[12,768]{1,0:T(8,128)S(1)}, f32[12,768]{1,0:T(8,128)S(1)}, u32[]{:S(2)}, u32[]{:S(2)}) collective-permute-start(f32[12,768]{1,0:T(8,128)S(1)} %get-tuple-element.46), channel_id=1, source_target_pairs={{0,2},{1,3},{2,0},{3,1},{4,6},{5,7},{6,4},{7,5},{8,10},{9,11},{10,... | collective-permute-start | bytes 110600 | tf_op jit(solution)/shard_map/ppermute | solution.py:367
  59.2 1.2 %collective-permute-start.3 = (f32[12,768]{1,0:T(8,128)S(1)}, f32[12,768]{1,0:T(8,128)S(1)}, u32[]{:S(2)}, u32[]{:S(2)}) collective-permute-start(f32[12,768]{1,0:T(8,128)S(1)} %get-tuple-element.45), channel_id=1, source_target_pairs={{0,3},{1,0},{2,1},{3,2},{4,7},{5,4},{6,5},{7,6},{8,11},{9,8},{10,9... | collective-permute-start | bytes 110600 | tf_op jit(solution)/shard_map/ppermute | solution.py:367
  60.4 0.6 collective-permute-done.1.b_ref
  61.0 1.0 %collective-permute-done.2.c_ref = f32[12,768]{1,0:T(8,128)S(1)} collective-permute-done((f32[12,768]{1,0:T(8,128)S(1)}, f32[12,768]{1,0:T(8,128)S(1)}, u32[]{:S(2)}, u32[]{:S(2)}) %collective-permute-start.2) | collective-permute-done | bytes 36896 | tf_op jit(solution)/shard_map/ppermute | solution.py:367
  62.1 0.5 collective-permute-done.3.d_ref
  62.5 6.5 %all-to-all-done.1.x_ref.y_ref = bf16[64,56,128]{2,1,0:T(8,128)(2,1)S(1)} async-done(((bf16[64,56,128]{2,1,0:T(8,128)(2,1)}), bf16[64,56,128]{2,1,0:T(8,128)(2,1)S(1)}, u32[]{:S(2)}, u32[]{:S(2)}) %all-to-all-start.1) | async-done | bytes 917536 | tf_op jit(solution)/shard_map/all_to_all | solution.py:353
  69.2 2.5 %collective-permute-start.4 = (f32[12,768]{1,0:T(8,128)S(1)}, f32[12,768]{1,0:T(8,128)S(1)}, u32[]{:S(2)}, u32[]{:S(2)}) collective-permute-start(f32[12,768]{1,0:T(8,128)S(1)} %shard_map.107), channel_id=1, source_target_pairs={{0,128},{64,192},{128,0},{192,64},{1,129},{65,193},{129,1},{193,65... | collective-permute-start | bytes 110600 | tf_op jit(solution)/shard_map/ppermute | solution.py:371
  71.7 5.8 %collective-permute-start.5 = (f32[12,768]{1,0:T(8,128)S(1)}, f32[12,768]{1,0:T(8,128)S(1)}, u32[]{:S(2)}, u32[]{:S(2)}) collective-permute-start(f32[12,768]{1,0:T(8,128)S(1)} %shard_map.107), channel_id=1, source_target_pairs={{0,192},{64,128},{128,64},{192,0},{1,193},{65,129},{129,65},{193,1... | collective-permute-start | bytes 110600 | tf_op jit(solution)/shard_map/ppermute | solution.py:371
  77.5 4.4 %shard_map.106 = (bf16[256,768]{1,0:T(8,128)(2,1)}, bf16[256,768]{1,0:T(8,128)(2,1)}, bf16[256,768]{1,0:T(8,128)(2,1)}, bf16[256,768]{1,0:T(8,128)(2,1)}) custom-call(s32[8,128]{1,0:T(8,128)S(1)} %get-tuple-element.25.count_ref, bf16[256,768]{1,0:T(8,128)(2,1)} %bitcast.19, bf16[256,768]{1,0:T(8,128)(2,1)} %bitcast.23, bf16[768,768]{1,0:T(8,128)(2,1)} %w_ref.3, ...), custom_call_target="tpu_custom_call" | custom-call | tf_op jit(solution)/shard_map/pallas_call | solution.py:303
  81.9 0.6 add_add_fusion
  (6 shorter events, 0.1 us)
Async XLA Ops:
  5.5 31.5 %all-to-all-start = ((bf16[64,40,128]{2,1,0:T(8,128)(2,1)}), bf16[64,40,128]{2,1,0:T(8,128)(2,1)S(1)}, u32[]{:S(2)}, u32[]{:S(2)}) async-start(bf16[64,40,128]{2,1,0:T(8,128)(2,1)} %get-tuple-element.26), calls=%async_computation | async-start | bytes 1310720 | tf_op jit(solution)/shard_map/all_to_all | solution.py:322
  24.5 2.9 %collective-permute-start = (bf16[64,40,128]{2,1,0:T(8,128)(2,1)}, bf16[64,40,128]{2,1,0:T(8,128)(2,1)S(1)}, u32[]{:S(2)}, u32[]{:S(2)}) collective-permute-start(bf16[64,40,128]{2,1,0:T(8,128)(2,1)} %get-tuple-element.28), channel_id=1, source_target_pairs={{0,64},{64,0},{128,192},{192,128},{1,65},{65,1},{129,193},{193,129... | collective-permute-start | bytes 1966088 | tf_op jit(solution)/shard_map/ppermute | solution.py:330
  27.3 0.8 %copy-start = (bf16[64,40,128]{2,1,0:T(8,128)(2,1)}, bf16[64,40,128]{2,1,0:T(8,128)(2,1)S(1)}, u32[]{:S(2)}) copy-start(bf16[64,40,128]{2,1,0:T(8,128)(2,1)S(1)} %collective-permute-done.got_ref) | copy-start | bytes 1966084
  40.1 28.9 %all-to-all-start.1 = ((bf16[64,56,128]{2,1,0:T(8,128)(2,1)}), bf16[64,56,128]{2,1,0:T(8,128)(2,1)S(1)}, u32[]{:S(2)}, u32[]{:S(2)}) async-start(bf16[64,56,128]{2,1,0:T(8,128)(2,1)} %get-tuple-element.29), calls=%async_computation.1 | async-start | bytes 1835008 | tf_op jit(solution)/shard_map/all_to_all | solution.py:353
  55.9 5.1 %collective-permute-start.1 = (f32[12,768]{1,0:T(8,128)S(1)}, f32[12,768]{1,0:T(8,128)S(1)}, u32[]{:S(2)}, u32[]{:S(2)}) collective-permute-start(f32[12,768]{1,0:T(8,128)S(1)} %get-tuple-element.47), channel_id=1, source_target_pairs={{0,1},{1,2},{2,3},{3,0},{4,5},{5,6},{6,7},{7,4},{8,9},{9,10},{10,1... | collective-permute-start | bytes 110600 | tf_op jit(solution)/shard_map/ppermute | solution.py:367
  56.8 5.2 %collective-permute-start.2 = (f32[12,768]{1,0:T(8,128)S(1)}, f32[12,768]{1,0:T(8,128)S(1)}, u32[]{:S(2)}, u32[]{:S(2)}) collective-permute-start(f32[12,768]{1,0:T(8,128)S(1)} %get-tuple-element.46), channel_id=1, source_target_pairs={{0,2},{1,3},{2,0},{3,1},{4,6},{5,7},{6,4},{7,5},{8,10},{9,11},{10,... | collective-permute-start | bytes 110600 | tf_op jit(solution)/shard_map/ppermute | solution.py:367
  59.2 3.3 %collective-permute-start.3 = (f32[12,768]{1,0:T(8,128)S(1)}, f32[12,768]{1,0:T(8,128)S(1)}, u32[]{:S(2)}, u32[]{:S(2)}) collective-permute-start(f32[12,768]{1,0:T(8,128)S(1)} %get-tuple-element.45), channel_id=1, source_target_pairs={{0,3},{1,0},{2,1},{3,2},{4,7},{5,4},{6,5},{7,6},{8,11},{9,8},{10,9... | collective-permute-start | bytes 110600 | tf_op jit(solution)/shard_map/ppermute | solution.py:367
  69.2 12.7 %collective-permute-start.4 = (f32[12,768]{1,0:T(8,128)S(1)}, f32[12,768]{1,0:T(8,128)S(1)}, u32[]{:S(2)}, u32[]{:S(2)}) collective-permute-start(f32[12,768]{1,0:T(8,128)S(1)} %shard_map.107), channel_id=1, source_target_pairs={{0,128},{64,192},{128,0},{192,64},{1,129},{65,193},{129,1},{193,65... | collective-permute-start | bytes 110600 | tf_op jit(solution)/shard_map/ppermute | solution.py:371
  71.7 10.2 %collective-permute-start.5 = (f32[12,768]{1,0:T(8,128)S(1)}, f32[12,768]{1,0:T(8,128)S(1)}, u32[]{:S(2)}, u32[]{:S(2)}) collective-permute-start(f32[12,768]{1,0:T(8,128)S(1)} %shard_map.107), channel_id=1, source_target_pairs={{0,192},{64,128},{128,64},{192,0},{1,193},{65,129},{129,65},{193,1... | collective-permute-start | bytes 110600 | tf_op jit(solution)/shard_map/ppermute | solution.py:371
  77.5 4.4 %collective-permute-start.6 = (f32[12,768]{1,0:T(8,128)S(1)}, f32[12,768]{1,0:T(8,128)S(1)}, u32[]{:S(2)}, u32[]{:S(2)}) collective-permute-start(f32[12,768]{1,0:T(8,128)S(1)} %shard_map.107), channel_id=1, source_target_pairs={{0,64},{64,0},{128,192},{192,128},{1,65},{65,1},{129,193},{193,129... | collective-permute-start | bytes 110600 | tf_op jit(solution)/shard_map/ppermute | solution.py:371

commit v6 on v5

--- a/solution.py
+++ b/solution.py
@@ -20,7 +20,6 @@
 PART_ROWS = 40
 LIMIT = 48
 GROUP = 4
-POWER = SCALE * 1.4426950408889634
 
 
 def iota(shape, dim):
@@ -112,7 +111,7 @@
     return slice(a, b), slice(f, f + HEAD_WIDTH), onehot((lane >= f) & (lane < f + HEAD_WIDTH))
 
 
-def forward_kernel(count_ref, q_ref, k_ref, v_ref, g_ref, at_ref, lse_ref, keep_ref, send_ref, qt, vt, big, part):
+def forward_kernel(count_ref, q_ref, k_ref, v_ref, g_ref, at_ref, stat_ref, keep_ref, send_ref, qt, vt, big, part):
     row_start, tile_count, core = lax.axis_index("seq") * ROWS, count_ref[0:1, 0:1], lax.axis_index("slide") % 2
     valid_row = (row_start + iota((ROWS, WIDTH), 0)) < tile_count
     g = jnp.where(valid_row, g_ref[...].astype(F32), 0.0).astype(BF)
@@ -122,14 +121,16 @@
     column = iota((1, ROWS), 1) & 15
     for start in range(0, HEADS, GROUP):
         group = [(h, *head_window(h)) for h in range(start, start + GROUP)]
-        scores = [jnp.where(valid_key, nn(k_ref[:, w] * here, qt[w, :]), MASKED) for _, w, _, here in group]
-        tops = [jnp.max(s, axis=0, keepdims=True) * POWER for s in scores]
-        probs = [jnp.exp2(s * POWER - m) for s, m in zip(scores, tops)]
+        scores = [jnp.where(valid_key, nn(k_ref[:, w] * here, qt[w, :]) * SCALE, MASKED) for _, w, _, here in group]
+        tops = [jnp.max(s, axis=0, keepdims=True) for s in scores]
+        probs = [jnp.exp(s - m) for s, m in zip(scores, tops)]
         totals = [jnp.sum(p, axis=0, keepdims=True) for p in probs]
         sums = [nn(vt[rows, :], p.astype(BF)) for (_, _, rows, _), p in zip(group, probs)]
         for (h, _, rows, _), o, m, l in zip(group, sums, tops, totals):
-            at_ref[rows, :] = (o * jnp.where(column == h, 0.0, 1.0 / l)).astype(BF)
-            lse_ref[h : h + 1, :] = jnp.where(column == h, 1e30, m + jnp.log2(l))
+            inv = jnp.where(column == h, 0.0, 1.0 / l)
+            at_ref[rows, :] = (o * inv).astype(BF)
+            stat_ref[h : h + 1, :] = m
+            stat_ref[HEADS + h : HEADS + h + 1, :] = inv
     partial = nn(at_ref[...], g)
     for t in range(6):
         big[t, 0:WIDTH, :] = partial[:, 128 * t : 128 * t + 128]
@@ -148,7 +149,7 @@
     out_ref[:, 16:56, :] = (keep_ref[...].astype(F32) + got_ref[...].astype(F32)).astype(BF)
 
 
-def backward_kernel(count_ref, q_ref, k_ref, v_ref, g_ref, w_ref, at_ref, lse_ref, strided_ref,
+def backward_kernel(count_ref, q_ref, k_ref, v_ref, g_ref, w_ref, at_ref, stat_ref, strided_ref,
                     dq_ref, dk_ref, dv_ref, layer_ref, ga_ref, s_ref, dp_ref, pass_ref, qt, kt, gat, dqt, dkt, dvt):
     row_start, tile_count = lax.axis_index("seq") * ROWS, count_ref[0:1, 0:1]
     pass_ref[...] = strided_ref[...]
@@ -161,9 +162,9 @@
     valid_key = (row_start + iota((ROWS, ROWS), 0)) < tile_count
     for start in range(0, HEADS, GROUP):
         group = [(h, *head_window(h)) for h in range(start, start + GROUP)]
-        scores = [jnp.where(valid_key, nn(k_ref[:, w] * here, qt[w, :]), MASKED) for _, w, _, here in group]
+        scores = [jnp.where(valid_key, nn(k_ref[:, w] * here, qt[w, :]) * SCALE, MASKED) for _, w, _, here in group]
         slopes = [nn(v_ref[:, w] * here, gat[w, :]) for _, w, _, here in group]
-        probs = [jnp.exp2(s * POWER - lse_ref[h : h + 1, :]) for (h, _, _, _), s in zip(group, scores)]
+        probs = [jnp.exp(s - stat_ref[h : h + 1, :]) * stat_ref[HEADS + h : HEADS + h + 1, :] for (h, _, _, _), s in zip(group, scores)]
         deltas = [
             jnp.sum(gat[rows, :].astype(F32) * at_ref[rows, :].astype(F32), axis=0, keepdims=True)
             for _, _, rows, _ in group
@@ -323,7 +324,7 @@
 
     part = (PEERS, PART_ROWS, LANES)
     at0, lse0, keep, swap = call(
-        forward_kernel, (count, q, k, v, g), [(tall, BF), ((HEADS, ROWS), F32), (part, BF), (part, BF)],
+        forward_kernel, (count, q, k, v, g), [(tall, BF), ((2 * HEADS, ROWS), F32), (part, BF), (part, BF)],
         [(tall, BF), (tall, BF), ((6, WIDTH + 16, LANES), F32), (((PEERS + 1) * PART_ROWS, LANES), F32)],
         near=(0,),
     )

time: 83 us -> 83 us (level)
  transfers between devices with their start and end apart: 9 -> 9, of which waited for: 6 -> 6; matrix products, arithmetic and copies ran while one was open for 2% -> 2% of each run, Pallas kernels for 23% -> 24%
where the time goes in v6:
time: 83 us; the launch traced here: 82.5 us
  starting transfers between devices  35 us (42%)
  Pallas kernels  26.9 us (32%)
  waiting for transfers between devices  15.9 us (19%)
  local copies, waits for them, and re-layouts  2.62 us (3%)
  between operations  1.41 us (2%)
    pallas_call x7, Pallas kernels, call(): pl.pallas_call(kernel, out_shape=[(pltpu.VMEM if n in keep else pltpu.HBM...  26.9 us
    all_to_all x1, starting transfers between devices, on_device(): x = lax.all_to_all(send, 'seq', 0, 0)  13.6 us
    ppermute x3, starting transfers between devices, on_device(): lax.ppermute(weight, 'slide', [(n, n ^ bits) for n in range(4)])  8.29 us
    all_to_all x1, starting transfers between devices, on_device(): y = lax.all_to_all(back, 'seq', 0, 0)  7.68 us
    all_to_all x1, waiting for transfers between devices, on_device(): x = lax.all_to_all(send, 'seq', 0, 0)  6.43 us
    all_to_all x1, waiting for transfers between devices, on_device(): y = lax.all_to_all(back, 'seq', 0, 0)  6.28 us
    ppermute x3, starting transfers between devices, on_device(): pieces.append(lax.ppermute(mine, 'seq', ring) if step else mine)  4.48 us
    ppermute x3, waiting for transfers between devices, on_device(): pieces.append(lax.ppermute(mine, 'seq', ring) if step else mine)  2.16 us
  transfers between devices with their start and end apart: 9, of which 6 were waited for; matrix products, arithmetic and copies ran while one was open for 2% of the time, Pallas kernels for 24%

profile of v6, /device:TPU:1, one launch (start us, length us, event | category | flops | bytes accessed | tf_op | source)
XLA Modules:
  0.0 82.5 jit_solution(2928526111573498918)
XLA Ops:
  1.3 4.2 %shard_map.101 = (bf16[64,40,128]{2,1,0:T(8,128)(2,1)}, s32[8,128]{1,0:T(8,128)S(1)}) custom-call(s32[1]{0:T(128)S(6)} %copy.13.count_ref, bf16[256,768]{1,0:T(8,128)(2,1)} %bitcast.16, bf16[256,768]{1,0:T(8,128)(2,1)} %bitcast.20, bf16[256,768]{1,0:T(8,128)(2,1)} %bitcast.24, bf16[256,768]{1,0:T(8,128)(2,1)} %bitcast.27), custom_call_target="tpu_custom_call" | custom-call | tf_op jit(solution)/shard_map/pallas_call | solution.py:304
  5.5 13.6 %all-to-all-start = ((bf16[64,40,128]{2,1,0:T(8,128)(2,1)}), bf16[64,40,128]{2,1,0:T(8,128)(2,1)S(1)}, u32[]{:S(2)}, u32[]{:S(2)}) async-start(bf16[64,40,128]{2,1,0:T(8,128)(2,1)} %get-tuple-element.26), calls=%async_computation | async-start | bytes 1310720 | tf_op jit(solution)/shard_map/all_to_all | solution.py:323
  19.1 5.3 %shard_map.102 = (bf16[768,256]{1,0:T(8,128)(2,1)}, f32[32,256]{1,0:T(8,128)}, bf16[64,40,128]{2,1,0:T(8,128)(2,1)}, bf16[64,40,128]{2,1,0:T(8,128)(2,1)}) custom-call(s32[8,128]{1,0:T(8,128)S(1)} %get-tuple-element.25.count_ref, bf16[256,768]{1,0:T(8,128)(2,1)} %bitcast.17, bf16[256,768]{1,0:T(8,128)(2,1)} %bitcast.21, bf16[256,768]{1,0:T(8,128)(2,1)} %bitcast.25, ...), custom_call_target="tpu_custom_call" | custom-call | tf_op jit(solution)/shard_map/pallas_call | solution.py:304
  24.5 0.9 %collective-permute-start = (bf16[64,40,128]{2,1,0:T(8,128)(2,1)}, bf16[64,40,128]{2,1,0:T(8,128)(2,1)S(1)}, u32[]{:S(2)}, u32[]{:S(2)}) collective-permute-start(bf16[64,40,128]{2,1,0:T(8,128)(2,1)} %get-tuple-element.28), channel_id=1, source_target_pairs={{0,64},{64,0},{128,192},{192,128},{1,65},{65,1},{129,193},{193,129... | collective-permute-start | bytes 1966088 | tf_op jit(solution)/shard_map/ppermute | solution.py:331
  25.4 0.9 %constant_dynamic-slice_fusion.w_ref = bf16[48,768]{1,0:T(8,128)(2,1)S(1)} fusion(bf16[768,768]{1,0:T(8,128)(2,1)} %w_ref.3, s32[]{:T(128)S(6)} %select_n.44), kind=kLoop, calls=%fused_computation.5 | loop fusion | bytes 147460 | tf_op jit(solution)/shard_map/dynamic_slice | solution.py:334
  26.3 1.0 %collective-permute-done.got_ref = bf16[64,40,128]{2,1,0:T(8,128)(2,1)S(1)} collective-permute-done((bf16[64,40,128]{2,1,0:T(8,128)(2,1)}, bf16[64,40,128]{2,1,0:T(8,128)(2,1)S(1)}, u32[]{:S(2)}, u32[]{:S(2)}) %collective-permute-start) | collective-permute-done | bytes 655392 | tf_op jit(solution)/shard_map/ppermute | solution.py:331
  27.3 0.8 %copy-done = bf16[64,40,128]{2,1,0:T(8,128)(2,1)} copy-done((bf16[64,40,128]{2,1,0:T(8,128)(2,1)}, bf16[64,40,128]{2,1,0:T(8,128)(2,1)S(1)}, u32[]{:S(2)}) %copy-start) | copy-done | bytes 655384
  28.2 2.4 %shard_map.103.joined_ref = bf16[64,56,128]{2,1,0:T(8,128)(2,1)} custom-call(bf16[64,40,128]{2,1,0:T(8,128)(2,1)} %get-tuple-element.27.keep_ref, bf16[64,40,128]{2,1,0:T(8,128)(2,1)} %copy-done), custom_call_target="tpu_custom_call" | custom-call | tf_op jit(solution)/shard_map/pallas_call | solution.py:304
  30.6 6.4 %all-to-all-done.x_ref = bf16[64,40,128]{2,1,0:T(8,128)(2,1)S(1)} async-done(((bf16[64,40,128]{2,1,0:T(8,128)(2,1)}), bf16[64,40,128]{2,1,0:T(8,128)(2,1)S(1)}, u32[]{:S(2)}, u32[]{:S(2)}) %all-to-all-start) | async-done | bytes 655392 | tf_op jit(solution)/shard_map/all_to_all | solution.py:323
  37.0 3.1 %shard_map.104 = (bf16[64,56,128]{2,1,0:T(8,128)(2,1)}, f32[4,12,768]{2,1,0:T(8,128)}) custom-call(s32[8,128]{1,0:T(8,128)S(1)} %get-tuple-element.25.count_ref, bf16[64,40,128]{2,1,0:T(8,128)(2,1)S(1)} %all-to-all-done.x_ref, bf16[48,768]{1,0:T(8,128)(2,1)S(1)} %constant_dynamic-slice_fusion.w_ref, ...), custom_call_target="tpu_custom_call", output_to_operand_aliasing={{0}: (3, {})} | custom-call | tf_op jit(solution)/shard_map/pallas_call | solution.py:304
  40.1 7.7 %all-to-all-start.1 = ((bf16[64,56,128]{2,1,0:T(8,128)(2,1)}), bf16[64,56,128]{2,1,0:T(8,128)(2,1)S(1)}, u32[]{:S(2)}, u32[]{:S(2)}) async-start(bf16[64,56,128]{2,1,0:T(8,128)(2,1)} %get-tuple-element.29), calls=%async_computation.1 | async-start | bytes 1835008 | tf_op jit(solution)/shard_map/all_to_all | solution.py:354
  47.9 7.4 %shard_map.105 = (f32[256,768]{1,0:T(8,128)S(1)}, f32[256,768]{1,0:T(8,128)S(1)}, f32[256,768]{1,0:T(8,128)S(1)}, f32[256,768]{1,0:T(8,128)}, bf16[256,768]{1,0:...) custom-call(s32[8,128]{1,0:T(8,128)S(1)} %get-tuple-element.25.count_ref, ...), custom_call_target="tpu_custom_call" | custom-call | tf_op jit(solution)/shard_map/pallas_call | solution.py:304
  55.2 0.9 %dynamic-slice_bitcast_fusion = (f32[12,768]{1,0:T(8,128)S(1)}, f32[12,768]{1,0:T(8,128)S(1)}, f32[12,768]{1,0:T(8,128)S(1)}, f32[12,768]{1,0:T(8,128)S(1)}) fusion(f32[4,12,768]{2,1,0:T(8,128)} %get-tuple-element.44, s32[]{:T(128)S(6)} %select_n.53, s32[]{:T(128)S(6)} %select_n.51, s32[]{:T(128)S(6)} %select_n.49, s32[]{:T(128)S(6)} %select_n.47), kind=kLoop, calls=%fused_computation.1 | loop fusion | bytes 294928 | tf_op jit(solution)/shard_map/jit(dynamic_index_in_dim)/squeeze | solution.py:366
  56.1 0.9 %collective-permute-start.1 = (f32[12,768]{1,0:T(8,128)S(1)}, f32[12,768]{1,0:T(8,128)S(1)}, u32[]{:S(2)}, u32[]{:S(2)}) collective-permute-start(f32[12,768]{1,0:T(8,128)S(1)} %get-tuple-element.47), channel_id=1, source_target_pairs={{0,1},{1,2},{2,3},{3,0},{4,5},{5,6},{6,7},{7,4},{8,9},{9,10},{10,1... | collective-permute-start | bytes 110600 | tf_op jit(solution)/shard_map/ppermute | solution.py:368
  57.0 2.4 %collective-permute-start.2 = (f32[12,768]{1,0:T(8,128)S(1)}, f32[12,768]{1,0:T(8,128)S(1)}, u32[]{:S(2)}, u32[]{:S(2)}) collective-permute-start(f32[12,768]{1,0:T(8,128)S(1)} %get-tuple-element.46), channel_id=1, source_target_pairs={{0,2},{1,3},{2,0},{3,1},{4,6},{5,7},{6,4},{7,5},{8,10},{9,11},{10,... | collective-permute-start | bytes 110600 | tf_op jit(solution)/shard_map/ppermute | solution.py:368
  59.4 1.2 %collective-permute-start.3 = (f32[12,768]{1,0:T(8,128)S(1)}, f32[12,768]{1,0:T(8,128)S(1)}, u32[]{:S(2)}, u32[]{:S(2)}) collective-permute-start(f32[12,768]{1,0:T(8,128)S(1)} %get-tuple-element.45), channel_id=1, source_target_pairs={{0,3},{1,0},{2,1},{3,2},{4,7},{5,4},{6,5},{7,6},{8,11},{9,8},{10,9... | collective-permute-start | bytes 110600 | tf_op jit(solution)/shard_map/ppermute | solution.py:368
  60.6 0.5 collective-permute-done.1.b_ref
  61.1 1.1 %collective-permute-done.2.c_ref = f32[12,768]{1,0:T(8,128)S(1)} collective-permute-done((f32[12,768]{1,0:T(8,128)S(1)}, f32[12,768]{1,0:T(8,128)S(1)}, u32[]{:S(2)}, u32[]{:S(2)}) %collective-permute-start.2) | collective-permute-done | bytes 36896 | tf_op jit(solution)/shard_map/ppermute | solution.py:368
  62.1 0.6 collective-permute-done.3.d_ref
  62.8 6.3 %all-to-all-done.1.x_ref.y_ref = bf16[64,56,128]{2,1,0:T(8,128)(2,1)S(1)} async-done(((bf16[64,56,128]{2,1,0:T(8,128)(2,1)}), bf16[64,56,128]{2,1,0:T(8,128)(2,1)S(1)}, u32[]{:S(2)}, u32[]{:S(2)}) %all-to-all-start.1) | async-done | bytes 917536 | tf_op jit(solution)/shard_map/all_to_all | solution.py:354
  69.2 2.5 %collective-permute-start.4 = (f32[12,768]{1,0:T(8,128)S(1)}, f32[12,768]{1,0:T(8,128)S(1)}, u32[]{:S(2)}, u32[]{:S(2)}) collective-permute-start(f32[12,768]{1,0:T(8,128)S(1)} %shard_map.107), channel_id=1, source_target_pairs={{0,128},{64,192},{128,0},{192,64},{1,129},{65,193},{129,1},{193,65... | collective-permute-start | bytes 110600 | tf_op jit(solution)/shard_map/ppermute | solution.py:372
  71.7 5.8 %collective-permute-start.5 = (f32[12,768]{1,0:T(8,128)S(1)}, f32[12,768]{1,0:T(8,128)S(1)}, u32[]{:S(2)}, u32[]{:S(2)}) collective-permute-start(f32[12,768]{1,0:T(8,128)S(1)} %shard_map.107), channel_id=1, source_target_pairs={{0,192},{64,128},{128,64},{192,0},{1,193},{65,129},{129,65},{193,1... | collective-permute-start | bytes 110600 | tf_op jit(solution)/shard_map/ppermute | solution.py:372
  77.5 4.4 %shard_map.106 = (bf16[256,768]{1,0:T(8,128)(2,1)}, bf16[256,768]{1,0:T(8,128)(2,1)}, bf16[256,768]{1,0:T(8,128)(2,1)}, bf16[256,768]{1,0:T(8,128)(2,1)}) custom-call(s32[8,128]{1,0:T(8,128)S(1)} %get-tuple-element.25.count_ref, bf16[256,768]{1,0:T(8,128)(2,1)} %bitcast.19, bf16[256,768]{1,0:T(8,128)(2,1)} %bitcast.23, bf16[768,768]{1,0:T(8,128)(2,1)} %w_ref.3, ...), custom_call_target="tpu_custom_call" | custom-call | tf_op jit(solution)/shard_map/pallas_call | solution.py:304
  81.9 0.6 add_add_fusion
  (6 shorter events, 0.1 us)
Async XLA Ops:
  5.5 31.5 %all-to-all-start = ((bf16[64,40,128]{2,1,0:T(8,128)(2,1)}), bf16[64,40,128]{2,1,0:T(8,128)(2,1)S(1)}, u32[]{:S(2)}, u32[]{:S(2)}) async-start(bf16[64,40,128]{2,1,0:T(8,128)(2,1)} %get-tuple-element.26), calls=%async_computation | async-start | bytes 1310720 | tf_op jit(solution)/shard_map/all_to_all | solution.py:323
  24.5 2.9 %collective-permute-start = (bf16[64,40,128]{2,1,0:T(8,128)(2,1)}, bf16[64,40,128]{2,1,0:T(8,128)(2,1)S(1)}, u32[]{:S(2)}, u32[]{:S(2)}) collective-permute-start(bf16[64,40,128]{2,1,0:T(8,128)(2,1)} %get-tuple-element.28), channel_id=1, source_target_pairs={{0,64},{64,0},{128,192},{192,128},{1,65},{65,1},{129,193},{193,129... | collective-permute-start | bytes 1966088 | tf_op jit(solution)/shard_map/ppermute | solution.py:331
  27.3 0.8 %copy-start = (bf16[64,40,128]{2,1,0:T(8,128)(2,1)}, bf16[64,40,128]{2,1,0:T(8,128)(2,1)S(1)}, u32[]{:S(2)}) copy-start(bf16[64,40,128]{2,1,0:T(8,128)(2,1)S(1)} %collective-permute-done.got_ref) | copy-start | bytes 1966084
  40.1 28.9 %all-to-all-start.1 = ((bf16[64,56,128]{2,1,0:T(8,128)(2,1)}), bf16[64,56,128]{2,1,0:T(8,128)(2,1)S(1)}, u32[]{:S(2)}, u32[]{:S(2)}) async-start(bf16[64,56,128]{2,1,0:T(8,128)(2,1)} %get-tuple-element.29), calls=%async_computation.1 | async-start | bytes 1835008 | tf_op jit(solution)/shard_map/all_to_all | solution.py:354
  56.1 5.0 %collective-permute-start.1 = (f32[12,768]{1,0:T(8,128)S(1)}, f32[12,768]{1,0:T(8,128)S(1)}, u32[]{:S(2)}, u32[]{:S(2)}) collective-permute-start(f32[12,768]{1,0:T(8,128)S(1)} %get-tuple-element.47), channel_id=1, source_target_pairs={{0,1},{1,2},{2,3},{3,0},{4,5},{5,6},{6,7},{7,4},{8,9},{9,10},{10,1... | collective-permute-start | bytes 110600 | tf_op jit(solution)/shard_map/ppermute | solution.py:368
  57.0 5.1 %collective-permute-start.2 = (f32[12,768]{1,0:T(8,128)S(1)}, f32[12,768]{1,0:T(8,128)S(1)}, u32[]{:S(2)}, u32[]{:S(2)}) collective-permute-start(f32[12,768]{1,0:T(8,128)S(1)} %get-tuple-element.46), channel_id=1, source_target_pairs={{0,2},{1,3},{2,0},{3,1},{4,6},{5,7},{6,4},{7,5},{8,10},{9,11},{10,... | collective-permute-start | bytes 110600 | tf_op jit(solution)/shard_map/ppermute | solution.py:368
  59.4 3.4 %collective-permute-start.3 = (f32[12,768]{1,0:T(8,128)S(1)}, f32[12,768]{1,0:T(8,128)S(1)}, u32[]{:S(2)}, u32[]{:S(2)}) collective-permute-start(f32[12,768]{1,0:T(8,128)S(1)} %get-tuple-element.45), channel_id=1, source_target_pairs={{0,3},{1,0},{2,1},{3,2},{4,7},{5,4},{6,5},{7,6},{8,11},{9,8},{10,9... | collective-permute-start | bytes 110600 | tf_op jit(solution)/shard_map/ppermute | solution.py:368
  69.2 12.7 %collective-permute-start.4 = (f32[12,768]{1,0:T(8,128)S(1)}, f32[12,768]{1,0:T(8,128)S(1)}, u32[]{:S(2)}, u32[]{:S(2)}) collective-permute-start(f32[12,768]{1,0:T(8,128)S(1)} %shard_map.107), channel_id=1, source_target_pairs={{0,128},{64,192},{128,0},{192,64},{1,129},{65,193},{129,1},{193,65... | collective-permute-start | bytes 110600 | tf_op jit(solution)/shard_map/ppermute | solution.py:372
  71.7 10.2 %collective-permute-start.5 = (f32[12,768]{1,0:T(8,128)S(1)}, f32[12,768]{1,0:T(8,128)S(1)}, u32[]{:S(2)}, u32[]{:S(2)}) collective-permute-start(f32[12,768]{1,0:T(8,128)S(1)} %shard_map.107), channel_id=1, source_target_pairs={{0,192},{64,128},{128,64},{192,0},{1,193},{65,129},{129,65},{193,1... | collective-permute-start | bytes 110600 | tf_op jit(solution)/shard_map/ppermute | solution.py:372
  77.5 4.4 %collective-permute-start.6 = (f32[12,768]{1,0:T(8,128)S(1)}, f32[12,768]{1,0:T(8,128)S(1)}, u32[]{:S(2)}, u32[]{:S(2)}) collective-permute-start(f32[12,768]{1,0:T(8,128)S(1)} %shard_map.107), channel_id=1, source_target_pairs={{0,64},{64,0},{128,192},{192,128},{1,65},{65,1},{129,193},{193,129... | collective-permute-start | bytes 110600 | tf_op jit(solution)/shard_map/ppermute | solution.py:372
